TPU v7x, 32 devices: a whole 2x2x4 slice. The times are simulated.
32 devices in a mesh: dp: 8 (over z, core), fsdp: 4 (over y, x).
Axes of the slice: x: 2, y: 2, z: 4, core: 2. Of those that a mesh axis runs over, the one named last changes fastest.
Arguments:
- context: bfloat16 [64, 208, 1024], P(('dp', 'fsdp')), may hold values from -6 to 6
- byte_ids: int32 [64, 1664], P(('dp', 'fsdp')), may hold values from 0 to 255
- segment_ids: int32 [64, 208], P(('dp', 'fsdp')), may hold values from -1 to 3, as said below
- cotangent: bfloat16 [64, 208, 1024], P(('dp', 'fsdp')), may hold values from -6 to 6
- byte_table: bfloat16 [256, 128], P(('dp', 'fsdp')), may hold values from -6 to 6
- norm_mixer: bfloat16 [1024], P(('dp', 'fsdp')), may hold values from 0.5 to 1.5
- proj_zgate: bfloat16 [1024, 2048], P(('dp', 'fsdp')), may hold values from -0.1875 to 0.1875
- proj_inputs: bfloat16 [1024, 2304], P(('dp', 'fsdp')), may hold values from -0.1875 to 0.1875
- proj_step: bfloat16 [1024, 32], P(('dp', 'fsdp')), may hold values from -0.1875 to 0.1875
- conv_kernel: bfloat16 [4, 2304], P(None, ('dp', 'fsdp')), may hold values from -3 to 3
- conv_bias: bfloat16 [2304], P(('dp', 'fsdp')), may hold values from -3 to 3
- step_bias: float32 [32], replicated, may hold values from -6.9 to -2.3
- decay_log: float32 [32], replicated, may hold values from 0 to 2.77
- skip_gain: float32 [32], replicated, may hold values from 0.5 to 1.5
- mixer_norm: bfloat16 [2048], P(('dp', 'fsdp')), may hold values from 0.5 to 1.5
- proj_mixed: bfloat16 [2048, 1024], P(('dp', 'fsdp')), may hold values from -0.125 to 0.125
- norm_attn: bfloat16 [1024], P(('dp', 'fsdp')), may hold values from 0.5 to 1.5
- proj_heads: bfloat16 [1024, 3072], P(('dp', 'fsdp')), may hold values from -0.1875 to 0.1875
- proj_attended: bfloat16 [1024, 1024], P(('dp', 'fsdp')), may hold values from -0.75 to 0.75
- norm_ffn: bfloat16 [1024], P(('dp', 'fsdp')), may hold values from 0.5 to 1.5
- ffn_gate: bfloat16 [1024, 4096], P(('dp', 'fsdp')), may hold values from -0.1875 to 0.1875
- ffn_up: bfloat16 [1024, 4096], P(('dp', 'fsdp')), may hold values from -0.1875 to 0.1875
- ffn_down: bfloat16 [4096, 1024], P(('dp', 'fsdp')), may hold values from -0.09375 to 0.09375
Outputs:
- mixed: float32 [64, 208, 1024], P(('dp', 'fsdp'))
- context_grad: float32 [64, 208, 1024], P(('dp', 'fsdp'))
- rms_stats: float32 [4], replicated
- byte_table_grad: float32 [256, 128], P(('dp', 'fsdp'))
- norm_mixer_grad: float32 [1024], P(('dp', 'fsdp'))
- proj_zgate_grad: float32 [1024, 2048], P(('dp', 'fsdp'))
- proj_inputs_grad: float32 [1024, 2304], P(('dp', 'fsdp'))
- proj_step_grad: float32 [1024, 32], P(('dp', 'fsdp'))
- conv_kernel_grad: float32 [4, 2304], P(None, ('dp', 'fsdp'))
- conv_bias_grad: float32 [2304], P(('dp', 'fsdp'))
- step_bias_grad: float32 [32], replicated
- decay_log_grad: float32 [32], replicated
- skip_gain_grad: float32 [32], replicated
- mixer_norm_grad: float32 [2048], P(('dp', 'fsdp'))
- proj_mixed_grad: float32 [2048, 1024], P(('dp', 'fsdp'))
- norm_attn_grad: float32 [1024], P(('dp', 'fsdp'))
- proj_heads_grad: float32 [1024, 3072], P(('dp', 'fsdp'))
- proj_attended_grad: float32 [1024, 1024], P(('dp', 'fsdp'))
- norm_ffn_grad: float32 [1024], P(('dp', 'fsdp'))
- ffn_gate_grad: float32 [1024, 4096], P(('dp', 'fsdp'))
- ffn_up_grad: float32 [1024, 4096], P(('dp', 'fsdp'))
- ffn_down_grad: float32 [4096, 1024], P(('dp', 'fsdp'))
Inputs may be any that keep to these rules, and one draw needn't show every extreme that they name: `segment_ids`: each row holds documents of whole patches: ids start at 0 at the row's first patch and rise by one at each document's start, never falling; the valid prefix of a row holds at most 4 documents (often fewer in short rows), after which padding marked -1 fills its tail; row r has at least 52 + 156 * r // 63 valid patches, the last row has no padding, and the first row always ends in padding.
All inputs are finite; a program needn't handle non-finite values.
Results may differ from a plain program's by a relative error of at most 0.03.
Values may be sent and summed in bfloat16 or wider, within the bound.
No kernel may reach another device: no remote copies, remote signals or barrier semaphores. Data moves between devices by JAX's collectives and lax.ppermute only.
A program may use at most 320 MiB of HBM per device.

v0:
```python
from functools import partial

import jax
import jax.numpy as jnp
from jax import lax
from jax.sharding import PartitionSpec as P

DI = 2048
NS = 128
PM = 64
HD = 64
HM = 32
HA = 16


EPS = 1e-05


def matmul(former, latter):
    return jnp.dot(former, latter, preferred_element_type=jnp.float32)


def matmul_left(former, latter):
    return lax.dot_general(
        former, latter, (((0,), (0,)), ((), ())), preferred_element_type=jnp.float32
    )


def matmul_right(former, latter):
    return lax.dot_general(
        former, latter, (((1,), (1,)), ((), ())), preferred_element_type=jnp.float32
    )


def rms_norm(values, scaling):
    return values * lax.rsqrt(jnp.mean(values * values, axis=-1, keepdims=True) + EPS) * scaling


def conv_silu(inputs, kernel, offset, segments):
    kernel_taps = kernel.shape[0]
    length = inputs.shape[1]
    summed = inputs * kernel[kernel_taps - 1]
    for shift_by in range(1, kernel_taps):
        shifted = jnp.pad(inputs, ((0, 0), (shift_by, 0), (0, 0)))[:, :length]
        shifted_ids = jnp.pad(segments, ((0, 0), (shift_by, 0)), constant_values=-2)[:, :length]
        linked = (shifted_ids == segments).astype(jnp.float32)[:, :, None]
        summed = summed + shifted * linked * kernel[kernel_taps - 1 - shift_by]
    return jax.nn.silu(summed + offset)


def mix_weights(gram_matrix, step_raw, step_bias, decay_log, allowed):
    step_size = jax.nn.softplus(step_raw + step_bias)
    decay_rate = step_size * -jnp.exp(decay_log)
    cumulated = jnp.swapaxes(jnp.cumsum(decay_rate, axis=1), 1, 2)
    between = cumulated[:, :, :, None] - cumulated[:, :, None, :]
    keep_mask = allowed[:, None]
    decayed = jnp.where(keep_mask, jnp.exp(jnp.where(keep_mask, between, 0.0)), 0.0)
    return gram_matrix[:, None] * decayed * jnp.swapaxes(step_size, 1, 2)[:, :, None, :]


def gate_norm(heads_out, skip_values, zgate_raw, skip_gain, norm_gain):
    combined = heads_out + skip_gain[:, None] * skip_values
    gated_rows = combined.reshape(zgate_raw.shape) * jax.nn.silu(zgate_raw)
    return rms_norm(gated_rows, norm_gain)


def silu_product(gate_raw, upper_raw):
    return jax.nn.silu(gate_raw) * upper_raw


def local(
    context,
    byte_ids,
    segment_ids,
    cotangent,
    byte_table,
    norm_mixer,
    proj_zgate,
    proj_inputs,
    proj_step,
    conv_kernel,
    conv_bias,
    step_bias,
    decay_log,
    skip_gain,
    mixer_norm,
    proj_mixed,
    norm_attn,
    proj_heads,
    proj_attended,
    norm_ffn,
    ffn_gate,
    ffn_up,
    ffn_down,
):
    row_count, length = segment_ids.shape
    tokens = row_count * length
    model_width = context.shape[2]
    mixer_full = (
        lax.all_gather(byte_table, ("dp", "fsdp"), axis=0, tiled=True),
        lax.all_gather(norm_mixer, ("dp", "fsdp"), axis=0, tiled=True),
        lax.all_gather(proj_zgate, ("dp", "fsdp"), axis=0, tiled=True),
        lax.all_gather(proj_inputs, ("dp", "fsdp"), axis=0, tiled=True),
        lax.all_gather(proj_step, ("dp", "fsdp"), axis=0, tiled=True),
        lax.all_gather(conv_kernel, ("dp", "fsdp"), axis=1, tiled=True),
        lax.all_gather(conv_bias, ("dp", "fsdp"), axis=0, tiled=True),
        lax.all_gather(mixer_norm, ("dp", "fsdp"), axis=0, tiled=True),
        lax.all_gather(proj_mixed, ("dp", "fsdp"), axis=0, tiled=True),
    )
    (
        table_full,
        gain_one,
        zgate_full,
        inputs_full,
        step_full,
        kernel_full,
        offset_full,
        gated_gain,
        mixed_full,
    ) = mixer_full
    symbols = jnp.arange(table_full.shape[0], dtype=jnp.int32)
    onehot = (byte_ids.reshape(-1)[:, None] == symbols[None, :]).astype(jnp.bfloat16)
    embedded = matmul(onehot, table_full).reshape(tokens, model_width)
    stream_zero = embedded + context.reshape(tokens, model_width).astype(jnp.float32)
    positions = jnp.arange(length, dtype=jnp.int32)
    causal = positions[:, None] >= positions[None, :]
    allowed = (segment_ids[:, :, None] == segment_ids[:, None, :]) & causal[None]
    normed_one, norm_one_back = jax.vjp(rms_norm, stream_zero, gain_one.astype(jnp.float32))
    normed_one_low = normed_one.astype(jnp.bfloat16)
    zgate = matmul(normed_one_low, zgate_full)
    inputs_raw = matmul(normed_one_low, inputs_full)
    step_raw = matmul(normed_one_low, step_full)
    activated, conv_back = jax.vjp(
        partial(conv_silu, segments=segment_ids),
        inputs_raw.reshape(row_count, length, -1),
        kernel_full.astype(jnp.float32),
        offset_full.astype(jnp.float32),
    )
    values_low = activated[:, :, :DI].astype(jnp.bfloat16).reshape(row_count, length, HM, PM)
    state_in = activated[:, :, DI : DI + NS].astype(jnp.bfloat16)
    state_out = activated[:, :, DI + NS :].astype(jnp.bfloat16)
    gram_matrix = jnp.einsum(
        "ntk,nsk->nts", state_out, state_in, preferred_element_type=jnp.float32
    )
    weights, weights_back = jax.vjp(
        partial(mix_weights, allowed=allowed),
        gram_matrix,
        step_raw.reshape(row_count, length, -1),
        step_bias,
        decay_log,
    )
    weights_low = weights.astype(jnp.bfloat16)
    heads_out = jnp.einsum(
        "nhts,nshp->nthp", weights_low, values_low, preferred_element_type=jnp.float32
    )
    normed_gate, gate_back = jax.vjp(
        gate_norm,
        heads_out,
        values_low.astype(jnp.float32),
        zgate.reshape(row_count, length, -1),
        skip_gain,
        gated_gain.astype(jnp.float32),
    )
    gate_low = normed_gate.reshape(tokens, -1).astype(jnp.bfloat16)
    mixer_out = matmul(gate_low, mixed_full)
    stream_one = stream_zero + mixer_out
    attention_full = (
        lax.all_gather(norm_attn, ("dp", "fsdp"), axis=0, tiled=True),
        lax.all_gather(proj_heads, ("dp", "fsdp"), axis=0, tiled=True),
        lax.all_gather(proj_attended, ("dp", "fsdp"), axis=0, tiled=True),
    )
    gain_two, heads_full, attended_full = attention_full
    normed_two, norm_two_back = jax.vjp(rms_norm, stream_one, gain_two.astype(jnp.float32))
    normed_two_low = normed_two.astype(jnp.bfloat16)
    joined = matmul(normed_two_low, heads_full)
    query_low = joined[:, :model_width].astype(jnp.bfloat16).reshape(row_count, length, HA, HD)
    key_low = (
        joined[:, model_width : 2 * model_width]
        .astype(jnp.bfloat16)
        .reshape(row_count, length, HA, HD)
    )
    value_low = joined[:, 2 * model_width :].astype(jnp.bfloat16).reshape(row_count, length, HA, HD)
    scale = HD ** (-0.5)
    scores = (
        jnp.einsum("nthd,nshd->nhts", query_low, key_low, preferred_element_type=jnp.float32)
        * scale
    )
    masked = jnp.where(allowed[:, None], scores, -1e30)
    highest = jnp.max(masked, axis=-1, keepdims=True)
    exponents = jnp.exp(masked - highest)
    summed = jnp.sum(exponents, axis=-1, keepdims=True)
    probabilities = (exponents / summed).astype(jnp.bfloat16)
    log_total = highest + jnp.log(summed)
    attended = jnp.einsum(
        "nhts,nshd->nthd", probabilities, value_low, preferred_element_type=jnp.float32
    )
    attended_low = attended.reshape(tokens, model_width).astype(jnp.bfloat16)
    attn_out = matmul(attended_low, attended_full)
    stream_two = stream_one + attn_out
    ffn_full = (
        lax.all_gather(norm_ffn, ("dp", "fsdp"), axis=0, tiled=True),
        lax.all_gather(ffn_gate, ("dp", "fsdp"), axis=0, tiled=True),
        lax.all_gather(ffn_up, ("dp", "fsdp"), axis=0, tiled=True),
        lax.all_gather(ffn_down, ("dp", "fsdp"), axis=0, tiled=True),
    )
    gain_three, gate_full, upper_full, down_full = ffn_full
    normed_three, norm_three_back = jax.vjp(rms_norm, stream_two, gain_three.astype(jnp.float32))
    normed_three_low = normed_three.astype(jnp.bfloat16)
    gate_pre = matmul(normed_three_low, gate_full)
    up_pre = matmul(normed_three_low, upper_full)
    hidden, hidden_back = jax.vjp(silu_product, gate_pre, up_pre)
    hidden_low = hidden.astype(jnp.bfloat16)
    ffn_out = matmul(hidden_low, down_full)
    stream_three = stream_two + ffn_out
    valid_rows = (segment_ids.reshape(tokens, 1) >= 0).astype(jnp.float32)
    moments = jnp.stack(
        [
            jnp.sum(valid_rows * stream_zero * stream_zero),
            jnp.sum(valid_rows * mixer_out * mixer_out),
            jnp.sum(valid_rows * attn_out * attn_out),
            jnp.sum(valid_rows * ffn_out * ffn_out),
            jnp.sum(valid_rows),
        ]
    )
    gate_use, upper_use, down_use = (
        lax.all_gather(ffn_gate, ("dp", "fsdp"), axis=0, tiled=True),
        lax.all_gather(ffn_up, ("dp", "fsdp"), axis=0, tiled=True),
        lax.all_gather(ffn_down, ("dp", "fsdp"), axis=0, tiled=True),
    )
    grad_three = cotangent.reshape(tokens, model_width).astype(jnp.float32)
    ffn_grad_low = grad_three.astype(jnp.bfloat16)
    grad_ffn_down = matmul_left(hidden_low, ffn_grad_low)
    grad_hidden = matmul_right(ffn_grad_low, down_use)
    grad_gate_pre, grad_up_pre = hidden_back(grad_hidden)
    gate_grad_low = grad_gate_pre.astype(jnp.bfloat16)
    upper_grad_low = grad_up_pre.astype(jnp.bfloat16)
    grad_ffn_gate = matmul_left(normed_three_low, gate_grad_low)
    grad_ffn_up = matmul_left(normed_three_low, upper_grad_low)
    grad_normed_three = matmul_right(gate_grad_low, gate_use) + matmul_right(
        upper_grad_low, upper_use
    )
    stream_part, grad_norm_ffn = norm_three_back(grad_normed_three)
    grad_two = grad_three + stream_part
    ffn_sums = (
        lax.psum_scatter(grad_norm_ffn, ("dp", "fsdp"), scatter_dimension=0, tiled=True),
        lax.psum_scatter(grad_ffn_gate, ("dp", "fsdp"), scatter_dimension=0, tiled=True),
        lax.psum_scatter(grad_ffn_up, ("dp", "fsdp"), scatter_dimension=0, tiled=True),
        lax.psum_scatter(grad_ffn_down, ("dp", "fsdp"), scatter_dimension=0, tiled=True),
    )
    heads_use, attended_use = (
        lax.all_gather(proj_heads, ("dp", "fsdp"), axis=0, tiled=True),
        lax.all_gather(proj_attended, ("dp", "fsdp"), axis=0, tiled=True),
    )
    attn_grad_low = grad_two.astype(jnp.bfloat16)
    grad_proj_attended = matmul_left(attended_low, attn_grad_low)
    grad_attended = (
        matmul_right(attn_grad_low, attended_use)
        .astype(jnp.bfloat16)
        .reshape(row_count, length, HA, HD)
    )
    rescored = (
        jnp.einsum("nthd,nshd->nhts", query_low, key_low, preferred_element_type=jnp.float32)
        * scale
    )
    remasked = jnp.where(allowed[:, None], rescored, -1e30)
    probs_again = jnp.where(allowed[:, None], jnp.exp(remasked - log_total), 0.0)
    grad_probs = jnp.einsum(
        "nthd,nshd->nhts", grad_attended, value_low, preferred_element_type=jnp.float32
    )
    grad_value_rows = jnp.einsum(
        "nhts,nthd->nshd",
        probs_again.astype(jnp.bfloat16),
        grad_attended,
        preferred_element_type=jnp.float32,
    )
    grad_scores = (
        probs_again * (grad_probs - jnp.sum(probs_again * grad_probs, axis=-1, keepdims=True))
    ).astype(jnp.bfloat16)
    grad_query = (
        jnp.einsum("nhts,nshd->nthd", grad_scores, key_low, preferred_element_type=jnp.float32)
        * scale
    )
    grad_key = (
        jnp.einsum("nhts,nthd->nshd", grad_scores, query_low, preferred_element_type=jnp.float32)
        * scale
    )
    grad_joined = jnp.concatenate(
        [
            grad_query.reshape(tokens, model_width),
            grad_key.reshape(tokens, model_width),
            grad_value_rows.reshape(tokens, model_width),
        ],
        axis=1,
    ).astype(jnp.bfloat16)
    grad_proj_heads = matmul_left(normed_two_low, grad_joined)
    grad_normed_two = matmul_right(grad_joined, heads_use)
    stream_part_two, grad_norm_attn = norm_two_back(grad_normed_two)
    grad_one = grad_two + stream_part_two
    attention_sums = (
        lax.psum_scatter(grad_norm_attn, ("dp", "fsdp"), scatter_dimension=0, tiled=True),
        lax.psum_scatter(grad_proj_heads, ("dp", "fsdp"), scatter_dimension=0, tiled=True),
        lax.psum_scatter(grad_proj_attended, ("dp", "fsdp"), scatter_dimension=0, tiled=True),
    )
    zgate_use, inputs_use, step_use, mixed_use = (
        lax.all_gather(proj_zgate, ("dp", "fsdp"), axis=0, tiled=True),
        lax.all_gather(proj_inputs, ("dp", "fsdp"), axis=0, tiled=True),
        lax.all_gather(proj_step, ("dp", "fsdp"), axis=0, tiled=True),
        lax.all_gather(proj_mixed, ("dp", "fsdp"), axis=0, tiled=True),
    )
    mixer_grad_low = grad_one.astype(jnp.bfloat16)
    grad_proj_mixed = matmul_left(gate_low, mixer_grad_low)
    grad_normed_gate = matmul_right(mixer_grad_low, mixed_use).reshape(row_count, length, -1)
    grad_heads, grad_skip_values, grad_zgate, grad_skip_gain, grad_gated_gain = gate_back(
        grad_normed_gate
    )
    heads_grad_low = grad_heads.astype(jnp.bfloat16)
    grad_weights = jnp.einsum(
        "nthp,nshp->nhts", heads_grad_low, values_low, preferred_element_type=jnp.float32
    )
    grad_values = (
        jnp.einsum(
            "nhts,nthp->nshp", weights_low, heads_grad_low, preferred_element_type=jnp.float32
        )
        + grad_skip_values
    )
    grad_gram, grad_step_raw, grad_step_bias, grad_decay_log = weights_back(grad_weights)
    gram_grad_low = grad_gram.astype(jnp.bfloat16)
    grad_state_out = jnp.einsum(
        "nts,nsk->ntk", gram_grad_low, state_in, preferred_element_type=jnp.float32
    )
    grad_state_in = jnp.einsum(
        "nts,ntk->nsk", gram_grad_low, state_out, preferred_element_type=jnp.float32
    )
    grad_activated = jnp.concatenate(
        [grad_values.reshape(row_count, length, -1), grad_state_in, grad_state_out], axis=-1
    )
    grad_inputs_raw, grad_conv_kernel, grad_conv_bias = conv_back(grad_activated)
    zgate_grad_low = grad_zgate.reshape(tokens, -1).astype(jnp.bfloat16)
    inputs_grad_low = grad_inputs_raw.reshape(tokens, -1).astype(jnp.bfloat16)
    step_grad_low = grad_step_raw.reshape(tokens, -1).astype(jnp.bfloat16)
    grad_proj_zgate = matmul_left(normed_one_low, zgate_grad_low)
    grad_proj_inputs = matmul_left(normed_one_low, inputs_grad_low)
    grad_proj_step = matmul_left(normed_one_low, step_grad_low)
    grad_normed_one = (
        matmul_right(zgate_grad_low, zgate_use)
        + matmul_right(inputs_grad_low, inputs_use)
        + matmul_right(step_grad_low, step_use)
    )
    stream_part_one, grad_norm_mixer = norm_one_back(grad_normed_one)
    grad_zero = grad_one + stream_part_one
    embed_grad_low = grad_zero.reshape(-1, table_full.shape[1]).astype(jnp.bfloat16)
    grad_byte_table = matmul_left(onehot, embed_grad_low)
    mixer_sums = (
        lax.psum_scatter(grad_byte_table, ("dp", "fsdp"), scatter_dimension=0, tiled=True),
        lax.psum_scatter(grad_norm_mixer, ("dp", "fsdp"), scatter_dimension=0, tiled=True),
        lax.psum_scatter(grad_proj_zgate, ("dp", "fsdp"), scatter_dimension=0, tiled=True),
        lax.psum_scatter(grad_proj_inputs, ("dp", "fsdp"), scatter_dimension=0, tiled=True),
        lax.psum_scatter(grad_proj_step, ("dp", "fsdp"), scatter_dimension=0, tiled=True),
        lax.psum_scatter(grad_conv_kernel, ("dp", "fsdp"), scatter_dimension=1, tiled=True),
        lax.psum_scatter(grad_conv_bias, ("dp", "fsdp"), scatter_dimension=0, tiled=True),
        lax.psum_scatter(grad_gated_gain, ("dp", "fsdp"), scatter_dimension=0, tiled=True),
        lax.psum_scatter(grad_proj_mixed, ("dp", "fsdp"), scatter_dimension=0, tiled=True),
    )
    totals, bias_total, decay_total, skip_total = lax.psum(
        (moments, grad_step_bias, grad_decay_log, grad_skip_gain), ("dp", "fsdp")
    )
    rms_stats = jnp.sqrt(totals[:4] / (totals[4] * model_width))
    return (
        stream_three.reshape(row_count, length, model_width),
        grad_zero.reshape(row_count, length, model_width),
        rms_stats,
        mixer_sums[0],
        mixer_sums[1],
        mixer_sums[2],
        mixer_sums[3],
        mixer_sums[4],
        mixer_sums[5],
        mixer_sums[6],
        bias_total,
        decay_total,
        skip_total,
        mixer_sums[7],
        mixer_sums[8],
        attention_sums[0],
        attention_sums[1],
        attention_sums[2],
        ffn_sums[0],
        ffn_sums[1],
        ffn_sums[2],
        ffn_sums[3],
    )


def solution(mesh):
    return jax.shard_map(
        local,
        mesh=mesh,
        in_specs=(
            P(("dp", "fsdp"), None, None),
            P(("dp", "fsdp"), None),
            P(("dp", "fsdp"), None),
            P(("dp", "fsdp"), None, None),
            P(("dp", "fsdp"), None),
            P(("dp", "fsdp")),
            P(("dp", "fsdp"), None),
            P(("dp", "fsdp"), None),
            P(("dp", "fsdp"), None),
            P(None, ("dp", "fsdp")),
            P(("dp", "fsdp")),
            P(),
            P(),
            P(),
            P(("dp", "fsdp")),
            P(("dp", "fsdp"), None),
            P(("dp", "fsdp")),
            P(("dp", "fsdp"), None),
            P(("dp", "fsdp"), None),
            P(("dp", "fsdp")),
            P(("dp", "fsdp"), None),
            P(("dp", "fsdp"), None),
            P(("dp", "fsdp"), None),
        ),
        out_specs=(
            P(("dp", "fsdp"), None, None),
            P(("dp", "fsdp"), None, None),
            P(),
            P(("dp", "fsdp"), None),
            P(("dp", "fsdp")),
            P(("dp", "fsdp"), None),
            P(("dp", "fsdp"), None),
            P(("dp", "fsdp"), None),
            P(None, ("dp", "fsdp")),
            P(("dp", "fsdp")),
            P(),
            P(),
            P(),
            P(("dp", "fsdp")),
            P(("dp", "fsdp"), None),
            P(("dp", "fsdp")),
            P(("dp", "fsdp"), None),
            P(("dp", "fsdp"), None),
            P(("dp", "fsdp")),
            P(("dp", "fsdp"), None),
            P(("dp", "fsdp"), None),
            P(("dp", "fsdp"), None),
        ),
        check_vma=False,
    )
```

profile of v0, /device:TPU:0, one launch (start us, length us, event | category | flops | bytes accessed | tf_op | source)
XLA Modules:
  0.0 3038.5 jit_solution(5021807410838806906)
XLA Ops:
  15.7 70.8 %all_gather.57 = bf16[256,128]{1,0:T(8,128)(2,1)S(1)} all-gather(bf16[8,128]{1,0:T(8,128)(2,1)} %param.27), channel_id=1, replica_groups=mesh['dp'=8,'fsdp'=4] {'dp','fsdp'}, dimensions={0}, use_global_device_ids=true | all-gather | bytes 67584 | tf_op jit(solution)/shard_map/all_gather | solution.py:100
  97.5 38.5 %all-reduce.28 = (bf16[1024]{0:T(1024)(128)(2,1)S(1)}, bf16[2304]{0:T(1024)(128)(2,1)S(1)}, bf16[2048]{0:T(1024)(128)(2,1)S(1)}, bf16[1024]{0:T(1024)(128)(2,1)S(1)}, bf16[1024]{0:T(1024)(128)(2,1)S(1)}) all-reduce(bf16[1024]{0:T(1024)(128)(2,1)S(1)} %dynamic-update-slice, ...), channel_id=1, replica_groups=mesh['dp'=8,'fsdp'=4] {'dp','fsdp'}, use_global_device_ids=true, to_apply=%add.15 | all-reduce | flops 7424 | bytes 29696
  139.0 65.8 %all-gather = bf16[32,72,4]{1,2,0:T(4,128)(2,1)S(1)} all-gather(bf16[1,72,4]{1,2,0:T(4,128)(2,1)S(1)} %bitcast.195), channel_id=1, replica_groups=mesh['dp'=8,'fsdp'=4] {'dp','fsdp'}, dimensions={0}, use_global_device_ids=true | all-gather | bytes 19008 | tf_op jit(solution)/shard_map/all_gather | solution.py:105
  217.4 66.1 %all_gather.62 = bf16[1024,32]{1,0:T(8,128)(2,1)S(1)} all-gather(bf16[32,32]{1,0:T(8,128)(2,1)} %param.31), channel_id=1, replica_groups=mesh['dp'=8,'fsdp'=4] {'dp','fsdp'}, dimensions={0}, use_global_device_ids=true | all-gather | bytes 67584 | tf_op jit(solution)/shard_map/all_gather | solution.py:104
  344.5 13.0 reshape.426
  382.8 32.3 %all-gather.22.cloned.1.call-done = bf16[1024,4096]{1,0:T(8,128)(2,1)} async-done(((bf16[32,4096]{1,0:T(8,128)(2,1)}), bf16[1024,4096]{1,0:T(8,128)(2,1)}) %all-gather.22.cloned.1.call-update) | async-done | bytes 8388624 | tf_op jit(solution)/shard_map/all_gather | solution.py:203
  424.0 70.1 %all-gather.20.cloned.1.call-done = bf16[1024,4096]{1,0:T(8,128)(2,1)} async-done(((bf16[32,4096]{1,0:T(8,128)(2,1)}), bf16[1024,4096]{1,0:T(8,128)(2,1)}) %all-gather.20.cloned.1.call-update) | async-done | bytes 8388624 | tf_op jit(solution)/shard_map/all_gather | solution.py:202
  503.1 70.0 %all-gather.24.cloned.1.call-done = bf16[4096,1024]{1,0:T(8,128)(2,1)} async-done(((bf16[128,1024]{1,0:T(8,128)(2,1)}), bf16[4096,1024]{1,0:T(8,128)(2,1)}) %all-gather.24.cloned.1.call-update) | async-done | bytes 8388624 | tf_op jit(solution)/shard_map/all_gather | solution.py:204
  573.1 14.2 multiply_convert_fusion.2
  668.3 14.0 fusion.3
  708.0 10.9 multiply_reduce_fusion.6
  780.6 10.1 fusion.115
  791.9 10.1 fusion.114
  812.2 48.7 %all-reduce.34.cloned.1.call-done = (f32[5]{0:T(128)}, f32[1024]{0:T(1024)}, f32[4,2304]{1,0:T(4,128)}, f32[2304]{0:T(1024)}, f32[32]{0:T(128)}, /*index=5*/f32[...) async-done(((f32[5]{0:T(128)}, f32[1024]{0:T(1024)}, f32[4,2304]{1,0:T(4,128)}, f32[2304]{0:T(1024)}, f32[32]{0:T(128)}, /*index=5*/f32[32]{0:T(128)}, ...) | async-done | bytes 66980 | tf_op jit(solution)/shard_map/psum | solution.py:364
  871.7 120.8 %all-reduce.32.cloned.1.call-done = f32[256,128]{1,0:T(8,128)} async-done(((f32[256,128]{1,0:T(8,128)}), f32[256,128]{1,0:T(8,128)}) %all-reduce.32.cloned.1.call-update) | async-done | bytes 131088
  993.8 134.5 %reduce-scatter.15.cloned.1.call-done = f32[32,32]{1,0:T(8,128)} async-done(((f32[1024,32]{1,0:T(8,128)}), f32[32,32]{1,0:T(8,128)}) %reduce-scatter.15.cloned.1.call-update) | async-done | bytes 4112 | tf_op jit(solution)/shard_map/reduce_scatter | solution.py:358
  1128.3 140.1 %reduce-scatter.21.cloned.1.call-done = f32[32,1024]{1,0:T(8,128)} async-done(((f32[1024,1024]{1,0:T(8,128)}), f32[32,1024]{1,0:T(8,128)}) %reduce-scatter.21.cloned.1.call-update) | async-done | bytes 131088 | tf_op jit(solution)/shard_map/reduce_scatter | solution.py:302
  1268.3 140.0 %reduce-scatter.13.cloned.1.call-done = f32[32,2304]{1,0:T(8,128)} async-done(((f32[1024,2304]{1,0:T(8,128)}), f32[32,2304]{1,0:T(8,128)}) %reduce-scatter.13.cloned.1.call-update) | async-done | bytes 294928 | tf_op jit(solution)/shard_map/reduce_scatter | solution.py:357
  1408.3 185.5 %reduce-scatter.11.cloned.1.call-done = f32[32,2048]{1,0:T(8,128)} async-done(((f32[1024,2048]{1,0:T(8,128)}), f32[32,2048]{1,0:T(8,128)}) %reduce-scatter.11.cloned.1.call-update) | async-done | bytes 262160 | tf_op jit(solution)/shard_map/reduce_scatter | solution.py:356
  1593.9 187.3 %reduce-scatter.17.cloned.1.call-done = f32[64,1024]{1,0:T(8,128)} async-done(((f32[2048,1024]{1,0:T(8,128)}), f32[64,1024]{1,0:T(8,128)}) %reduce-scatter.17.cloned.1.call-update) | async-done | bytes 262160 | tf_op jit(solution)/shard_map/reduce_scatter | solution.py:362
  1781.2 163.9 %reduce-scatter.19.cloned.1.call-done = f32[32,3072]{1,0:T(8,128)} async-done(((f32[1024,3072]{1,0:T(8,128)}), f32[32,3072]{1,0:T(8,128)}) %reduce-scatter.19.cloned.1.call-update) | async-done | bytes 393232 | tf_op jit(solution)/shard_map/reduce_scatter | solution.py:301
  1945.1 359.4 %reduce-scatter.27.cloned.1.call-done = f32[128,1024]{1,0:T(8,128)} async-done(((f32[4096,1024]{1,0:T(8,128)}), f32[128,1024]{1,0:T(8,128)}) %reduce-scatter.27.cloned.1.call-update) | async-done | bytes 524304 | tf_op jit(solution)/shard_map/reduce_scatter | solution.py:248
  2304.5 361.8 %reduce-scatter.25.cloned.1.call-done = f32[32,4096]{1,0:T(8,128)} async-done(((f32[1024,4096]{1,0:T(8,128)}), f32[32,4096]{1,0:T(8,128)}) %reduce-scatter.25.cloned.1.call-update) | async-done | bytes 524304 | tf_op jit(solution)/shard_map/reduce_scatter | solution.py:247
  2666.3 361.9 %reduce-scatter.23.cloned.1.call-done = f32[32,4096]{1,0:T(8,128)} async-done(((f32[1024,4096]{1,0:T(8,128)}), f32[32,4096]{1,0:T(8,128)}) %reduce-scatter.23.cloned.1.call-update) | async-done | bytes 524304 | tf_op jit(solution)/shard_map/reduce_scatter | solution.py:246
  (436 shorter events, 332.1 us)
Async XLA Ops:
  7.2 285.4 %all-gather.10.cloned.1.call-start = ((), (), s32[]{:S(2)}) async-start(), calls=%async_computation.9 | async-start | bytes 4866048 | tf_op jit(solution)/shard_map/all_gather | solution.py:103
  7.9 311.0 %all-gather.12.cloned.1.call-start = ((), (), s32[]{:S(2)}) async-start(), calls=%async_computation.10 | async-start | bytes 4325376 | tf_op jit(solution)/shard_map/all_gather | solution.py:102
  8.7 321.9 %all-gather.14.cloned.1.call-start = ((), (), s32[]{:S(2)}) async-start(), calls=%async_computation.11 | async-start | bytes 4325376 | tf_op jit(solution)/shard_map/all_gather | solution.py:108
  9.4 327.1 %all-gather.16.cloned.1.call-start = ((), (), s32[]{:S(2)}) async-start(), calls=%async_computation.12 | async-start | bytes 6488064 | tf_op jit(solution)/shard_map/all_gather | solution.py:169
  10.0 367.8 %all-gather.18.cloned.1.call-start = ((), (), s32[]{:S(2)}) async-start(), calls=%async_computation.13 | async-start | bytes 2162688 | tf_op jit(solution)/shard_map/all_gather | solution.py:170
  10.6 404.5 %all-gather.22.cloned.1.call-start = ((), (), s32[]{:S(2)}) async-start(), calls=%async_computation.15 | async-start | bytes 8650752 | tf_op jit(solution)/shard_map/all_gather | solution.py:203
  11.1 482.9 %all-gather.20.cloned.1.call-start = ((), (), s32[]{:S(2)}) async-start(), calls=%async_computation.14 | async-start | bytes 8650752 | tf_op jit(solution)/shard_map/all_gather | solution.py:202
  11.9 561.2 %all-gather.24.cloned.1.call-start = ((), (), s32[]{:S(2)}) async-start(), calls=%async_computation.16 | async-start | bytes 8650752 | tf_op jit(solution)/shard_map/all_gather | solution.py:204
  12.6 848.3 %all-reduce.34.cloned.1.call-start = ((), (), s32[]{:S(2)}) async-start(), calls=%async_computation.27 | async-start | bytes 143360 | tf_op jit(solution)/shard_map/psum | solution.py:364
  15.6 77.1 %copy-start.63 = (s32[3328]{0:T(1024)}, s32[3328]{0:T(1024)S(1)}, u32[]{:S(2)}) copy-start(s32[3328]{0:T(1024)S(1)} %eq.49) | copy-start | bytes 39940
  137.8 146.4 %copy-start.61 = (f32[1024]{0:T(1024)}, f32[1024]{0:T(1024)S(1)}, u32[]{:S(2)}) copy-start(f32[1024]{0:T(1024)S(1)} %get-tuple-element.97) | copy-start | bytes 12292
  211.8 72.4 %copy-start.19 = (bf16[2,208,1024]{2,1,0:T(8,128)(2,1)S(1)}, bf16[2,208,1024]{2,1,0:T(8,128)(2,1)}, u32[]{:S(2)}) copy-start(bf16[2,208,1024]{2,1,0:T(8,128)(2,1)} %param.23) | copy-start | bytes 2555908
  336.5 314.7 %copy-start.85 = (f32[416]{0:T(512)}, f32[416]{0:T(512)S(1)}, u32[]{:S(2)}) copy-start(f32[416]{0:T(512)S(1)} %fusion.85) | copy-start | bytes 4996
  382.8 111.3 %copy-start.43 = (bf16[416,1024]{1,0:T(8,128)(2,1)}, bf16[416,1024]{1,0:T(8,128)(2,1)S(1)}, u32[]{:S(2)}) copy-start(bf16[416,1024]{1,0:T(8,128)(2,1)S(1)} %multiply_convert_fusion.15) | copy-start | bytes 2555908
  738.1 254.4 %all-reduce.32.cloned.1.call-start = ((), (), s32[]{:S(2)}) async-start(), calls=%async_computation.26 | async-start | bytes 262144
  741.7 386.5 %reduce-scatter.15.cloned.1.call-start = ((), (), s32[]{:S(2)}) async-start(), calls=%async_computation.19 | async-start | bytes 540672 | tf_op jit(solution)/shard_map/reduce_scatter | solution.py:358
  744.3 524.1 %reduce-scatter.21.cloned.1.call-start = ((), (), s32[]{:S(2)}) async-start(), calls=%async_computation.22 | async-start | bytes 4325376 | tf_op jit(solution)/shard_map/reduce_scatter | solution.py:302
  747.7 660.7 %reduce-scatter.13.cloned.1.call-start = ((), (), s32[]{:S(2)}) async-start(), calls=%async_computation.18 | async-start | bytes 9732096 | tf_op jit(solution)/shard_map/reduce_scatter | solution.py:357
  754.6 839.3 %reduce-scatter.11.cloned.1.call-start = ((), (), s32[]{:S(2)}) async-start(), calls=%async_computation.17 | async-start | bytes 8650752 | tf_op jit(solution)/shard_map/reduce_scatter | solution.py:356
  761.8 1019.4 %reduce-scatter.17.cloned.1.call-start = ((), (), s32[]{:S(2)}) async-start(), calls=%async_computation.20 | async-start | bytes 8650752 | tf_op jit(solution)/shard_map/reduce_scatter | solution.py:362
  769.5 1175.6 %reduce-scatter.19.cloned.1.call-start = ((), (), s32[]{:S(2)}) async-start(), calls=%async_computation.21 | async-start | bytes 12976128 | tf_op jit(solution)/shard_map/reduce_scatter | solution.py:301
  779.5 1525.1 %reduce-scatter.27.cloned.1.call-start = ((), (), s32[]{:S(2)}) async-start(), calls=%async_computation.25 | async-start | bytes 17301504 | tf_op jit(solution)/shard_map/reduce_scatter | solution.py:248
  790.8 1875.5 %reduce-scatter.25.cloned.1.call-start = ((), (), s32[]{:S(2)}) async-start(), calls=%async_computation.24 | async-start | bytes 17301504 | tf_op jit(solution)/shard_map/reduce_scatter | solution.py:247
  802.0 2226.2 %reduce-scatter.23.cloned.1.call-start = ((), (), s32[]{:S(2)}) async-start(), calls=%async_computation.23 | async-start | bytes 17301504 | tf_op jit(solution)/shard_map/reduce_scatter | solution.py:246
  (107 other events, 808.0 us)
Sparse Core Ops, SparseCore 0:
  10.9 66.5 all-gather.9
  80.4 61.1 all-gather.11
  144.5 60.7 all-gather.13
  208.0 69.0 all-gather.15
  279.8 56.0 all-gather.17
  338.6 76.3 all-gather.21
  417.9 76.1 all-gather.19
  497.0 76.1 all-gather.23
  738.2 122.6 all-reduce.33
  867.2 125.1 all-reduce.31
  995.4 132.8 reduce-scatter.14
  1131.0 137.3 reduce-scatter.20
  1274.8 133.4 reduce-scatter.12
  1411.2 182.6 reduce-scatter.10
  1596.7 184.4 reduce-scatter.16
  1788.7 156.3 reduce-scatter.18
  1947.8 356.6 reduce-scatter.26
  2307.3 358.9 reduce-scatter.24
  2669.2 358.9 reduce-scatter.22
where the time goes:
time: 3050 us; the launch traced here: 3040 us
  waiting for transfers between devices  2380 us (78%)
  blocking collectives  241 us (8%)
  matrix products  214 us (7%)
  local copies, waits for them, and re-layouts  123 us (4%)
  other arithmetic  61.1 us (2%)
    reduce_scatter x1, waiting for transfers between devices, local(): lax.psum_scatter(grad_ffn_gate, ('dp', 'fsdp'), scatter_dimension=0, tile...  362 us
    reduce_scatter x1, waiting for transfers between devices, local(): lax.psum_scatter(grad_ffn_up, ('dp', 'fsdp'), scatter_dimension=0, tiled=...  362 us
    reduce_scatter x1, waiting for transfers between devices, local(): lax.psum_scatter(grad_ffn_down, ('dp', 'fsdp'), scatter_dimension=0, tile...  359 us
    reduce_scatter x1, waiting for transfers between devices, local(): lax.psum_scatter(grad_proj_mixed, ('dp', 'fsdp'), scatter_dimension=0, ti...  187 us
    reduce_scatter x1, waiting for transfers between devices, local(): lax.psum_scatter(grad_proj_zgate, ('dp', 'fsdp'), scatter_dimension=0, ti...  186 us
    reduce_scatter x1, waiting for transfers between devices, local(): lax.psum_scatter(grad_proj_heads, ('dp', 'fsdp'), scatter_dimension=0, ti...  164 us
    reduce_scatter x1, waiting for transfers between devices, local(): lax.psum_scatter(grad_proj_attended, ('dp', 'fsdp'), scatter_dimension=0,...  140 us
    reduce_scatter x1, waiting for transfers between devices, local(): lax.psum_scatter(grad_proj_inputs, ('dp', 'fsdp'), scatter_dimension=0, t...  140 us
  transfers between devices with their start and end apart: 19, of which 14 were waited for; matrix products, arithmetic and copies ran while one was open for 7% of the time, Pallas kernels for 0%

commit v1 on v0

--- a/solution.py
+++ b/solution.py
@@ -3,6 +3,8 @@
 import jax
 import jax.numpy as jnp
 from jax import lax
+from jax.experimental import pallas as pl
+from jax.experimental.pallas import tpu as pltpu
 from jax.sharding import PartitionSpec as P
 
 DI = 2048
@@ -66,6 +68,188 @@
 
 def silu_product(gate_raw, upper_raw):
     return jax.nn.silu(gate_raw) * upper_raw
+
+
+AXES = ("dp", "fsdp")
+
+
+def axis_bits():
+    bits = []
+    for name in AXES:
+        size = lax.axis_size(name)
+        step = size // 2
+        while step:
+            bits.append((name, size, step))
+            step //= 2
+    return bits
+
+
+def phases(flip):
+    bits = axis_bits()
+    outer = [k for k, b in enumerate(bits) if b[0] == "dp" and b[2] > 1]
+    core = [k for k, b in enumerate(bits) if b[0] == "dp" and b[2] == 1]
+    inner = [k for k, b in enumerate(bits) if b[0] == "fsdp"]
+    return bits, outer[::-1] + (inner if flip else inner[::-1]) + core
+
+
+def swap(v, bit):
+    name, size, step = bit
+    return lax.ppermute(v, name, [(i, i ^ step) for i in range(size)])
+
+
+def own_bit(bit):
+    return (lax.axis_index(bit[0]) // bit[2]) % 2
+
+
+def own_index():
+    return lax.axis_index("dp") * lax.axis_size("fsdp") + lax.axis_index("fsdp")
+
+
+def bit_weight(bit):
+    return bit[2] * (lax.axis_size("fsdp") if bit[0] == "dp" else 1)
+
+
+def assemble_kernel(offsets, me_ref, *refs):
+    pieces, out_ref, sems = refs[:-2], refs[-2], refs[-1]
+    me = me_ref[0]
+    copies = []
+    count = 0
+    for piece, places in zip(pieces, offsets):
+        for j, place in enumerate(places):
+            copies.append(
+                pltpu.make_async_copy(piece.at[j], out_ref.at[me ^ place], sems.at[count])
+            )
+            count += 1
+    for c in copies:
+        c.start()
+    for c in copies:
+        c.wait()
+
+
+def tie(*values):
+    return lax.optimization_barrier(values)
+
+
+class Gather:
+    def __init__(self, shard, flip):
+        self.rows, self.columns = shard.shape
+        self.bits, self.order = phases(flip)
+        self.pieces = [(shard[None], [0])]
+        self.phase = 0
+
+    def step(self):
+        k = self.order[self.phase]
+        weight = bit_weight(self.bits[k])
+        if len(self.pieces) > 1 and self.phase < len(self.order) - 1:
+            joined = jnp.concatenate([p for p, _ in self.pieces], axis=0)
+            self.pieces = [(joined, sum((o for _, o in self.pieces), []))]
+        self.pieces = self.pieces + [
+            (swap(p, self.bits[k]), [o ^ weight for o in offs]) for p, offs in self.pieces
+        ]
+        self.phase += 1
+
+    def last(self):
+        return self.pieces[-1][0]
+
+    def set_first(self, v):
+        self.pieces[0] = (v, self.pieces[0][1])
+
+    def done(self):
+        while self.phase < len(self.order):
+            self.step()
+        count = 2 ** len(self.bits)
+        me = own_index().astype(jnp.int32).reshape(1)
+        out = pl.pallas_call(
+            partial(assemble_kernel, [o for _, o in self.pieces]),
+            out_shape=jax.ShapeDtypeStruct((count, self.rows, self.columns), jnp.bfloat16),
+            in_specs=[pl.BlockSpec(memory_space=pltpu.SMEM)]
+            + [pl.BlockSpec(memory_space=pl.ANY)] * len(self.pieces),
+            out_specs=pl.BlockSpec(memory_space=pltpu.VMEM),
+            scratch_shapes=[pltpu.SemaphoreType.DMA((count,))],
+            compiler_params=pltpu.CompilerParams(vmem_limit_bytes=24 * 1024 * 1024),
+        )(me, *[p for p, _ in self.pieces])
+        return out.reshape(count * self.rows, self.columns)
+
+
+def gather_small(shard):
+    bits = axis_bits()
+    out = shard[None]
+    for bit in bits[::-1]:
+        other = swap(out, bit)
+        mine = own_bit(bit) == 0
+        out = jnp.concatenate([jnp.where(mine, out, other), jnp.where(mine, other, out)], axis=0)
+    return out
+
+
+def scatter_sum(part, flip, core_done, wide=False):
+    bits, order = phases(flip)
+    names = [k for k in range(len(bits)) if not (core_done and bits[k][0] == "dp" and bits[k][2] == 1)]
+    count = 2 ** len(names)
+    part = part.reshape([2] * len(names) + [part.shape[0] // count, part.shape[1]])
+    for n, k in enumerate([k for k in order[::-1] if k in names]):
+        axis = names.index(k)
+        names.remove(k)
+        mine = own_bit(bits[k])
+        send = lax.dynamic_index_in_dim(part, 1 - mine, axis, keepdims=False)
+        keep = lax.dynamic_index_in_dim(part, mine, axis, keepdims=False)
+        total = keep.astype(jnp.float32) + swap(send, bits[k]).astype(jnp.float32)
+        part = total if not names else total.astype(part.dtype)
+    return part.astype(jnp.float32)
+
+
+def core_columns(former, core):
+    outer = lax.axis_size("dp") // 2
+    group = former.shape[1] // (2 * outer)
+    return jnp.concatenate(
+        [lax.dynamic_slice_in_dim(former, (2 * i + core) * group, group, 1) for i in range(outer)],
+        axis=1,
+    )
+
+
+class Scatter:
+    def __init__(self, former, latter, flip):
+        self.bits, order = phases(flip)
+        self.core = [k for k, b in enumerate(self.bits) if b[0] == "dp" and b[2] == 1][0]
+        mine = own_bit(self.bits[self.core])
+        send = matmul_left(core_columns(former, 1 - mine), latter).astype(jnp.bfloat16)
+        self.received = swap(send, self.bits[self.core])
+        self.keep = matmul_left(core_columns(former, mine), latter)
+        self.names = [k for k in range(len(self.bits)) if k != self.core]
+        self.order = [k for k in order[::-1] if k != self.core]
+        self.shape = None
+
+    def step(self):
+        total = self.keep.astype(jnp.float32) + self.received.astype(jnp.float32)
+        if not self.names:
+            self.keep = total
+            return
+        part = total.astype(jnp.bfloat16)
+        if self.shape is None:
+            count = 2 ** len(self.names)
+            self.shape = part.shape
+            part = part.reshape([2] * len(self.names) + [part.shape[0] // count, part.shape[1]])
+        k = self.order.pop(0)
+        axis = self.names.index(k)
+        self.names.remove(k)
+        mine = own_bit(self.bits[k])
+        self.received = swap(
+            lax.dynamic_index_in_dim(part, 1 - mine, axis, keepdims=False), self.bits[k]
+        )
+        self.keep = lax.dynamic_index_in_dim(part, mine, axis, keepdims=False)
+
+    def done(self):
+        while self.names:
+            self.step()
+        self.step()
+        return self.keep
+
+
+def advance(value, *pipes):
+    tied = tie(value, *[p.received for p in pipes])
+    for p, received in zip(pipes, tied[1:]):
+        p.received = received
+        p.step()
+    return tied[0]
 
 
 def local(
@@ -96,28 +280,63 @@
     row_count, length = segment_ids.shape
     tokens = row_count * length
     model_width = context.shape[2]
-    mixer_full = (
-        lax.all_gather(byte_table, ("dp", "fsdp"), axis=0, tiled=True),
-        lax.all_gather(norm_mixer, ("dp", "fsdp"), axis=0, tiled=True),
-        lax.all_gather(proj_zgate, ("dp", "fsdp"), axis=0, tiled=True),
-        lax.all_gather(proj_inputs, ("dp", "fsdp"), axis=0, tiled=True),
-        lax.all_gather(proj_step, ("dp", "fsdp"), axis=0, tiled=True),
-        lax.all_gather(conv_kernel, ("dp", "fsdp"), axis=1, tiled=True),
-        lax.all_gather(conv_bias, ("dp", "fsdp"), axis=0, tiled=True),
-        lax.all_gather(mixer_norm, ("dp", "fsdp"), axis=0, tiled=True),
-        lax.all_gather(proj_mixed, ("dp", "fsdp"), axis=0, tiled=True),
-    )
-    (
-        table_full,
-        gain_one,
-        zgate_full,
-        inputs_full,
-        step_full,
-        kernel_full,
-        offset_full,
-        gated_gain,
-        mixed_full,
-    ) = mixer_full
+    model_rows = norm_mixer.shape[0]
+    small = [
+        byte_table.reshape(-1),
+        norm_mixer,
+        conv_kernel.reshape(-1),
+        conv_bias,
+        mixer_norm,
+        norm_attn,
+        norm_ffn,
+    ]
+    lengths = [v.shape[0] for v in small]
+    packed = jnp.concatenate(small)
+    packed = jnp.pad(packed, (0, -packed.shape[0] % 1024)).reshape(8, -1)
+    everyone = gather_small(packed).reshape(-1, packed.size)
+    unpacked = []
+    start = 0
+    for count in lengths:
+        unpacked.append(everyone[:, start : start + count])
+        start += count
+    table_full = unpacked[0].reshape(-1, byte_table.shape[1])
+    gain_one = unpacked[1].reshape(-1)
+    taps = conv_kernel.shape[0]
+    kernel_full = jnp.swapaxes(
+        unpacked[2].reshape(-1, taps, conv_kernel.shape[1]), 0, 1
+    ).reshape(taps, -1)
+    offset_full = unpacked[3].reshape(-1)
+    gated_gain = unpacked[4].reshape(-1)
+    gain_two = unpacked[5].reshape(-1)
+    gain_three = unpacked[6].reshape(-1)
+    wide = proj_inputs.shape[1]
+    step_padded = jnp.pad(proj_step, ((0, 0), (0, 128 - proj_step.shape[1])))
+    g_inputs = Gather(jnp.concatenate([proj_inputs, step_padded], axis=1), False)
+    g_zgate = Gather(proj_zgate, True)
+    g_mixed = Gather(proj_mixed, False)
+    g_heads = Gather(proj_heads, True)
+    g_attended = Gather(proj_attended, False)
+    g_gate = Gather(ffn_gate, False)
+    g_upper = Gather(ffn_up, True)
+    g_down = Gather(ffn_down, False)
+    before = None
+    for several in ([g_inputs, g_zgate], [g_mixed, g_heads], [g_attended, g_gate], [g_upper], [g_down]):
+        if before is not None:
+            tied = tie(*[g.pieces[0][0] for g in several], *[g.last() for g in before])
+            for g, v in zip(several, tied):
+                g.set_first(v)
+        for g in several:
+            g.step()
+            g.step()
+        before = several
+    inputs_step_full = g_inputs.done()
+    zgate_full = g_zgate.done()
+    mixed_full = g_mixed.done()
+    heads_full = g_heads.done()
+    attended_full = g_attended.done()
+    gate_full = g_gate.done()
+    upper_full = g_upper.done()
+    down_full = g_down.done()
     symbols = jnp.arange(table_full.shape[0], dtype=jnp.int32)
     onehot = (byte_ids.reshape(-1)[:, None] == symbols[None, :]).astype(jnp.bfloat16)
     embedded = matmul(onehot, table_full).reshape(tokens, model_width)
@@ -128,8 +347,9 @@
     normed_one, norm_one_back = jax.vjp(rms_norm, stream_zero, gain_one.astype(jnp.float32))
     normed_one_low = normed_one.astype(jnp.bfloat16)
     zgate = matmul(normed_one_low, zgate_full)
-    inputs_raw = matmul(normed_one_low, inputs_full)
-    step_raw = matmul(normed_one_low, step_full)
+    inputs_step = matmul(normed_one_low, inputs_step_full)
+    inputs_raw = inputs_step[:, :wide]
+    step_raw = inputs_step[:, wide : wide + HM]
     activated, conv_back = jax.vjp(
         partial(conv_silu, segments=segment_ids),
         inputs_raw.reshape(row_count, length, -1),
@@ -164,12 +384,6 @@
     gate_low = normed_gate.reshape(tokens, -1).astype(jnp.bfloat16)
     mixer_out = matmul(gate_low, mixed_full)
     stream_one = stream_zero + mixer_out
-    attention_full = (
-        lax.all_gather(norm_attn, ("dp", "fsdp"), axis=0, tiled=True),
-        lax.all_gather(proj_heads, ("dp", "fsdp"), axis=0, tiled=True),
-        lax.all_gather(proj_attended, ("dp", "fsdp"), axis=0, tiled=True),
-    )
-    gain_two, heads_full, attended_full = attention_full
     normed_two, norm_two_back = jax.vjp(rms_norm, stream_one, gain_two.astype(jnp.float32))
     normed_two_low = normed_two.astype(jnp.bfloat16)
     joined = matmul(normed_two_low, heads_full)
@@ -197,13 +411,6 @@
     attended_low = attended.reshape(tokens, model_width).astype(jnp.bfloat16)
     attn_out = matmul(attended_low, attended_full)
     stream_two = stream_one + attn_out
-    ffn_full = (
-        lax.all_gather(norm_ffn, ("dp", "fsdp"), axis=0, tiled=True),
-        lax.all_gather(ffn_gate, ("dp", "fsdp"), axis=0, tiled=True),
-        lax.all_gather(ffn_up, ("dp", "fsdp"), axis=0, tiled=True),
-        lax.all_gather(ffn_down, ("dp", "fsdp"), axis=0, tiled=True),
-    )
-    gain_three, gate_full, upper_full, down_full = ffn_full
     normed_three, norm_three_back = jax.vjp(rms_norm, stream_two, gain_three.astype(jnp.float32))
     normed_three_low = normed_three.astype(jnp.bfloat16)
     gate_pre = matmul(normed_three_low, gate_full)
@@ -222,42 +429,29 @@
             jnp.sum(valid_rows),
         ]
     )
-    gate_use, upper_use, down_use = (
-        lax.all_gather(ffn_gate, ("dp", "fsdp"), axis=0, tiled=True),
-        lax.all_gather(ffn_up, ("dp", "fsdp"), axis=0, tiled=True),
-        lax.all_gather(ffn_down, ("dp", "fsdp"), axis=0, tiled=True),
-    )
     grad_three = cotangent.reshape(tokens, model_width).astype(jnp.float32)
     ffn_grad_low = grad_three.astype(jnp.bfloat16)
-    grad_ffn_down = matmul_left(hidden_low, ffn_grad_low)
-    grad_hidden = matmul_right(ffn_grad_low, down_use)
+    grad_ffn_down = Scatter(hidden_low, ffn_grad_low, False)
+    grad_hidden = matmul_right(ffn_grad_low, down_full)
     grad_gate_pre, grad_up_pre = hidden_back(grad_hidden)
     gate_grad_low = grad_gate_pre.astype(jnp.bfloat16)
     upper_grad_low = grad_up_pre.astype(jnp.bfloat16)
-    grad_ffn_gate = matmul_left(normed_three_low, gate_grad_low)
-    grad_ffn_up = matmul_left(normed_three_low, upper_grad_low)
-    grad_normed_three = matmul_right(gate_grad_low, gate_use) + matmul_right(
-        upper_grad_low, upper_use
+    grad_ffn_gate = Scatter(normed_three_low, gate_grad_low, True)
+    grad_ffn_up = Scatter(normed_three_low, upper_grad_low, False)
+    grad_normed_three = matmul_right(gate_grad_low, gate_full) + matmul_right(
+        upper_grad_low, upper_full
     )
     stream_part, grad_norm_ffn = norm_three_back(grad_normed_three)
     grad_two = grad_three + stream_part
-    ffn_sums = (
-        lax.psum_scatter(grad_norm_ffn, ("dp", "fsdp"), scatter_dimension=0, tiled=True),
-        lax.psum_scatter(grad_ffn_gate, ("dp", "fsdp"), scatter_dimension=0, tiled=True),
-        lax.psum_scatter(grad_ffn_up, ("dp", "fsdp"), scatter_dimension=0, tiled=True),
-        lax.psum_scatter(grad_ffn_down, ("dp", "fsdp"), scatter_dimension=0, tiled=True),
-    )
-    heads_use, attended_use = (
-        lax.all_gather(proj_heads, ("dp", "fsdp"), axis=0, tiled=True),
-        lax.all_gather(proj_attended, ("dp", "fsdp"), axis=0, tiled=True),
-    )
     attn_grad_low = grad_two.astype(jnp.bfloat16)
-    grad_proj_attended = matmul_left(attended_low, attn_grad_low)
+    attn_grad_low = advance(attn_grad_low, grad_ffn_down)
+    grad_proj_attended = Scatter(attended_low, attn_grad_low, False)
     grad_attended = (
-        matmul_right(attn_grad_low, attended_use)
+        matmul_right(attn_grad_low, attended_full)
         .astype(jnp.bfloat16)
         .reshape(row_count, length, HA, HD)
     )
+    grad_attended = advance(grad_attended, grad_ffn_gate, grad_ffn_up)
     rescored = (
         jnp.einsum("nthd,nshd->nhts", query_low, key_low, preferred_element_type=jnp.float32)
         * scale
@@ -276,6 +470,7 @@
     grad_scores = (
         probs_again * (grad_probs - jnp.sum(probs_again * grad_probs, axis=-1, keepdims=True))
     ).astype(jnp.bfloat16)
+    grad_scores = advance(grad_scores, grad_ffn_down)
     grad_query = (
         jnp.einsum("nhts,nshd->nthd", grad_scores, key_low, preferred_element_type=jnp.float32)
         * scale
@@ -292,28 +487,21 @@
         ],
         axis=1,
     ).astype(jnp.bfloat16)
-    grad_proj_heads = matmul_left(normed_two_low, grad_joined)
-    grad_normed_two = matmul_right(grad_joined, heads_use)
+    grad_proj_heads = Scatter(normed_two_low, grad_joined, True)
+    grad_joined = advance(grad_joined, grad_ffn_down, grad_ffn_gate, grad_ffn_up)
+    grad_normed_two = matmul_right(grad_joined, heads_full)
     stream_part_two, grad_norm_attn = norm_two_back(grad_normed_two)
     grad_one = grad_two + stream_part_two
-    attention_sums = (
-        lax.psum_scatter(grad_norm_attn, ("dp", "fsdp"), scatter_dimension=0, tiled=True),
-        lax.psum_scatter(grad_proj_heads, ("dp", "fsdp"), scatter_dimension=0, tiled=True),
-        lax.psum_scatter(grad_proj_attended, ("dp", "fsdp"), scatter_dimension=0, tiled=True),
-    )
-    zgate_use, inputs_use, step_use, mixed_use = (
-        lax.all_gather(proj_zgate, ("dp", "fsdp"), axis=0, tiled=True),
-        lax.all_gather(proj_inputs, ("dp", "fsdp"), axis=0, tiled=True),
-        lax.all_gather(proj_step, ("dp", "fsdp"), axis=0, tiled=True),
-        lax.all_gather(proj_mixed, ("dp", "fsdp"), axis=0, tiled=True),
-    )
     mixer_grad_low = grad_one.astype(jnp.bfloat16)
-    grad_proj_mixed = matmul_left(gate_low, mixer_grad_low)
-    grad_normed_gate = matmul_right(mixer_grad_low, mixed_use).reshape(row_count, length, -1)
+    grad_proj_mixed = Scatter(gate_low, mixer_grad_low, False)
+    grad_normed_gate = matmul_right(mixer_grad_low, mixed_full).reshape(row_count, length, -1)
     grad_heads, grad_skip_values, grad_zgate, grad_skip_gain, grad_gated_gain = gate_back(
         grad_normed_gate
     )
     heads_grad_low = grad_heads.astype(jnp.bfloat16)
+    heads_grad_low = advance(
+        heads_grad_low, grad_ffn_down, grad_ffn_gate, grad_ffn_up, grad_proj_attended, grad_proj_heads
+    )
     grad_weights = jnp.einsum(
         "nthp,nshp->nhts", heads_grad_low, values_low, preferred_element_type=jnp.float32
     )
@@ -323,8 +511,14 @@
         )
         + grad_skip_values
     )
+    grad_weights = advance(
+        grad_weights, grad_ffn_gate, grad_ffn_up, grad_proj_attended, grad_proj_heads, grad_proj_mixed
+    )
     grad_gram, grad_step_raw, grad_step_bias, grad_decay_log = weights_back(grad_weights)
     gram_grad_low = grad_gram.astype(jnp.bfloat16)
+    gram_grad_low = advance(
+        gram_grad_low, grad_proj_attended, grad_proj_heads, grad_proj_mixed
+    )
     grad_state_out = jnp.einsum(
         "nts,nsk->ntk", gram_grad_low, state_in, preferred_element_type=jnp.float32
     )
@@ -338,56 +532,83 @@
     zgate_grad_low = grad_zgate.reshape(tokens, -1).astype(jnp.bfloat16)
     inputs_grad_low = grad_inputs_raw.reshape(tokens, -1).astype(jnp.bfloat16)
     step_grad_low = grad_step_raw.reshape(tokens, -1).astype(jnp.bfloat16)
-    grad_proj_zgate = matmul_left(normed_one_low, zgate_grad_low)
-    grad_proj_inputs = matmul_left(normed_one_low, inputs_grad_low)
-    grad_proj_step = matmul_left(normed_one_low, step_grad_low)
-    grad_normed_one = (
-        matmul_right(zgate_grad_low, zgate_use)
-        + matmul_right(inputs_grad_low, inputs_use)
-        + matmul_right(step_grad_low, step_use)
+    grad_proj_zgate = Scatter(normed_one_low, zgate_grad_low, True)
+    inputs_step_grad_low = jnp.concatenate(
+        [inputs_grad_low, jnp.pad(step_grad_low, ((0, 0), (0, 128 - step_grad_low.shape[1])))], axis=1
+    )
+    grad_inputs_step = Scatter(normed_one_low, inputs_step_grad_low, False)
+    grad_normed_one = matmul_right(zgate_grad_low, zgate_full) + matmul_right(
+        inputs_step_grad_low, inputs_step_full
     )
     stream_part_one, grad_norm_mixer = norm_one_back(grad_normed_one)
     grad_zero = grad_one + stream_part_one
     embed_grad_low = grad_zero.reshape(-1, table_full.shape[1]).astype(jnp.bfloat16)
     grad_byte_table = matmul_left(onehot, embed_grad_low)
-    mixer_sums = (
-        lax.psum_scatter(grad_byte_table, ("dp", "fsdp"), scatter_dimension=0, tiled=True),
-        lax.psum_scatter(grad_norm_mixer, ("dp", "fsdp"), scatter_dimension=0, tiled=True),
-        lax.psum_scatter(grad_proj_zgate, ("dp", "fsdp"), scatter_dimension=0, tiled=True),
-        lax.psum_scatter(grad_proj_inputs, ("dp", "fsdp"), scatter_dimension=0, tiled=True),
-        lax.psum_scatter(grad_proj_step, ("dp", "fsdp"), scatter_dimension=0, tiled=True),
-        lax.psum_scatter(grad_conv_kernel, ("dp", "fsdp"), scatter_dimension=1, tiled=True),
-        lax.psum_scatter(grad_conv_bias, ("dp", "fsdp"), scatter_dimension=0, tiled=True),
-        lax.psum_scatter(grad_gated_gain, ("dp", "fsdp"), scatter_dimension=0, tiled=True),
-        lax.psum_scatter(grad_proj_mixed, ("dp", "fsdp"), scatter_dimension=0, tiled=True),
-    )
-    totals, bias_total, decay_total, skip_total = lax.psum(
-        (moments, grad_step_bias, grad_decay_log, grad_skip_gain), ("dp", "fsdp")
-    )
+    late = jnp.concatenate(
+        [
+            grad_byte_table.reshape(-1, byte_table.size),
+            grad_norm_mixer.reshape(-1, model_rows),
+        ],
+        axis=1,
+    )
+    late = jnp.pad(late, ((0, 0), (0, -late.shape[1] % 1024)))
+    late = scatter_sum(late, False, False).reshape(-1)
+    table_sum = late[: byte_table.size].reshape(byte_table.shape)
+    norm_mixer_sum = late[byte_table.size : byte_table.size + model_rows]
+    (
+        totals,
+        bias_total,
+        decay_total,
+        skip_total,
+        kernel_sum,
+        offset_sum,
+        gated_sum,
+        norm_attn_sum,
+        norm_ffn_sum,
+    ) = lax.psum(
+        (
+            moments,
+            grad_step_bias,
+            grad_decay_log,
+            grad_skip_gain,
+            grad_conv_kernel,
+            grad_conv_bias,
+            grad_gated_gain,
+            grad_norm_attn,
+            grad_norm_ffn,
+        ),
+        ("dp", "fsdp"),
+    )
+
+    def own_part(total, share):
+        length = share.shape[-1]
+        return lax.dynamic_slice_in_dim(total, own_index() * length, length, total.ndim - 1)
+
+    grad_inputs_step = grad_inputs_step.done()
     rms_stats = jnp.sqrt(totals[:4] / (totals[4] * model_width))
     return (
         stream_three.reshape(row_count, length, model_width),
         grad_zero.reshape(row_count, length, model_width),
         rms_stats,
-        mixer_sums[0],
-        mixer_sums[1],
-        mixer_sums[2],
-        mixer_sums[3],
-        mixer_sums[4],
-        mixer_sums[5],
-        mixer_sums[6],
+        table_sum,
+        norm_mixer_sum,
+        grad_proj_zgate.done(),
+        grad_inputs_step[:, :wide],
+        grad_inputs_step[:, wide : wide + HM],
+        own_part(kernel_sum, conv_kernel),
+        own_part(offset_sum, conv_bias),
         bias_total,
         decay_total,
         skip_total,
-        mixer_sums[7],
-        mixer_sums[8],
-        attention_sums[0],
-        attention_sums[1],
-        attention_sums[2],
-        ffn_sums[0],
-        ffn_sums[1],
-        ffn_sums[2],
-        ffn_sums[3],
+        own_part(gated_sum, mixer_norm),
+        grad_proj_mixed.done(),
+        own_part(norm_attn_sum, norm_attn),
+        grad_proj_heads.done(),
+        grad_proj_attended.done(),
+        own_part(norm_ffn_sum, norm_ffn),
+        grad_ffn_gate.done(),
+        grad_ffn_up.done(),
+        grad_ffn_down.done(),
     )
 
 

time: 3050 us -> 986 us (0.32)
  waiting for transfers between devices: 2380 us -> 326 us
  blocking collectives: 241 us -> 40.8 us
  starting transfers between devices: 1.14 us -> 86.7 us
  other arithmetic: 61.1 us -> 120 us
  local copies, waits for them, and re-layouts: 123 us -> 164 us
  Pallas kernels: 0 us -> 34.5 us
    reduce_scatter x9 -> x0, waiting for transfers between devices: 2030 us -> none  [the longest x1 362 us: local(): lax.psum_scatter(grad_ffn_gate, ('dp', 'fsdp'), scatter_dimension=0, tile...]
    ppermute x0 -> x98, waiting for transfers between devices: none -> 326 us  [swap(): return lax.ppermute(v, name, [(i, i ^ step) for i in range(size)])]
    all_gather x3 -> x0, blocking collectives: 203 us -> none  [the longest x1 70.8 us: local(): lax.all_gather(byte_table, ('dp', 'fsdp'), axis=0, tiled=True)]
    all_gather x8 -> x0, waiting for transfers between devices: 172 us -> none  [the longest x1 70.1 us: local(): lax.all_gather(ffn_gate, ('dp', 'fsdp'), axis=0, tiled=True)]
    unnamed x20 -> x0, waiting for transfers between devices: 126 us -> none
    ppermute x0 -> x98, starting transfers between devices: none -> 86.7 us  [swap(): return lax.ppermute(v, name, [(i, i ^ step) for i in range(size)])]
    psum x1 -> x0, waiting for transfers between devices: 48.7 us -> none  [local(): lax.psum((moments, grad_step_bias, grad_decay_log, grad_skip_gain), ('dp'...]
    convert_element_type x2 -> x32, other arithmetic: 2.66 us -> 48.5 us  [the longest x29 44 us: step(): part = total.astype(jnp.bfloat16)]
  transfers between devices with their start and end apart: 19 -> 98, of which waited for: 14 -> 37; matrix products, arithmetic and copies ran while one was open for 7% -> 41% of each run, Pallas kernels for 0% -> 3%
where the time goes in v1:
time: 986 us; the launch traced here: 974 us
  waiting for transfers between devices  326 us (33%)
  matrix products  196 us (20%)
  local copies, waits for them, and re-layouts  164 us (17%)
  other arithmetic  120 us (12%)
  starting transfers between devices  86.7 us (9%)
  blocking collectives  40.8 us (4%)
  Pallas kernels  34.5 us (3%)
    ppermute x98, waiting for transfers between devices, swap(): return lax.ppermute(v, name, [(i, i ^ step) for i in range(size)])  326 us
    ppermute x98, starting transfers between devices, swap(): return lax.ppermute(v, name, [(i, i ^ step) for i in range(size)])  86.7 us
    dot_general x17, matrix products, matmul_left(): lax.dot_general(former, latter, (((0,), (0,)), ((), ())), preferred_eleme...  62.5 us
    dot_general x9, matrix products, matmul(): return jnp.dot(former, latter, preferred_element_type=jnp.float32)  52.4 us
    convert_element_type x29, other arithmetic, step(): part = total.astype(jnp.bfloat16)  44 us
    psum x1, blocking collectives, local(): lax.psum((moments, grad_step_bias, grad_decay_log, grad_skip_gain, grad_c...  40.8 us
    dot_general x8, matrix products, matmul_right(): lax.dot_general(former, latter, (((1,), (1,)), ((), ())), preferred_eleme...  36.3 us
    pallas_call x8, Pallas kernels, done(): pl.pallas_call(partial(assemble_kernel, [o for _, o in self.pieces]), out...  34.5 us
  transfers between devices with their start and end apart: 98, of which 37 were waited for; matrix products, arithmetic and copies ran while one was open for 41% of the time, Pallas kernels for 3%

profile of v1, /device:TPU:0, one launch (start us, length us, event | category | flops | bytes accessed | tf_op | source)
XLA Modules:
  0.0 974.3 jit_solution(9406447547782946458)
XLA Ops:
  64.3 12.2 %collective-permute-done.12 = bf16[2,32,2048]{2,1,0:T(8,128)(2,1)S(1)} collective-permute-done((bf16[2,32,2048]{2,1,0:T(8,128)(2,1)}, bf16[2,32,2048]{2,1,0:T(8,128)(2,1)S(1)}, u32[]{:S(2)}, u32[]{:S(2)}) %collective-permute-start.12) | collective-permute-done | bytes 262176 | tf_op jit(solution)/shard_map/ppermute | solution.py:97
  97.3 18.7 %collective-permute-done.18 = bf16[2,64,1024]{2,1,0:T(8,128)(2,1)S(1)} collective-permute-done((bf16[2,64,1024]{2,1,0:T(8,128)(2,1)S(1)}, bf16[2,64,1024]{2,1,0:T(8,128)(2,1)S(1)}, u32[]{:S(2)}, u32[]{:S(2)}) %collective-permute-start.18) | collective-permute-done | bytes 262176 | tf_op jit(solution)/shard_map/ppermute | solution.py:97
  138.2 16.4 %collective-permute-done.30 = bf16[2,32,1024]{2,1,0:T(8,128)(2,1)S(1)} collective-permute-done((bf16[2,32,1024]{2,1,0:T(8,128)(2,1)S(1)}, bf16[2,32,1024]{2,1,0:T(8,128)(2,1)S(1)}, u32[]{:S(2)}, u32[]{:S(2)}) %collective-permute-start.30) | collective-permute-done | bytes 131104 | tf_op jit(solution)/shard_map/ppermute | solution.py:97
  155.7 10.0 %collective-permute-done.36 = bf16[2,32,4096]{2,1,0:T(8,128)(2,1)S(1)} collective-permute-done((bf16[2,32,4096]{2,1,0:T(8,128)(2,1)S(1)}, bf16[2,32,4096]{2,1,0:T(8,128)(2,1)S(1)}, u32[]{:S(2)}, u32[]{:S(2)}) %collective-permute-start.36) | collective-permute-done | bytes 524320 | tf_op jit(solution)/shard_map/ppermute | solution.py:97
  175.1 11.8 %collective-permute-done.25 = bf16[4,32,3072]{2,1,0:T(8,128)(2,1)S(1)} collective-permute-done((bf16[4,32,3072]{2,1,0:T(8,128)(2,1)S(1)}, bf16[4,32,3072]{2,1,0:T(8,128)(2,1)S(1)}, u32[]{:S(2)}, u32[]{:S(2)}) %collective-permute-start.25) | collective-permute-done | bytes 786464 | tf_op jit(solution)/shard_map/ppermute | solution.py:97
  188.4 9.7 collective-permute-done.32.refs_1_
  212.7 12.1 %collective-permute-done.8.refs_1_ = bf16[8,32,2432]{2,1,0:T(8,128)(2,1)S(1)} collective-permute-done((bf16[8,32,2432]{2,1,0:T(8,128)(2,1)S(1)}, bf16[8,32,2432]{2,1,0:T(8,128)(2,1)S(1)}, u32[]{:S(2)}, u32[]{:S(2)}) %collective-permute-start.8) | collective-permute-done | bytes 1245216 | tf_op jit(solution)/shard_map/ppermute | solution.py:97
  227.0 19.4 %collective-permute-done.20.refs_1_ = bf16[8,64,1024]{2,1,0:T(8,128)(2,1)S(1)} collective-permute-done((bf16[8,64,1024]{2,1,0:T(8,128)(2,1)S(1)}, bf16[8,64,1024]{2,1,0:T(8,128)(2,1)S(1)}, u32[]{:S(2)}, u32[]{:S(2)}) %collective-permute-start.20) | collective-permute-done | bytes 1048608 | tf_op jit(solution)/shard_map/ppermute | solution.py:97
  308.6 8.0 multiply_reduce_fusion.10
  365.0 11.7 %collective-permute-done.44.refs_1_ = bf16[8,32,4096]{2,1,0:T(8,128)(2,1)} collective-permute-done((bf16[8,32,4096]{2,1,0:T(8,128)(2,1)}, bf16[8,32,4096]{2,1,0:T(8,128)(2,1)}, u32[]{:S(2)}, u32[]{:S(2)}) %collective-permute-start.44) | collective-permute-done | bytes 2097184 | tf_op jit(solution)/shard_map/ppermute | solution.py:97
  412.7 12.5 %fusion.7 = (bf16[416,4096]{1,0:T(8,128)(2,1)}, bf16[416,4096]{1,0:T(8,128)(2,1)}, bf16[416,4096]{1,0:T(8,128)(2,1)}) fusion(f32[416,4096]{1,0:T(8,128)} %fusion.221, f32[4096,416]{0,1:T(8,128)} %fusion.222, bf16[416,1024]{1,0:T(8,128)(2,1)} %copy-done.62, bf16[1024,4096]{1,0:T(8,128)(2,1)S(1)} %bitcast.408), kind=kOutput, calls=%fused_computation.16 | convolution fusion | flops 3516923904 | bytes 33095680 | tf_op jit(solution)/shard_map/dot_general | solution.py:22
  523.2 11.4 %multiply_convert_fusion.1 = bf16[2,16,208,208]{2,3,1,0:T(8,128)(2,1)S(1)} fusion(f32[2,16,208,208]{2,3,1,0:T(8,128)} %fusion.90, f32[2,16,208]{2,1,0:T(8,128)} %log_add_fusion, pred[2,208,208]{1,2,0:T(8,128)(4,1)S(1)} %compare_and_fusion, bf16[2,208,16,64]{1,3,2,0:T(8,128)(2,1)} %copy.205, bf16[2,208,16,64]{1,3,2,0:T(8,128)(2,1)} %copy.206), kind=kOutput, calls=%fused_computation.20 | convolution fusion | flops 371038912 | bytes 10123776 | tf_op jit(solution)/shard_map/sub | solution.py:471
  566.6 18.3 %collective-permute-done.59 = bf16[2,2,2,32,4096]{4,3,1,0,2:T(8,128)(2,1)} collective-permute-done((bf16[2,2,2,32,4096]{4,3,1,0,2:T(8,128)(2,1)}, bf16[2,2,2,32,4096]{4,3,1,0,2:T(8,128)(2,1)}, u32[]{:S(2)}, u32[]{:S(2)}) %collective-permute-start.59) | collective-permute-done | bytes 2097184 | tf_op jit(solution)/shard_map/ppermute | solution.py:97
  600.4 8.7 fusion.53
  644.8 9.5 collective-permute-done.60
  701.1 24.0 %collective-permute-done.79 = bf16[2,2,2,32,2048]{4,3,1,0,2:T(8,128)(2,1)S(1)} collective-permute-done((bf16[2,2,2,32,2048]{4,3,1,0,2:T(8,128)(2,1)S(1)}, bf16[2,2,2,32,2048]{4,3,1,0,2:T(8,128)(2,1)S(1)}, u32[]{:S(2)}, u32[]{:S(2)}) %collective-permute-start.79) | collective-permute-done | bytes 1048608 | tf_op jit(solution)/shard_map/ppermute | solution.py:97
  728.6 11.4 %collective-permute-done.67 = bf16[2,2,2,32,1024]{4,3,1,0,2:T(8,128)(2,1)S(1)} collective-permute-done((bf16[2,2,2,32,1024]{4,3,1,0,2:T(8,128)(2,1)S(1)}, bf16[2,2,2,32,1024]{4,3,1,0,2:T(8,128)(2,1)S(1)}, u32[]{:S(2)}, u32[]{:S(2)}) %collective-permute-start.67) | collective-permute-done | bytes 524320 | tf_op jit(solution)/shard_map/ppermute | solution.py:97
  740.0 12.8 %fusion.4 = (f32[2,32,208]{2,1,0:T(8,128)S(1)}, f32[2,32,208]{2,1,0:T(8,128)S(1)}, f32[2,32,208]{2,1,0:T(8,128)S(1)}, bf16[2,208,208]{2,1,0:T(8,128)(2,1)}) fusion(f32[2,32,208,208]{3,2,1,0:T(8,128)S(1)} %fusion.224, f32[2,32,208]{2,1,0:T(8,128)S(1)} %copy-done.122, f32[2,32,208]{2,1,0:T(8,128)S(1)} %copy-done.100, f32[2,208,208]{2,1,0:T(8,128)S(1)} %copy-done.79, ...), kind=kLoop, calls=%fused_computation.13 | loop fusion | flops 41406976 | bytes 11947520 | tf_op jit(solution)/shard_map/transpose(jvp())/reduce_sum | solution.py:57
  788.5 13.9 %collective-permute-done.72 = bf16[2,2,2,64,1024]{4,3,1,0,2:T(8,128)(2,1)S(1)} collective-permute-done((bf16[2,2,2,64,1024]{4,3,1,0,2:T(8,128)(2,1)S(1)}, bf16[2,2,2,64,1024]{4,3,1,0,2:T(8,128)(2,1)S(1)}, u32[]{:S(2)}, u32[]{:S(2)}) %collective-permute-start.72) | collective-permute-done | bytes 1048608 | tf_op jit(solution)/shard_map/ppermute | solution.py:97
  821.2 40.8 %all-reduce.19 = (f32[5]{0:T(128)S(1)}, f32[4,2304]{1,0:T(4,128)}, f32[2304]{0:T(1024)S(1)}, f32[32]{0:T(128)}, f32[32]{0:T(128)}, /*index=5*/f32[32]{0:T(128)},...) all-reduce(f32[5]{0:T(128)S(1)} %copy-done.209, ...), channel_id=1, replica_groups=mesh['dp'=8,'fsdp'=4] {'dp','fsdp'}, use_global_device_ids=true, to_apply=%region_25.26 | all-reduce | flops 15717 | bytes 125736 | tf_op jit(solution)/shard_map/psum | solution.py:568
  889.2 13.1 %collective-permute-done.93 = bf16[2,32,1024]{2,1,0:T(8,128)(2,1)S(1)} collective-permute-done((bf16[2,32,1024]{2,1,0:T(8,128)(2,1)S(1)}, bf16[2,32,1024]{2,1,0:T(8,128)(2,1)S(1)}, u32[]{:S(2)}, u32[]{:S(2)}) %collective-permute-start.93) | collective-permute-done | bytes 131104 | tf_op jit(solution)/shard_map/ppermute | solution.py:97
  918.2 22.6 %collective-permute-done.84 = bf16[2,2,2,32,2432]{4,3,1,0,2:T(8,128)(2,1)S(1)} collective-permute-done((bf16[2,2,2,32,2432]{4,3,1,0,2:T(8,128)(2,1)S(1)}, bf16[2,2,2,32,2432]{4,3,1,0,2:T(8,128)(2,1)S(1)}, u32[]{:S(2)}, u32[]{:S(2)}) %collective-permute-start.84) | collective-permute-done | bytes 1245216 | tf_op jit(solution)/shard_map/ppermute | solution.py:97
  942.4 11.2 %collective-permute-done.85 = bf16[2,2,32,2432]{3,2,1,0:T(8,128)(2,1)S(1)} collective-permute-done((bf16[2,2,32,2432]{3,2,1,0:T(8,128)(2,1)S(1)}, bf16[2,2,32,2432]{3,2,1,0:T(8,128)(2,1)S(1)}, u32[]{:S(2)}, u32[]{:S(2)}) %collective-permute-start.85) | collective-permute-done | bytes 622624 | tf_op jit(solution)/shard_map/ppermute | solution.py:97
  957.3 9.7 collective-permute-done.86
  (974 shorter events, 619.0 us)
Async XLA Ops:
  10.1 48.3 %collective-permute-start.5 = (bf16[1,32,2432]{2,1,0:T(8,128)(2,1)}, bf16[1,32,2432]{2,1,0:T(8,128)(2,1)}, u32[]{:S(2)}, u32[]{:S(2)}) collective-permute-start(bf16[1,32,2432]{2,1,0:T(8,128)(2,1)} %fusion.152), channel_id=1, source_target_pairs={{0,8},{4,12},{8,0},{12,4},{16,24},{20,28},{24,16},{28,20},{1,9},{5... | collective-permute-start | bytes 466952 | tf_op jit(solution)/shard_map/ppermute | solution.py:97
  86.9 47.1 %collective-permute-start.7 = (bf16[4,32,2432]{2,1,0:T(8,128)(2,1)S(1)}, bf16[4,32,2432]{2,1,0:T(8,128)(2,1)S(1)}, u32[]{:S(2)}, u32[]{:S(2)}) collective-permute-start(bf16[4,32,2432]{2,1,0:T(8,128)(2,1)S(1)} %pad_maximum_fusion.7), channel_id=1, source_target_pairs={{0,1},{1,0},{2,3},{3,2},{4,5},{5,4},{6,7},{7,6},{8,9},{9,8},{10,11... | collective-permute-start | bytes 1867784 | tf_op jit(solution)/shard_map/ppermute | solution.py:97
  116.0 50.5 %collective-permute-start.19 = (bf16[4,64,1024]{2,1,0:T(8,128)(2,1)S(1)}, bf16[4,64,1024]{2,1,0:T(8,128)(2,1)S(1)}, u32[]{:S(2)}, u32[]{:S(2)}) collective-permute-start(bf16[4,64,1024]{2,1,0:T(8,128)(2,1)S(1)} %pad_maximum_fusion.9), channel_id=1, source_target_pairs={{0,1},{1,0},{2,3},{3,2},{4,5},{5,4},{6,7},{7,6},{8,9},{9,8},{10,11... | collective-permute-start | bytes 1572872 | tf_op jit(solution)/shard_map/ppermute | solution.py:97
  118.2 81.9 %collective-permute-start.14 = (bf16[8,32,2048]{2,1,0:T(8,128)(2,1)S(1)}, bf16[8,32,2048]{2,1,0:T(8,128)(2,1)S(1)}, u32[]{:S(2)}, u32[]{:S(2)}) collective-permute-start(bf16[8,32,2048]{2,1,0:T(8,128)(2,1)S(1)} %pad_maximum_fusion.2.refs_0_), channel_id=1, source_target_pairs={{0,1},{1,0},{2,3},{3,2},{4,5},{5,4},{6,7},{7,6},{8,9},{9,8},{10,11... | collective-permute-start | bytes 3145736 | tf_op jit(solution)/shard_map/ppermute | solution.py:97
  133.8 68.5 %collective-permute-start.15 = (bf16[8,32,2048]{2,1,0:T(8,128)(2,1)S(1)}, bf16[8,32,2048]{2,1,0:T(8,128)(2,1)S(1)}, u32[]{:S(2)}, u32[]{:S(2)}) collective-permute-start(bf16[8,32,2048]{2,1,0:T(8,128)(2,1)S(1)} %pad_maximum_fusion.2.refs_0_), channel_id=1, source_target_pairs={{0,4},{4,0},{8,12},{12,8},{16,20},{20,16},{24,28},{28,24},{1,5},{5... | collective-permute-start | bytes 3145736 | tf_op jit(solution)/shard_map/ppermute | solution.py:97
  260.5 71.5 %collective-permute-start.27 = (bf16[8,32,3072]{2,1,0:T(8,128)(2,1)}, bf16[8,32,3072]{2,1,0:T(8,128)(2,1)}, u32[]{:S(2)}, u32[]{:S(2)}) collective-permute-start(bf16[8,32,3072]{2,1,0:T(8,128)(2,1)} %constant_dynamic-update-slice_fusion.4.refs_0_), channel_id=1, source_target_pairs={{0,4},{4,0},{8,12},{12,8},{16,20},{20,16},{24,28},{28,24},{1,5},{5... | collective-permute-start | bytes 4718600 | tf_op jit(solution)/shard_map/ppermute | solution.py:97
  260.6 65.3 %collective-permute-start.43 = (bf16[4,32,4096]{2,1,0:T(8,128)(2,1)}, bf16[4,32,4096]{2,1,0:T(8,128)(2,1)}, u32[]{:S(2)}, u32[]{:S(2)}) collective-permute-start(bf16[4,32,4096]{2,1,0:T(8,128)(2,1)} %pad_maximum_fusion.4), channel_id=1, source_target_pairs={{0,2},{1,3},{2,0},{3,1},{4,6},{5,7},{6,4},{7,5},{8,10},{9,11},{10,... | collective-permute-start | bytes 3145736 | tf_op jit(solution)/shard_map/ppermute | solution.py:97
  269.9 94.9 %collective-permute-start.38 = (bf16[8,32,4096]{2,1,0:T(8,128)(2,1)}, bf16[8,32,4096]{2,1,0:T(8,128)(2,1)}, u32[]{:S(2)}, u32[]{:S(2)}) collective-permute-start(bf16[8,32,4096]{2,1,0:T(8,128)(2,1)} %constant_dynamic-update-slice_fusion.12.refs_0_), channel_id=1, source_target_pairs={{0,2},{1,3},{2,0},{3,1},{4,6},{5,7},{6,4},{7,5},{8,10},{9,11},{10,... | collective-permute-start | bytes 6291464 | tf_op jit(solution)/shard_map/ppermute | solution.py:97
  270.4 58.4 %collective-permute-start.49 = (bf16[4,128,1024]{2,1,0:T(8,128)(2,1)}, bf16[4,128,1024]{2,1,0:T(8,128)(2,1)}, u32[]{:S(2)}, u32[]{:S(2)}) collective-permute-start(bf16[4,128,1024]{2,1,0:T(8,128)(2,1)} %pad_maximum_fusion.5), channel_id=1, source_target_pairs={{0,1},{1,0},{2,3},{3,2},{4,5},{5,4},{6,7},{7,6},{8,9},{9,8},{10,11... | collective-permute-start | bytes 3145736 | tf_op jit(solution)/shard_map/ppermute | solution.py:97
  271.5 60.6 %collective-permute-start.28 = (bf16[8,32,3072]{2,1,0:T(8,128)(2,1)}, bf16[8,32,3072]{2,1,0:T(8,128)(2,1)}, u32[]{:S(2)}, u32[]{:S(2)}) collective-permute-start(bf16[8,32,3072]{2,1,0:T(8,128)(2,1)} %collective-permute-done.26.refs_1_), channel_id=1, source_target_pairs={{0,4},{4,0},{8,12},{12,8},{16,20},{20,16},{24,28},{28,24},{1,5},{5... | collective-permute-start | bytes 4718600 | tf_op jit(solution)/shard_map/ppermute | solution.py:97
  325.9 61.6 %collective-permute-start.39 = (bf16[8,32,4096]{2,1,0:T(8,128)(2,1)}, bf16[8,32,4096]{2,1,0:T(8,128)(2,1)}, u32[]{:S(2)}, u32[]{:S(2)}) collective-permute-start(bf16[8,32,4096]{2,1,0:T(8,128)(2,1)} %constant_dynamic-update-slice_fusion.12.refs_0_), channel_id=1, source_target_pairs={{0,4},{4,0},{8,12},{12,8},{16,20},{20,16},{24,28},{28,24},{1,5},{5... | collective-permute-start | bytes 6291464 | tf_op jit(solution)/shard_map/ppermute | solution.py:97
  328.8 47.9 %collective-permute-start.44 = (bf16[8,32,4096]{2,1,0:T(8,128)(2,1)}, bf16[8,32,4096]{2,1,0:T(8,128)(2,1)}, u32[]{:S(2)}, u32[]{:S(2)}) collective-permute-start(bf16[8,32,4096]{2,1,0:T(8,128)(2,1)} %constant_dynamic-update-slice_fusion.16.refs_0_), channel_id=1, source_target_pairs={{0,1},{1,0},{2,3},{3,2},{4,5},{5,4},{6,7},{7,6},{8,9},{9,8},{10,11... | collective-permute-start | bytes 6291464 | tf_op jit(solution)/shard_map/ppermute | solution.py:97
  332.0 63.0 %collective-permute-start.45 = (bf16[8,32,4096]{2,1,0:T(8,128)(2,1)}, bf16[8,32,4096]{2,1,0:T(8,128)(2,1)}, u32[]{:S(2)}, u32[]{:S(2)}) collective-permute-start(bf16[8,32,4096]{2,1,0:T(8,128)(2,1)} %constant_dynamic-update-slice_fusion.16.refs_0_), channel_id=1, source_target_pairs={{0,4},{4,0},{8,12},{12,8},{16,20},{20,16},{24,28},{28,24},{1,5},{5... | collective-permute-start | bytes 6291464 | tf_op jit(solution)/shard_map/ppermute | solution.py:97
  332.0 56.1 %collective-permute-start.50 = (bf16[8,128,1024]{2,1,0:T(8,128)(2,1)}, bf16[8,128,1024]{2,1,0:T(8,128)(2,1)}, u32[]{:S(2)}, u32[]{:S(2)}) collective-permute-start(bf16[8,128,1024]{2,1,0:T(8,128)(2,1)} %constant_dynamic-update-slice_fusion.20.refs_0_), channel_id=1, source_target_pairs={{0,2},{1,3},{2,0},{3,1},{4,6},{5,7},{6,4},{7,5},{8,10},{9,11},{10,... | collective-permute-start | bytes 6291464 | tf_op jit(solution)/shard_map/ppermute | solution.py:97
  491.9 48.8 %collective-permute-start.56 = (bf16[2,2,2,128,1024]{4,3,1,0,2:T(8,128)(2,1)}, bf16[2,2,2,128,1024]{4,3,1,0,2:T(8,128)(2,1)}, u32[]{:S(2)}, u32[]{:S(2)}) collective-permute-start(bf16[2,2,2,128,1024]{4,3,1,0,2:T(8,128)(2,1)} %bitcast.398), channel_id=1, source_target_pairs={{0,2},{1,3},{2,0},{3,1},{4,6},{5,7},{6,4},{7,5},{8,10},{9,11},{10,... | collective-permute-start | bytes 6291464 | tf_op jit(solution)/shard_map/ppermute | solution.py:97
  506.4 60.2 %collective-permute-start.58 = (bf16[2,2,2,32,4096]{4,3,1,0,2:T(8,128)(2,1)}, bf16[2,2,2,32,4096]{4,3,1,0,2:T(8,128)(2,1)}, u32[]{:S(2)}, u32[]{:S(2)}) collective-permute-start(bf16[2,2,2,32,4096]{4,3,1,0,2:T(8,128)(2,1)} %bitcast.397), channel_id=1, source_target_pairs={{0,1},{1,0},{2,3},{3,2},{4,5},{5,4},{6,7},{7,6},{8,9},{9,8},{10,11... | collective-permute-start | bytes 6291464 | tf_op jit(solution)/shard_map/ppermute | solution.py:97
  517.0 67.8 %collective-permute-start.59 = (bf16[2,2,2,32,4096]{4,3,1,0,2:T(8,128)(2,1)}, bf16[2,2,2,32,4096]{4,3,1,0,2:T(8,128)(2,1)}, u32[]{:S(2)}, u32[]{:S(2)}) collective-permute-start(bf16[2,2,2,32,4096]{4,3,1,0,2:T(8,128)(2,1)} %bitcast.396), channel_id=1, source_target_pairs={{0,2},{1,3},{2,0},{3,1},{4,6},{5,7},{6,4},{7,5},{8,10},{9,11},{10,... | collective-permute-start | bytes 6291464 | tf_op jit(solution)/shard_map/ppermute | solution.py:97
  519.2 125.5 %collective-permute-start.63 = (bf16[512,1024]{1,0:T(8,128)(2,1)}, bf16[512,1024]{1,0:T(8,128)(2,1)}, u32[]{:S(2)}, u32[]{:S(2)}) collective-permute-start(bf16[512,1024]{1,0:T(8,128)(2,1)} %convolution_convert_fusion.8), channel_id=1, source_target_pairs={{0,4},{4,0},{8,12},{12,8},{16,20},{20,16},{24,28},{28,24},{1,5},{5... | collective-permute-start | bytes 3145736 | tf_op jit(solution)/shard_map/ppermute | solution.py:97
  562.0 92.3 %collective-permute-start.64 = (bf16[512,3072]{1,0:T(8,128)(2,1)}, bf16[512,3072]{1,0:T(8,128)(2,1)}, u32[]{:S(2)}, u32[]{:S(2)}) collective-permute-start(bf16[512,3072]{1,0:T(8,128)(2,1)} %convolution_convert_fusion.3), channel_id=1, source_target_pairs={{0,4},{4,0},{8,12},{12,8},{16,20},{20,16},{24,28},{28,24},{1,5},{5... | collective-permute-start | bytes 9437192 | tf_op jit(solution)/shard_map/ppermute | solution.py:97
  594.1 60.2 %collective-permute-start.61 = (bf16[2,2,32,4096]{3,2,1,0:T(8,128)(2,1)}, bf16[2,2,32,4096]{3,2,1,0:T(8,128)(2,1)}, u32[]{:S(2)}, u32[]{:S(2)}) collective-permute-start(bf16[2,2,32,4096]{3,2,1,0:T(8,128)(2,1)} %dynamic-slice_bitcast_fusion.1), channel_id=1, source_target_pairs={{0,2},{1,3},{2,0},{3,1},{4,6},{5,7},{6,4},{7,5},{8,10},{9,11},{10,... | collective-permute-start | bytes 3145736 | tf_op jit(solution)/shard_map/ppermute | solution.py:97
  598.7 55.6 %collective-permute-start.62 = (bf16[2,2,32,4096]{3,2,1,0:T(8,128)(2,1)}, bf16[2,2,32,4096]{3,2,1,0:T(8,128)(2,1)}, u32[]{:S(2)}, u32[]{:S(2)}) collective-permute-start(bf16[2,2,32,4096]{3,2,1,0:T(8,128)(2,1)} %dynamic-slice_bitcast_fusion), channel_id=1, source_target_pairs={{0,1},{1,0},{2,3},{3,2},{4,5},{5,4},{6,7},{7,6},{8,9},{9,8},{10,11... | collective-permute-start | bytes 3145736 | tf_op jit(solution)/shard_map/ppermute | solution.py:97
  644.7 82.7 %collective-permute-start.69 = (bf16[1024,1024]{1,0:T(8,128)(2,1)}, bf16[1024,1024]{1,0:T(8,128)(2,1)}, u32[]{:S(2)}, u32[]{:S(2)}) collective-permute-start(bf16[1024,1024]{1,0:T(8,128)(2,1)} %convolution_convert_fusion.7), channel_id=1, source_target_pairs={{0,4},{4,0},{8,12},{12,8},{16,20},{20,16},{24,28},{28,24},{1,5},{5... | collective-permute-start | bytes 6291464 | tf_op jit(solution)/shard_map/ppermute | solution.py:97
  656.9 71.7 %collective-permute-start.65 = (bf16[2,32,4096]{2,1,0:T(8,128)(2,1)}, bf16[2,32,4096]{2,1,0:T(8,128)(2,1)}, u32[]{:S(2)}, u32[]{:S(2)}) collective-permute-start(bf16[2,32,4096]{2,1,0:T(8,128)(2,1)} %dynamic-slice_bitcast_fusion.8), channel_id=1, source_target_pairs={{0,16},{4,20},{8,24},{12,28},{16,0},{20,4},{24,8},{28,12},{1,17},{... | collective-permute-start | bytes 1572872 | tf_op jit(solution)/shard_map/ppermute | solution.py:97
  665.7 74.3 %collective-permute-start.68 = (bf16[2,2,2,32,3072]{4,3,1,0,2:T(8,128)(2,1)}, bf16[2,2,2,32,3072]{4,3,1,0,2:T(8,128)(2,1)}, u32[]{:S(2)}, u32[]{:S(2)}) collective-permute-start(bf16[2,2,2,32,3072]{4,3,1,0,2:T(8,128)(2,1)} %bitcast.399), channel_id=1, source_target_pairs={{0,1},{1,0},{2,3},{3,2},{4,5},{5,4},{6,7},{7,6},{8,9},{9,8},{10,11... | collective-permute-start | bytes 4718600 | tf_op jit(solution)/shard_map/ppermute | solution.py:97
  (302 other events, 5111.9 us)

commit v2 on v1

v2 whole, which is shorter than its diff:
```python
from functools import partial

import jax
import jax.numpy as jnp
from jax import lax
from jax.experimental import pallas as pl
from jax.experimental.pallas import tpu as pltpu
from jax.sharding import PartitionSpec as P

DI = 2048
NS = 128
PM = 64
HD = 64
HM = 32


EPS = 1e-05


def matmul(former, latter):
    return jnp.dot(former, latter, preferred_element_type=jnp.float32)


def matmul_left(former, latter):
    return lax.dot_general(
        former, latter, (((0,), (0,)), ((), ())), preferred_element_type=jnp.float32
    )


def matmul_right(former, latter):
    return lax.dot_general(
        former, latter, (((1,), (1,)), ((), ())), preferred_element_type=jnp.float32
    )


def rms_norm(values, scaling):
    return values * lax.rsqrt(jnp.mean(values * values, axis=-1, keepdims=True) + EPS) * scaling


VMEM_LIMIT = 48 * 1024 * 1024
BRIEF = pl.CostEstimate(flops=1024, transcendentals=0, bytes_accessed=1024)


def column_sum(v):
    return jnp.sum(v, axis=0, keepdims=True)


def sigmoid(v):
    return 1.0 / (1.0 + jnp.exp(-v))


def down_rows(v, count):
    return pltpu.roll(v, count, 0)


def up_rows(v, count):
    return pltpu.roll(v, v.shape[0] - count, 0)


def turned(v):
    length = v.shape[0]
    row = lax.broadcasted_iota(jnp.int32, (length, length), 0)
    column = lax.broadcasted_iota(jnp.int32, (length, length), 1)
    unit = (row == column).astype(jnp.float32)
    return lax.dot_general(
        v,
        unit,
        (((0,), (0,)), ((), ())),
        precision=lax.Precision.HIGHEST,
        preferred_element_type=jnp.float32,
    )


def turned_back(v):
    length = v.shape[1]
    row = lax.broadcasted_iota(jnp.int32, (length, length), 0)
    column = lax.broadcasted_iota(jnp.int32, (length, length), 1)
    unit = (row == column).astype(jnp.float32)
    return lax.dot_general(
        unit,
        v,
        (((1,), (1,)), ((), ())),
        precision=lax.Precision.HIGHEST,
        preferred_element_type=jnp.float32,
    )


def allowed_mask(ids_column, ids_row):
    length = ids_column.shape[0]
    row = lax.broadcasted_iota(jnp.int32, (length, length), 0)
    column = lax.broadcasted_iota(jnp.int32, (length, length), 1)
    return (ids_column == ids_row) & (row >= column)


def link_columns(ids_column, taps):
    length = ids_column.shape[0]
    place = lax.broadcasted_iota(jnp.int32, (length, 128), 0)
    wide = jnp.broadcast_to(ids_column, (length, 128))
    return [
        ((down_rows(wide, j) == wide) & (place >= j)).astype(jnp.float32)[:, :1]
        for j in range(1, taps)
    ]


def conv_chunk(raw, taps_chunk, offset, links):
    taps = taps_chunk.shape[0]
    shifted = [raw] + [down_rows(raw, j) * links[j - 1] for j in range(1, taps)]
    total = offset
    for j in range(taps):
        total = total + shifted[j] * taps_chunk[taps - 1 - j : taps - j]
    return total, shifted


def step_terms(step_raw, step_bias, decay_log):
    shifted = step_raw + step_bias
    step = jnp.maximum(shifted, 0.0) + jnp.log1p(jnp.exp(-jnp.abs(shifted)))
    rate = -jnp.exp(decay_log) * step
    length = step.shape[0]
    place = lax.broadcasted_iota(jnp.int32, step.shape, 0)
    total = rate
    shift = 1
    while shift < length:
        total = total + jnp.where(place >= shift, down_rows(total, shift), 0.0)
        shift *= 2
    return shifted, step, rate, total


def mixer_forward_kernel(
    raw_ref, zgate_ref, ids_column_ref, ids_row_ref, taps_ref, offset_ref,
    bias_ref, decay_ref, skip_ref, gain_ref,
    values_ref, states_ref, combined_ref, gate_ref,
):
    taps = taps_ref.shape[0]
    ids_column = ids_column_ref[0]
    links = link_columns(ids_column, taps)
    channels = taps_ref.shape[1]
    for start in range(0, channels, 256):
        part = slice(start, start + 256)
        total, _ = conv_chunk(raw_ref[0, :, part], taps_ref[:, part], offset_ref[:, part], links)
        low = (total * sigmoid(total)).astype(jnp.bfloat16)
        if start < DI:
            values_ref[0, :, part] = low
        else:
            states_ref[0] = low
    state_in, state_out = states_ref[0, :, :NS], states_ref[0, :, NS:]
    gram = matmul_right(state_out, state_in)
    _, step, _, total = step_terms(
        raw_ref[0, :, channels : channels + 128], bias_ref[...], decay_ref[...]
    )
    total_rows, step_rows = turned(total), turned(step)
    mask = allowed_mask(ids_column, ids_row_ref[0])
    gram = jnp.where(mask, gram, 0.0)
    length = gram.shape[0]
    first = lax.broadcasted_iota(jnp.int32, (length, 2 * PM), 1) < PM
    squares = jnp.zeros((length, 1), jnp.float32)
    for pair in range(HM // 2):
        lanes = slice(pair * 2 * PM, (pair + 1) * 2 * PM)
        values = values_ref[0, :, lanes]
        outs = []
        for head in (2 * pair, 2 * pair + 1):
            between = total[:, head : head + 1] - total_rows[head : head + 1, :]
            decayed = jnp.exp(jnp.where(mask, between, 0.0))
            mix = gram * decayed * step_rows[head : head + 1, :]
            outs.append(matmul(mix.astype(jnp.bfloat16), values))
        combined = jnp.where(first, outs[0], outs[1]) + skip_ref[:, lanes] * values.astype(
            jnp.float32
        )
        combined_ref[0, :, lanes] = combined
        zgate = zgate_ref[0, :, lanes]
        gated = combined * (zgate * sigmoid(zgate))
        squares = squares + jnp.sum(gated * gated, axis=1, keepdims=True)
    scale = lax.rsqrt(squares / DI + EPS)
    for start in range(0, DI, 256):
        part = slice(start, start + 256)
        zgate = zgate_ref[0, :, part]
        gated = combined_ref[0, :, part] * (zgate * sigmoid(zgate))
        gate_ref[0, :, part] = (gated * scale * gain_ref[:, part]).astype(jnp.bfloat16)


def gate_backward_kernel(
    grad_ref, zgate_ref, gain_ref, values_ref, combined_ref,
    zgrad_ref, heads_ref, gain_grad_ref, skip_grad_ref,
):
    @pl.when(pl.program_id(0) == 0)
    def _():
        for ref in (gain_grad_ref, skip_grad_ref):
            ref[...] = jnp.zeros(ref.shape, ref.dtype)

    length = grad_ref.shape[1]
    squares = jnp.zeros((length, 1), jnp.float32)
    product = jnp.zeros((length, 1), jnp.float32)
    for start in range(0, DI, 256):
        part = slice(start, start + 256)
        zgate = zgate_ref[0, :, part]
        gated = combined_ref[0, :, part] * (zgate * sigmoid(zgate))
        squares = squares + jnp.sum(gated * gated, axis=1, keepdims=True)
        product = product + jnp.sum(
            gated * grad_ref[0, :, part] * gain_ref[:, part], axis=1, keepdims=True
        )
    scale = lax.rsqrt(squares / DI + EPS)
    inner = scale * scale * scale * (product / DI)
    for start in range(0, DI, 256):
        part = slice(start, start + 256)
        zgate = zgate_ref[0, :, part]
        combined = combined_ref[0, :, part]
        sig = sigmoid(zgate)
        silu = zgate * sig
        gated = combined * silu
        grad = grad_ref[0, :, part]
        gain_grad_ref[:, part] += column_sum(grad * gated * scale)
        grad_gated = scale * grad * gain_ref[:, part] - gated * inner
        grad_combined = grad_gated * silu
        zgrad_ref[0, :, part] = (grad_gated * combined * (sig + silu * (1.0 - sig))).astype(
            jnp.bfloat16
        )
        skip_grad_ref[:, part] += column_sum(
            grad_combined * values_ref[0, :, part].astype(jnp.float32)
        )
        heads_ref[0, :, part] = grad_combined.astype(jnp.bfloat16)


def mixer_backward_kernel(
    heads_ref, raw_ref, ids_column_ref, ids_row_ref, taps_ref, offset_ref,
    bias_ref, decay_ref, skip_ref, values_ref, states_ref,
    xgrad_ref, taps_grad_ref, offset_grad_ref, bias_grad_ref, decay_grad_ref, through_ref,
):
    taps = taps_ref.shape[0]
    channels = taps_ref.shape[1]
    length = raw_ref.shape[1]

    @pl.when(pl.program_id(0) == 0)
    def _():
        for ref in (taps_grad_ref, offset_grad_ref, bias_grad_ref, decay_grad_ref):
            ref[...] = jnp.zeros(ref.shape, ref.dtype)

    ids_column = ids_column_ref[0]
    links = link_columns(ids_column, taps)
    state_in, state_out = states_ref[0, :, :NS], states_ref[0, :, NS:]
    shifted_step, step, rate, total = step_terms(
        raw_ref[0, :, channels : channels + 128], bias_ref[...], decay_ref[...]
    )
    total_rows, step_rows = turned(total), turned(step)
    mask = allowed_mask(ids_column, ids_row_ref[0])
    gram = jnp.where(mask, matmul_right(state_out, state_in), 0.0)
    first = lax.broadcasted_iota(jnp.int32, (length, 2 * PM), 1) < PM
    lane = lax.broadcasted_iota(jnp.int32, (length, 128), 1)
    row = lax.broadcasted_iota(jnp.int32, (128, length), 0)
    grad_gram = jnp.zeros((length, length), jnp.float32)
    by_row = jnp.zeros((length, 128), jnp.float32)
    by_column = jnp.zeros((128, length), jnp.float32)
    nothing = jnp.zeros((length, 2 * PM), jnp.bfloat16)
    for pair in range(HM // 2):
        lanes = slice(pair * 2 * PM, (pair + 1) * 2 * PM)
        values = values_ref[0, :, lanes]
        heads = heads_ref[0, :, lanes]
        outs = []
        for head, own in ((2 * pair, first), (2 * pair + 1, ~first)):
            between = total[:, head : head + 1] - total_rows[head : head + 1, :]
            decayed = jnp.where(mask, jnp.exp(jnp.where(mask, between, 0.0)), 0.0)
            step_row = step_rows[head : head + 1, :]
            mixed = gram * decayed
            grad_mix = matmul_right(jnp.where(own, heads, nothing), values)
            outs.append(matmul_left((mixed * step_row).astype(jnp.bfloat16), heads))
            grad_gram = grad_gram + grad_mix * decayed * step_row
            direct = grad_mix * mixed
            by_column = by_column + jnp.where(row == head, column_sum(direct), 0.0)
            by_row = by_row + jnp.where(
                lane == head, jnp.sum(direct * step_row, axis=1, keepdims=True), 0.0
            )
        through_ref[:, lanes] = jnp.where(first, outs[0], outs[1]) + skip_ref[
            :, lanes
        ] * heads.astype(jnp.float32)
    grad_step = turned_back(by_column)
    grad_total = by_row - grad_step * step
    place = lax.broadcasted_iota(jnp.int32, grad_total.shape, 0)
    shift = 1
    while shift < length:
        grad_total = grad_total + jnp.where(
            place < length - shift, up_rows(grad_total, shift), 0.0
        )
        shift *= 2
    decay_grad_ref[...] += column_sum(grad_total * rate)
    grad_step = grad_step - grad_total * jnp.exp(decay_ref[...])
    grad_raw = jnp.where(lane < HM, grad_step * sigmoid(shifted_step), 0.0)
    bias_grad_ref[...] += column_sum(grad_raw)
    xgrad_ref[0, :, channels : channels + 128] = grad_raw.astype(jnp.bfloat16)
    gram_low = grad_gram.astype(jnp.bfloat16)
    grad_in = matmul_left(gram_low, state_out)
    grad_out = matmul(gram_low, state_in)
    for start in range(0, channels, 128):
        part = slice(start, start + 128)
        chunk_taps = taps_ref[:, part]
        total, shifted = conv_chunk(raw_ref[0, :, part], chunk_taps, offset_ref[:, part], links)
        sig = sigmoid(total)
        if start < DI:
            grad = through_ref[:, part]
        else:
            grad = grad_in if start == DI else grad_out
        grad = grad * (sig + total * sig * (1.0 - sig))
        offset_grad_ref[:, part] += column_sum(grad)
        back = grad * chunk_taps[taps - 1 : taps]
        sums = [column_sum(grad * shifted[0])]
        for j in range(1, taps):
            sums.append(column_sum(grad * shifted[j]))
            linked = grad * links[j - 1]
            back = back + up_rows(linked, j) * chunk_taps[taps - 1 - j : taps - j]
        taps_grad_ref[:, part] += jnp.concatenate(sums[::-1], axis=0)
        xgrad_ref[0, :, part] = back.astype(jnp.bfloat16)


def whole(rows, columns):
    return pl.BlockSpec((rows, columns), lambda n: (0, 0))


def mixer_forward(raw, zgate, ids, taps, offset, bias, decay, skip, gain):
    count, length, columns = raw.shape
    row = lambda c: pl.BlockSpec((1, length, c), lambda n: (n, 0, 0))
    channels = taps.shape[1]
    return pl.pallas_call(
        mixer_forward_kernel,
        grid=(count,),
        in_specs=[
            row(columns), row(DI), row(1), pl.BlockSpec((1, 1, length), lambda n: (n, 0, 0)),
            whole(*taps.shape), whole(1, channels), whole(1, 128), whole(1, 128),
            whole(1, DI), whole(1, DI),
        ],
        out_specs=[row(DI), row(2 * NS), row(DI), row(DI)],
        out_shape=[
            jax.ShapeDtypeStruct((count, length, DI), jnp.bfloat16),
            jax.ShapeDtypeStruct((count, length, 2 * NS), jnp.bfloat16),
            jax.ShapeDtypeStruct((count, length, DI), jnp.float32),
            jax.ShapeDtypeStruct((count, length, DI), jnp.bfloat16),
        ],
        compiler_params=pltpu.CompilerParams(vmem_limit_bytes=VMEM_LIMIT),
        cost_estimate=BRIEF,
    )(raw, zgate, ids[:, :, None], ids[:, None, :], taps, offset, bias, decay, skip, gain)


def gate_backward(grad, zgate, gain, values, combined):
    count, length, _ = grad.shape
    row = lambda c: pl.BlockSpec((1, length, c), lambda n: (n, 0, 0))
    one = lambda r, c: jax.ShapeDtypeStruct((r, c), jnp.float32)
    return pl.pallas_call(
        gate_backward_kernel,
        grid=(count,),
        in_specs=[row(DI), row(DI), whole(1, DI), row(DI), row(DI)],
        out_specs=[row(DI), row(DI), whole(1, DI), whole(1, DI)],
        out_shape=[
            jax.ShapeDtypeStruct((count, length, DI), jnp.bfloat16),
            jax.ShapeDtypeStruct((count, length, DI), jnp.bfloat16),
            one(1, DI), one(1, DI),
        ],
        compiler_params=pltpu.CompilerParams(vmem_limit_bytes=VMEM_LIMIT),
        cost_estimate=BRIEF,
    )(grad, zgate, gain, values, combined)


def mixer_backward(heads, raw, ids, taps, offset, bias, decay, skip, values, states):
    count, length, columns = raw.shape
    row = lambda c: pl.BlockSpec((1, length, c), lambda n: (n, 0, 0))
    channels = taps.shape[1]
    one = lambda r, c: jax.ShapeDtypeStruct((r, c), jnp.float32)
    return pl.pallas_call(
        mixer_backward_kernel,
        grid=(count,),
        in_specs=[
            row(DI), row(columns), row(1),
            pl.BlockSpec((1, 1, length), lambda n: (n, 0, 0)),
            whole(*taps.shape), whole(1, channels), whole(1, 128), whole(1, 128),
            whole(1, DI), row(DI), row(2 * NS),
        ],
        out_specs=[
            row(columns), whole(*taps.shape), whole(1, channels), whole(1, 128), whole(1, 128),
        ],
        out_shape=[
            jax.ShapeDtypeStruct((count, length, columns), jnp.bfloat16),
            one(*taps.shape), one(1, channels), one(1, 128), one(1, 128),
        ],
        scratch_shapes=[pltpu.VMEM((length, DI), jnp.float32)],
        compiler_params=pltpu.CompilerParams(vmem_limit_bytes=VMEM_LIMIT),
        cost_estimate=BRIEF,
    )(heads, raw, ids[:, :, None], ids[:, None, :], taps, offset, bias, decay, skip, values, states)


def head_scores(query, key, own, mask, nothing):
    scores = matmul_right(jnp.where(own, query, nothing), key) * HD ** (-0.5)
    masked = jnp.where(mask, scores, -1e30)
    highest = jnp.max(masked, axis=1, keepdims=True)
    exponents = jnp.exp(masked - highest)
    return exponents / jnp.sum(exponents, axis=1, keepdims=True)


def attention_forward_kernel(joined_ref, ids_column_ref, ids_row_ref, out_ref):
    mask = allowed_mask(ids_column_ref[0], ids_row_ref[0])
    length, width = out_ref.shape[1:]
    first = lax.broadcasted_iota(jnp.int32, (length, 2 * HD), 1) < HD
    nothing = jnp.zeros((length, 2 * HD), jnp.bfloat16)
    for start in range(0, width, 2 * HD):
        query, key, value = (
            joined_ref[0, :, k * width + start : k * width + start + 2 * HD] for k in range(3)
        )
        outs = []
        for own in (first, ~first):
            chances = head_scores(query, key, own, mask, nothing)
            outs.append(matmul(chances.astype(jnp.bfloat16), value))
        out_ref[0, :, start : start + 2 * HD] = jnp.where(first, outs[0], outs[1]).astype(
            jnp.bfloat16
        )


def attention_backward_kernel(joined_ref, grad_ref, ids_column_ref, ids_row_ref, *rest):
    out_ref = rest[-1]
    mask = allowed_mask(ids_column_ref[0], ids_row_ref[0])
    length, width = grad_ref.shape[1:]
    first = lax.broadcasted_iota(jnp.int32, (length, 2 * HD), 1) < HD
    nothing = jnp.zeros((length, 2 * HD), jnp.bfloat16)
    scale = HD ** (-0.5)
    for start in range(0, width, 2 * HD):
        query, key, value = (
            joined_ref[0, :, k * width + start : k * width + start + 2 * HD] for k in range(3)
        )
        grad = grad_ref[0, :, start : start + 2 * HD]
        outs = [[], [], []]
        for own in (first, ~first):
            chances = head_scores(query, key, own, mask, nothing)
            grad_chances = matmul_right(jnp.where(own, grad, nothing), value)
            inner = jnp.sum(chances * grad_chances, axis=1, keepdims=True)
            grad_scores = (chances * (grad_chances - inner)).astype(jnp.bfloat16)
            outs[0].append(matmul(grad_scores, key) * scale)
            outs[1].append(matmul_left(grad_scores, query) * scale)
            outs[2].append(matmul_left(chances.astype(jnp.bfloat16), grad))
        for k in range(3):
            out_ref[0, :, k * width + start : k * width + start + 2 * HD] = jnp.where(
                first, outs[k][0], outs[k][1]
            ).astype(jnp.bfloat16)


def attention_forward(joined, ids):
    count, length, columns = joined.shape
    row = lambda c: pl.BlockSpec((1, length, c), lambda n: (n, 0, 0))
    return pl.pallas_call(
        attention_forward_kernel,
        grid=(count,),
        in_specs=[row(columns), row(1), pl.BlockSpec((1, 1, length), lambda n: (n, 0, 0))],
        out_specs=row(columns // 3),
        out_shape=jax.ShapeDtypeStruct((count, length, columns // 3), jnp.bfloat16),
        compiler_params=pltpu.CompilerParams(vmem_limit_bytes=VMEM_LIMIT),
        cost_estimate=BRIEF,
    )(joined, ids[:, :, None], ids[:, None, :])


def attention_backward(joined, grad, ids, waits):
    count, length, columns = joined.shape
    row = lambda c: pl.BlockSpec((1, length, c), lambda n: (n, 0, 0))
    return pl.pallas_call(
        attention_backward_kernel,
        grid=(count,),
        in_specs=[
            row(columns), row(columns // 3), row(1),
            pl.BlockSpec((1, 1, length), lambda n: (n, 0, 0)),
        ] + [pl.BlockSpec(memory_space=pl.ANY)] * len(waits),
        out_specs=row(columns),
        out_shape=jax.ShapeDtypeStruct((count, length, columns), jnp.bfloat16),
        compiler_params=pltpu.CompilerParams(vmem_limit_bytes=VMEM_LIMIT),
        cost_estimate=BRIEF,
    )(joined, grad, ids[:, :, None], ids[:, None, :], *waits)


def ffn_kernel(
    rows, fold, source_ref, grad_ref, gate_ref, upper_ref, folded_ref,
    hidden_ref, gate_grad_ref, upper_grad_ref, out_ref, back_ref, down_ref,
):
    @pl.when(pl.program_id(0) == 0)
    def _():
        out_ref[...] = jnp.zeros(out_ref.shape, jnp.float32)
        back_ref[...] = jnp.zeros(back_ref.shape, jnp.float32)

    width = out_ref.shape[1]
    for d in range(folded_ref.shape[0] // rows):
        for q in range(fold):
            place = (d * fold + q) * rows
            down_ref[place : place + rows, :] = folded_ref[
                d * rows : (d + 1) * rows, q * width : (q + 1) * width
            ]
    source, grad = source_ref[...], grad_ref[...]
    gate_pre = matmul(source, gate_ref[...])
    up_pre = matmul(source, upper_ref[...])
    sig = sigmoid(gate_pre)
    silu = gate_pre * sig
    hidden = (silu * up_pre).astype(jnp.bfloat16)
    hidden_ref[...] = hidden
    out_ref[...] += matmul(hidden, down_ref[...])
    grad_hidden = matmul_right(grad, down_ref[...])
    gate_grad = (grad_hidden * up_pre * (sig + silu * (1.0 - sig))).astype(jnp.bfloat16)
    upper_grad = (grad_hidden * silu).astype(jnp.bfloat16)
    gate_grad_ref[...] = gate_grad
    upper_grad_ref[...] = upper_grad
    back_ref[...] += matmul_right(gate_grad, gate_ref[...]) + matmul_right(
        upper_grad, upper_ref[...]
    )


def feed_forward(source, grad, full, rows, hidden_width, fold):
    tokens, width = source.shape
    tile = 512
    steps = hidden_width // tile
    all_rows = lambda c: pl.BlockSpec((tokens, c), lambda j: (0, j))
    fixed = pl.BlockSpec((tokens, width), lambda j: (0, 0))
    down_block = 2 * hidden_width // (fold * width)
    return pl.pallas_call(
        partial(ffn_kernel, rows, fold),
        grid=(steps,),
        in_specs=[
            fixed,
            fixed,
            pl.BlockSpec((width, tile), lambda j: (0, j)),
            pl.BlockSpec((width, tile), lambda j: (0, steps + j)),
            pl.BlockSpec((tile // fold, fold * width), lambda j: (j, down_block)),
        ],
        out_specs=[all_rows(tile)] * 3 + [fixed] * 2,
        out_shape=[jax.ShapeDtypeStruct((tokens, hidden_width), jnp.bfloat16)] * 3
        + [jax.ShapeDtypeStruct((tokens, width), jnp.float32)] * 2,
        scratch_shapes=[pltpu.VMEM((tile, width), jnp.bfloat16)],
        compiler_params=pltpu.CompilerParams(vmem_limit_bytes=VMEM_LIMIT),
        cost_estimate=BRIEF,
    )(source, grad, full, full, full)


AXES = ("dp", "fsdp")


def axis_bits():
    bits = []
    for name in AXES:
        size = lax.axis_size(name)
        step = size // 2
        while step:
            bits.append((name, size, step))
            step //= 2
    return bits


def phases(flip):
    bits = axis_bits()
    outer = [k for k, b in enumerate(bits) if b[0] == "dp" and b[2] > 1]
    core = [k for k, b in enumerate(bits) if b[0] == "dp" and b[2] == 1]
    inner = [k for k, b in enumerate(bits) if b[0] == "fsdp"]
    return bits, outer + (inner if flip else inner[::-1]) + core


def swap(v, bit):
    name, size, step = bit
    return lax.ppermute(v, name, [(i, i ^ step) for i in range(size)])


def own_bit(bit):
    return (lax.axis_index(bit[0]) // bit[2]) % 2


def own_index():
    return lax.axis_index("dp") * lax.axis_size("fsdp") + lax.axis_index("fsdp")


def bit_weight(bit):
    return bit[2] * (lax.axis_size("fsdp") if bit[0] == "dp" else 1)


def assemble_kernel(offsets, me_ref, *refs):
    pieces, out_ref, sems = refs[:-2], refs[-2], refs[-1]
    me = me_ref[0]
    copies = []
    count = 0
    for piece, places in zip(pieces, offsets):
        for j, place in enumerate(places):
            copies.append(
                pltpu.make_async_copy(piece.at[j], out_ref.at[me ^ place], sems.at[count])
            )
            count += 1
    for c in copies:
        c.start()
    for c in copies:
        c.wait()


def tie(*values):
    return lax.optimization_barrier(values)


class Gather:
    def __init__(self, shard, flip):
        self.rows, self.columns = shard.shape
        self.bits, self.order = phases(flip)
        self.pieces = [(shard[None], [0])]
        self.phase = 0

    def step(self):
        k = self.order[self.phase]
        weight = bit_weight(self.bits[k])
        if len(self.pieces) > 1 and self.phase < len(self.order) - 1:
            joined = jnp.concatenate([p for p, _ in self.pieces], axis=0)
            self.pieces = [(joined, sum((o for _, o in self.pieces), []))]
        self.pieces = self.pieces + [
            (swap(p, self.bits[k]), [o ^ weight for o in offs]) for p, offs in self.pieces
        ]
        self.phase += 1

    def done(self):
        while self.phase < len(self.order):
            self.step()
        count = 2 ** len(self.bits)
        me = own_index().astype(jnp.int32).reshape(1)
        out = pl.pallas_call(
            partial(assemble_kernel, [o for _, o in self.pieces]),
            out_shape=jax.ShapeDtypeStruct((count, self.rows, self.columns), jnp.bfloat16),
            in_specs=[pl.BlockSpec(memory_space=pltpu.SMEM)]
            + [pl.BlockSpec(memory_space=pl.ANY)] * len(self.pieces),
            out_specs=pl.BlockSpec(memory_space=pltpu.VMEM),
            scratch_shapes=[pltpu.SemaphoreType.DMA((count,))],
            compiler_params=pltpu.CompilerParams(vmem_limit_bytes=24 * 1024 * 1024),
            cost_estimate=BRIEF,
        )(me, *[p for p, _ in self.pieces])
        return out.reshape(count * self.rows, self.columns)


def unfold_kernel(start, fold, full_ref, out_ref, sems):
    columns = out_ref.shape[3]
    copies = [
        pltpu.make_async_copy(
            full_ref.at[:, :, pl.ds(start + q * columns, columns)], out_ref.at[:, q], sems.at[q]
        )
        for q in range(fold)
    ]
    for c in copies:
        c.start()
    for c in copies:
        c.wait()


def unfold(full, rows, start, fold, columns):
    count = full.shape[0] // rows
    out = pl.pallas_call(
        partial(unfold_kernel, start, fold),
        out_shape=jax.ShapeDtypeStruct((count, fold, rows, columns), full.dtype),
        in_specs=[pl.BlockSpec(memory_space=pl.ANY)],
        out_specs=pl.BlockSpec(memory_space=pltpu.VMEM),
        scratch_shapes=[pltpu.SemaphoreType.DMA((fold,))],
        compiler_params=pltpu.CompilerParams(vmem_limit_bytes=24 * 1024 * 1024),
        cost_estimate=BRIEF,
    )(full.reshape(count, rows, full.shape[1]))
    return out.reshape(count * fold * rows, columns)


def gather_round(gathers, values=(), fresh=()):
    sizes = [len(g.pieces) for g in gathers]
    tied = tie(
        *values, *[g.pieces[0][0] for g in fresh], *[p for g in gathers for p, _ in g.pieces]
    )
    head = len(values)
    for g in fresh:
        g.pieces[0] = (tied[head], g.pieces[0][1])
        head += 1
    for g, size in zip(gathers, sizes):
        g.pieces = [(tied[head + k], g.pieces[k][1]) for k in range(size)]
        head += size
    for g in [*gathers, *fresh]:
        if g.phase < len(g.order):
            g.step()
    return tied[: len(values)]


def gather_small(shard):
    bits = axis_bits()
    out = shard[None]
    for bit in bits[::-1]:
        other = swap(out, bit)
        mine = own_bit(bit) == 0
        out = jnp.concatenate([jnp.where(mine, out, other), jnp.where(mine, other, out)], axis=0)
    return out


def scatter_sum(part, flip, core_done, wide=False):
    bits, order = phases(flip)
    names = [k for k in range(len(bits)) if not (core_done and bits[k][0] == "dp" and bits[k][2] == 1)]
    count = 2 ** len(names)
    part = part.reshape([2] * len(names) + [part.shape[0] // count, part.shape[1]])
    for n, k in enumerate([k for k in order[::-1] if k in names]):
        axis = names.index(k)
        names.remove(k)
        mine = own_bit(bits[k])
        send = lax.dynamic_index_in_dim(part, 1 - mine, axis, keepdims=False)
        keep = lax.dynamic_index_in_dim(part, mine, axis, keepdims=False)
        total = keep.astype(jnp.float32) + swap(send, bits[k]).astype(jnp.float32)
        part = total if not names else total.astype(part.dtype)
    return part.astype(jnp.float32)


def core_columns(former, core):
    outer = lax.axis_size("dp") // 2
    group = former.shape[1] // (2 * outer)
    return jnp.concatenate(
        [lax.dynamic_slice_in_dim(former, (2 * i + core) * group, group, 1) for i in range(outer)],
        axis=1,
    )


def grads_kernel(plan, rows, counts, core_ref, *refs):
    formers, latters = refs[: counts[0]], refs[counts[0] : counts[0] + counts[1]]
    products = {}
    for out_ref, items in zip(refs[counts[0] + counts[1] :], plan):
        start = 0
        for former, latter, fold, low, high in items:
            if (former, latter) not in products:
                products[former, latter] = matmul_left(
                    formers[former][...], latters[latter][...]
                ).astype(jnp.bfloat16)
            product = products[former, latter]
            if fold == 1:
                out_ref[:, start : start + high - low] = product[:, low:high]
            else:
                width = product.shape[1]
                for d in range(product.shape[0] // (fold * rows)):
                    for q in range(low // width, high // width):
                        to = start + q * width - low
                        place = (d * fold + q) * rows
                        out_ref[d * rows : (d + 1) * rows, to : to + width] = product[
                            place : place + rows, :
                        ]
            start += high - low


def part_grads(formers, latters, plan, rows, core):
    tokens = formers[0].shape[0]
    outer = lax.axis_size("dp") // 2
    groups = [f.shape[1] // (2 * outer) for f in formers]
    height = rows * lax.axis_size("fsdp")
    widths = [sum(item[4] - item[3] for item in items) for items in plan]
    shapes = [jax.ShapeDtypeStruct((outer * height, w), jnp.bfloat16) for w in widths]
    if any(g % 128 for g in groups):
        outs = []
        for items in plan:
            parts = []
            for former, latter, fold, low, high in items:
                product = matmul_left(core_columns(formers[former], core), latters[latter])
                width = product.shape[1]
                product = jnp.swapaxes(product.reshape(-1, fold, rows, width), 1, 2)
                parts.append(product.reshape(-1, fold * width)[:, low:high])
            outs.append(jnp.concatenate(parts, axis=1).astype(jnp.bfloat16))
        return outs
    return pl.pallas_call(
        partial(grads_kernel, plan, rows, (len(formers), len(latters))),
        grid_spec=pltpu.PrefetchScalarGridSpec(
            num_scalar_prefetch=1,
            grid=(outer,),
            in_specs=[pl.BlockSpec((tokens, g), lambda i, c: (0, 2 * i + c[0])) for g in groups]
            + [pl.BlockSpec(v.shape, lambda i, c: (0, 0)) for v in latters],
            out_specs=[pl.BlockSpec((height, w), lambda i, c: (i, 0)) for w in widths],
        ),
        out_shape=shapes,
        compiler_params=pltpu.CompilerParams(vmem_limit_bytes=VMEM_LIMIT),
        cost_estimate=BRIEF,
    )(core.astype(jnp.int32).reshape(1), *formers, *latters)


class Scatter:
    def __init__(self, send, keep, flip):
        self.bits, order = phases(flip)
        self.core = [k for k, b in enumerate(self.bits) if b[0] == "dp" and b[2] == 1][0]
        self.received = swap(send, self.bits[self.core])
        self.keep = keep
        self.names = [k for k in range(len(self.bits)) if k != self.core]
        self.order = [k for k in order[::-1] if k != self.core]
        self.partner = None

    def step(self):
        self.send = None
        keep, received = self.keep, self.received
        if not self.names:
            self.keep = keep.astype(jnp.float32) + received.astype(jnp.float32)
            self.received = None
            return
        shape = [2] * len(self.names) + [-1, keep.shape[-1]]
        keep, received = keep.reshape(shape), received.reshape(shape)
        k = self.order.pop(0)
        axis = self.names.index(k)
        self.names.remove(k)
        mine = own_bit(self.bits[k])

        def half(which):
            former, latter = (
                lax.dynamic_index_in_dim(v, which, axis, keepdims=False).astype(jnp.float32)
                for v in (keep, received)
            )
            return (former + latter).astype(jnp.bfloat16)

        self.send = (half(1 - mine), self.bits[k])
        self.keep = half(mine)

    def merge(self):
        other = self.partner
        if other is None or self.send is None or self.send[1][0] != "dp":
            return
        side_by_side = lambda *v: jnp.concatenate(v, axis=-1)
        self.send = (side_by_side(self.send[0], other.send[0]), self.send[1])
        self.keep = side_by_side(self.keep, other.keep)
        self.partner = other.received = other.send = None

    def launch(self):
        if self.send is not None:
            self.received = swap(*self.send)

    def done(self):
        while self.received is not None:
            self.step()
            self.launch()
        return self.keep


def scatter_pair(formers, latters, plan, rows):
    mine = own_bit(("dp", lax.axis_size("dp"), 1))
    sends = part_grads(formers, latters, plan, rows, 1 - mine)
    keeps = part_grads(formers, latters, plan, rows, mine)
    pair = [Scatter(send, keep, flip) for send, keep, flip in zip(sends, keeps, (False, True))]
    pair[0].partner = pair[1]
    return pair


class SmallScatter:
    def __init__(self, part):
        self.bits, order = phases(False)
        self.names = list(range(len(self.bits)))
        self.order = order[::-1]
        self.keep = part.reshape([2] * len(self.bits) + [1, part.shape[1]])
        self.received = None
        self.step()
        self.launch()

    def step(self):
        self.send = None
        if self.received is not None:
            self.keep = self.keep + self.received
            self.received = None
        if not self.names:
            return
        k = self.order.pop(0)
        axis = self.names.index(k)
        self.names.remove(k)
        mine = own_bit(self.bits[k])
        self.send = (
            lax.dynamic_index_in_dim(self.keep, 1 - mine, axis, keepdims=False), self.bits[k]
        )
        self.keep = lax.dynamic_index_in_dim(self.keep, mine, axis, keepdims=False)

    launch = Scatter.launch
    done = Scatter.done


class SmallSum:
    def __init__(self, part):
        bits, order = phases(False)
        self.bits = bits
        self.names = order[::-1]
        self.keep = part
        self.received = swap(part, bits[self.names.pop(0)])

    def step(self):
        self.keep = self.keep + self.received
        self.received = None
        self.send = (self.keep, self.bits[self.names.pop(0)]) if self.names else None

    launch = Scatter.launch
    done = Scatter.done


def advance(values, pipes):
    pipes = [p for p in pipes if p.received is not None]
    size = len(values)
    tied = tie(*values, *[p.received for p in pipes], *[p.keep for p in pipes])
    for k, p in enumerate(pipes):
        p.received, p.keep = tied[size + k], tied[size + len(pipes) + k]
        p.step()
    for p in pipes:
        if isinstance(p, Scatter):
            p.merge()
    values = tied[:size]
    pipes = [p for p in pipes if p.send is not None]
    tied = tie(*values, *[p.send[0] for p in pipes], *[p.keep for p in pipes])
    for k, p in enumerate(pipes):
        p.send = (tied[size + k], p.send[1])
        p.keep = tied[size + len(pipes) + k]
        p.launch()
    return tied[:size]


def local(
    context,
    byte_ids,
    segment_ids,
    cotangent,
    byte_table,
    norm_mixer,
    proj_zgate,
    proj_inputs,
    proj_step,
    conv_kernel,
    conv_bias,
    step_bias,
    decay_log,
    skip_gain,
    mixer_norm,
    proj_mixed,
    norm_attn,
    proj_heads,
    proj_attended,
    norm_ffn,
    ffn_gate,
    ffn_up,
    ffn_down,
):
    row_count, length = segment_ids.shape
    tokens = row_count * length
    model_width = context.shape[2]
    model_rows = norm_mixer.shape[0]
    small = [
        byte_table.reshape(-1),
        norm_mixer,
        conv_kernel.reshape(-1),
        conv_bias,
        mixer_norm,
        norm_attn,
        norm_ffn,
    ]
    lengths = [v.shape[0] for v in small]
    packed = jnp.concatenate(small)
    packed = jnp.pad(packed, (0, -packed.shape[0] % 1024)).reshape(8, -1)
    everyone = gather_small(packed).reshape(-1, packed.size)
    unpacked = []
    start = 0
    for count in lengths:
        unpacked.append(everyone[:, start : start + count])
        start += count
    table_full = unpacked[0].reshape(-1, byte_table.shape[1])
    gain_one = unpacked[1].reshape(-1)
    taps = conv_kernel.shape[0]
    kernel_full = jnp.swapaxes(
        unpacked[2].reshape(-1, taps, conv_kernel.shape[1]), 0, 1
    ).reshape(taps, -1)
    offset_full = unpacked[3].reshape(-1)
    gated_gain = unpacked[4].reshape(-1)
    gain_two = unpacked[5].reshape(-1)
    gain_three = unpacked[6].reshape(-1)
    wide = proj_inputs.shape[1]
    step_padded = jnp.pad(proj_step, ((0, 0), (0, 128 - proj_step.shape[1])))
    g_inputs = Gather(jnp.concatenate([proj_inputs, step_padded], axis=1), False)
    g_zgate = Gather(proj_zgate, True)
    fold_mixed = proj_mixed.shape[0] // model_rows
    fold_down = ffn_down.shape[0] // model_rows
    folded = lambda v, fold: [v[q * model_rows : (q + 1) * model_rows] for q in range(fold)]
    outer_shard = jnp.concatenate(
        [ffn_gate, ffn_up]
        + folded(ffn_down, fold_down)
        + folded(proj_mixed, fold_mixed)
        + [proj_heads, proj_attended],
        axis=1,
    )
    outer_full = lax.all_gather(outer_shard, AXES, axis=0, tiled=True)
    g_inputs.step()
    g_zgate.step()
    (table_full,) = gather_round([g_inputs, g_zgate], [table_full])
    gather_round([g_inputs, g_zgate])
    gather_round([g_inputs, g_zgate])
    gather_round([g_inputs, g_zgate])
    gather_round([g_inputs, g_zgate])
    inputs_step_full = g_inputs.done()
    zgate_full = g_zgate.done()
    symbols = jnp.arange(table_full.shape[0], dtype=jnp.int32)
    onehot = (byte_ids.reshape(-1)[:, None] == symbols[None, :]).astype(jnp.bfloat16)
    embedded = matmul(onehot, table_full).reshape(tokens, model_width)
    stream_zero = embedded + context.reshape(tokens, model_width).astype(jnp.float32)
    normed_one, norm_one_back = jax.vjp(rms_norm, stream_zero, gain_one.astype(jnp.float32))
    normed_one_low = normed_one.astype(jnp.bfloat16)
    zgate = matmul(normed_one_low, zgate_full).reshape(row_count, length, -1)
    raw = matmul(normed_one_low, inputs_step_full).reshape(row_count, length, -1)
    ids = segment_ids.astype(jnp.float32)
    pad_heads = lambda v: jnp.pad(v, (0, 128 - HM)).reshape(1, 128)
    mixer_terms = (
        ids,
        kernel_full.astype(jnp.float32),
        offset_full.astype(jnp.float32).reshape(1, -1),
        pad_heads(step_bias),
        pad_heads(decay_log),
        jnp.repeat(skip_gain, PM).reshape(1, -1),
        gated_gain.astype(jnp.float32).reshape(1, -1),
    )
    values_low, states_low, combined, gate_low = mixer_forward(raw, zgate, *mixer_terms)
    gate_low = gate_low.reshape(tokens, -1)
    outer_full, _ = tie(outer_full, gate_low)
    hidden_width = ffn_gate.shape[1]
    mixed_start = 2 * hidden_width + fold_down * model_width
    heads_start = mixed_start + fold_mixed * model_width
    attended_start = heads_start + proj_heads.shape[1]
    heads_full = outer_full[:, heads_start:attended_start]
    attended_full = outer_full[:, attended_start:]
    mixed_full = unfold(outer_full, model_rows, mixed_start, fold_mixed, model_width)
    mixer_out = matmul(gate_low, mixed_full)
    stream_one = stream_zero + mixer_out
    normed_two, norm_two_back = jax.vjp(rms_norm, stream_one, gain_two.astype(jnp.float32))
    normed_two_low = normed_two.astype(jnp.bfloat16)
    joined = matmul(normed_two_low, heads_full).astype(jnp.bfloat16)
    joined = joined.reshape(row_count, length, -1)
    attended_low = attention_forward(joined, ids).reshape(tokens, model_width)
    attn_out = matmul(attended_low, attended_full)
    stream_two = stream_one + attn_out
    normed_three, norm_three_back = jax.vjp(rms_norm, stream_two, gain_three.astype(jnp.float32))
    normed_three_low = normed_three.astype(jnp.bfloat16)
    ffn_grad_low = cotangent.reshape(tokens, model_width)
    grad_three = ffn_grad_low.astype(jnp.float32)
    hidden_low, gate_grad_low, upper_grad_low, ffn_out, grad_normed_three = feed_forward(
        normed_three_low, ffn_grad_low, outer_full, model_rows, hidden_width, fold_down
    )
    stream_three = stream_two + ffn_out
    valid_rows = (segment_ids.reshape(tokens, 1) >= 0).astype(jnp.float32)
    moments = jnp.stack(
        [
            jnp.sum(valid_rows * stream_zero * stream_zero),
            jnp.sum(valid_rows * mixer_out * mixer_out),
            jnp.sum(valid_rows * attn_out * attn_out),
            jnp.sum(valid_rows * ffn_out * ffn_out),
            jnp.sum(valid_rows),
        ]
    )
    fold_width = fold_down * model_width
    pipes = scatter_pair(
        [normed_three_low, hidden_low],
        [gate_grad_low, upper_grad_low, ffn_grad_low],
        [
            [(0, 0, 1, 0, hidden_width), (1, 2, fold_down, 0, fold_width // 2)],
            [(0, 1, 1, 0, hidden_width), (1, 2, fold_down, fold_width // 2, fold_width)],
        ],
        model_rows,
    )
    s_ffn = pipes[0]
    stream_part, grad_norm_ffn = norm_three_back(grad_normed_three)
    grad_two = grad_three + stream_part
    attn_grad_low = grad_two.astype(jnp.bfloat16)
    attn_grad_low, grad_two = advance((attn_grad_low, grad_two), pipes)
    grad_attended = (
        matmul_right(attn_grad_low, attended_full)
        .astype(jnp.bfloat16)
        .reshape(row_count, length, model_width)
    )
    grad_joined = attention_backward(joined, grad_attended, ids, []).reshape(tokens, -1)
    (grad_joined,) = advance((grad_joined,), pipes)
    heads_width = proj_heads.shape[1]
    cut_heads = (heads_width + model_width) // 2
    pair = scatter_pair(
        [normed_two_low, attended_low],
        [grad_joined, attn_grad_low],
        [
            [(0, 0, 1, 0, cut_heads)],
            [(0, 0, 1, cut_heads, heads_width), (1, 1, 1, 0, model_width)],
        ],
        model_rows,
    )
    s_heads = pair[0]
    pipes += pair
    grad_normed_two = matmul_right(grad_joined, heads_full)
    stream_part_two, grad_norm_attn = norm_two_back(grad_normed_two)
    grad_one = grad_two + stream_part_two
    mixer_grad_low = grad_one.astype(jnp.bfloat16)
    mixer_grad_low, grad_one = advance((mixer_grad_low, grad_one), pipes)
    grad_normed_gate = matmul_right(mixer_grad_low, mixed_full).reshape(row_count, length, -1)
    zgate_grad_low, heads_grad_low, grad_gated_gain, skip_lanes = gate_backward(
        grad_normed_gate, zgate, mixer_terms[-1], values_low, combined
    )
    zgate_grad_low = zgate_grad_low.reshape(tokens, -1)
    pair = scatter_pair(
        [normed_one_low, gate_low],
        [zgate_grad_low, mixer_grad_low],
        [
            [(0, 0, 1, 0, zgate_grad_low.shape[1])],
            [(1, 1, fold_mixed, 0, fold_mixed * model_width)],
        ],
        model_rows,
    )
    s_zgate = pair[0]
    pipes += pair
    zgate_grad_low, heads_grad_low = advance((zgate_grad_low, heads_grad_low), pipes)
    inputs_step_grad_low, grad_conv_kernel, grad_conv_bias, bias_lanes, decay_lanes = (
        mixer_backward(heads_grad_low, raw, *mixer_terms[:-1], values_low, states_low)
    )
    inputs_step_grad_low = inputs_step_grad_low.reshape(tokens, -1)
    (inputs_step_grad_low,) = advance((inputs_step_grad_low,), pipes)
    channels = inputs_step_grad_low.shape[1]
    middle = (channels // 256) * 128
    pair = scatter_pair(
        [normed_one_low],
        [inputs_step_grad_low],
        [[(0, 0, 1, 0, middle)], [(0, 0, 1, middle, channels)]],
        model_rows,
    )
    s_inputs = pair[0]
    pipes = pair + pipes
    small_grads = [
        moments,
        bias_lanes[0, :HM],
        decay_lanes[0, :HM],
        jnp.sum(skip_lanes.reshape(HM, PM), axis=1),
        grad_conv_kernel.reshape(-1),
        grad_conv_bias.reshape(-1),
        grad_gated_gain.reshape(-1),
        grad_norm_attn,
        grad_norm_ffn,
    ]
    small_lengths = [v.shape[0] for v in small_grads]
    small_packed = jnp.concatenate(small_grads)
    s_small = SmallSum(jnp.pad(small_packed, (0, -small_packed.shape[0] % 1024)).reshape(8, -1))
    pipes += [s_small]
    (inputs_step_grad_low,) = advance((inputs_step_grad_low,), pipes)
    grad_normed_one = matmul_right(zgate_grad_low, zgate_full) + matmul_right(
        inputs_step_grad_low, inputs_step_full
    )
    stream_part_one, grad_norm_mixer = norm_one_back(grad_normed_one)
    grad_zero = grad_one + stream_part_one
    embed_grad_low = grad_zero.reshape(-1, table_full.shape[1]).astype(jnp.bfloat16)
    grad_byte_table = matmul_left(onehot, embed_grad_low)
    late = jnp.concatenate(
        [
            grad_byte_table.reshape(-1, byte_table.size),
            grad_norm_mixer.reshape(-1, model_rows),
        ],
        axis=1,
    )
    late = jnp.pad(late, ((0, 0), (0, -late.shape[1] % 128)))
    s_late = SmallScatter(late)
    pipes = pipes[:2] + [s_late] + pipes[2:]
    while any(p.received is not None for p in pipes):
        advance((), pipes)
    late = s_late.done().reshape(-1)
    grad_inputs_step = s_inputs.done()
    zgate_mixed = s_zgate.done()
    attention_sums = s_heads.done()
    ffn_sums = s_ffn.done()
    half_fold = fold_width // 2
    second = hidden_width + half_fold
    down_sums = [ffn_sums[:, hidden_width:second], ffn_sums[:, second + hidden_width :]]
    zgate_width = zgate_grad_low.shape[1]

    def stacked(v):
        return jnp.concatenate(
            [v[:, q : q + model_width] for q in range(0, v.shape[1], model_width)], axis=0
        )

    table_sum = late[: byte_table.size].reshape(byte_table.shape)
    norm_mixer_sum = late[byte_table.size : byte_table.size + model_rows]
    small_sums = s_small.done().reshape(-1)
    sums = []
    start = 0
    for count in small_lengths:
        sums.append(small_sums[start : start + count])
        start += count
    totals, bias_total, decay_total, skip_total = sums[:4]
    kernel_sum = sums[4].reshape(taps, -1)
    offset_sum, gated_sum, norm_attn_sum, norm_ffn_sum = sums[5:]

    def own_part(total, share):
        length = share.shape[-1]
        return lax.dynamic_slice_in_dim(total, own_index() * length, length, total.ndim - 1)

    rms_stats = jnp.sqrt(totals[:4] / (totals[4] * model_width))
    return (
        stream_three.reshape(row_count, length, model_width),
        grad_zero.reshape(row_count, length, model_width),
        rms_stats,
        table_sum,
        norm_mixer_sum,
        zgate_mixed[:, :zgate_width],
        grad_inputs_step[:, :wide],
        grad_inputs_step[:, wide : wide + HM],
        own_part(kernel_sum, conv_kernel),
        own_part(offset_sum, conv_bias),
        bias_total,
        decay_total,
        skip_total,
        own_part(gated_sum, mixer_norm),
        stacked(zgate_mixed[:, zgate_width:]),
        own_part(norm_attn_sum, norm_attn),
        attention_sums[:, :heads_width],
        attention_sums[:, heads_width:],
        own_part(norm_ffn_sum, norm_ffn),
        ffn_sums[:, :hidden_width],
        ffn_sums[:, second : second + hidden_width],
        stacked(jnp.concatenate(down_sums, axis=1)),
    )


def solution(mesh):
    return jax.shard_map(
        local,
        mesh=mesh,
        in_specs=(
            P(("dp", "fsdp"), None, None),
            P(("dp", "fsdp"), None),
            P(("dp", "fsdp"), None),
            P(("dp", "fsdp"), None, None),
            P(("dp", "fsdp"), None),
            P(("dp", "fsdp")),
            P(("dp", "fsdp"), None),
            P(("dp", "fsdp"), None),
            P(("dp", "fsdp"), None),
            P(None, ("dp", "fsdp")),
            P(("dp", "fsdp")),
            P(),
            P(),
            P(),
            P(("dp", "fsdp")),
            P(("dp", "fsdp"), None),
            P(("dp", "fsdp")),
            P(("dp", "fsdp"), None),
            P(("dp", "fsdp"), None),
            P(("dp", "fsdp")),
            P(("dp", "fsdp"), None),
            P(("dp", "fsdp"), None),
            P(("dp", "fsdp"), None),
        ),
        out_specs=(
            P(("dp", "fsdp"), None, None),
            P(("dp", "fsdp"), None, None),
            P(),
            P(("dp", "fsdp"), None),
            P(("dp", "fsdp")),
            P(("dp", "fsdp"), None),
            P(("dp", "fsdp"), None),
            P(("dp", "fsdp"), None),
            P(None, ("dp", "fsdp")),
            P(("dp", "fsdp")),
            P(),
            P(),
            P(),
            P(("dp", "fsdp")),
            P(("dp", "fsdp"), None),
            P(("dp", "fsdp")),
            P(("dp", "fsdp"), None),
            P(("dp", "fsdp"), None),
            P(("dp", "fsdp")),
            P(("dp", "fsdp"), None),
            P(("dp", "fsdp"), None),
            P(("dp", "fsdp"), None),
        ),
        check_vma=False,
    )
```

time: 986 us -> 763 us (0.77)
  matrix products: 196 us -> 48.5 us
  Pallas kernels: 34.5 us -> 154 us
  local copies, waits for them, and re-layouts: 164 us -> 92.2 us
  other arithmetic: 120 us -> 77.1 us
  blocking collectives: 40.8 us -> 0 us
  starting transfers between devices: 86.7 us -> 60.2 us
  waiting for transfers between devices: 326 us -> 305 us
  between operations: 5.51 us -> 16.6 us
    pallas_call x0 -> x15, Pallas kernels: none -> 146 us  [the longest x8 48.3 us: part_grads(): pl.pallas_call(partial(grads_kernel, plan, rows, (len(formers), len(latte...]
    ppermute x98 -> x59, waiting for transfers between devices: 326 us -> 252 us  [swap(): return lax.ppermute(v, name, [(i, i ^ step) for i in range(size)])]
    dot_general x17 -> x1, matrix products: 62.5 us -> 1.55 us  [matmul_left(): lax.dot_general(former, latter, (((0,), (0,)), ((), ())), preferred_eleme...]
    all_gather x0 -> x1, waiting for transfers between devices: none -> 53.1 us  [local(): outer_full = lax.all_gather(outer_shard, AXES, axis=0, tiled=True)]
    psum x1 -> x0, blocking collectives: 40.8 us -> none  [local(): lax.psum((moments, grad_step_bias, grad_decay_log, grad_skip_gain, grad_c...]
    reshape x15 -> x6, local copies, waits for them, and re-layouts: 38.1 us -> 0.21 us  [the longest x1 0.08 us: __init__(): self.keep = part.reshape([2] * len(self.bits) + [1, part.shape[1]])]
    dot_general x12 -> x0, matrix products: 33.8 us -> none  [the longest x1 7.9 us: local(): jnp.einsum('nhts,nshp->nthp', weights_low, values_low, preferred_element_...]
    ppermute x98 -> x59, starting transfers between devices: 86.7 us -> 60.2 us  [swap(): return lax.ppermute(v, name, [(i, i ^ step) for i in range(size)])]
  transfers between devices with their start and end apart: 98 -> 60, of which waited for: 37 -> 31; matrix products, arithmetic and copies ran while one was open for 41% -> 11% of each run, Pallas kernels for 3% -> 12%
where the time goes in v2:
time: 763 us; the launch traced here: 754 us
  waiting for transfers between devices  305 us (40%)
  Pallas kernels  154 us (20%)
  local copies, waits for them, and re-layouts  92.2 us (12%)
  other arithmetic  77.1 us (10%)
  starting transfers between devices  60.2 us (8%)
  matrix products  48.5 us (6%)
  between operations  16.6 us (2%)
    ppermute x59, waiting for transfers between devices, swap(): return lax.ppermute(v, name, [(i, i ^ step) for i in range(size)])  252 us
    ppermute x59, starting transfers between devices, swap(): return lax.ppermute(v, name, [(i, i ^ step) for i in range(size)])  60.2 us
    convert_element_type x36, other arithmetic, half(): return (former + latter).astype(jnp.bfloat16)  54.8 us
    all_gather x1, waiting for transfers between devices, local(): outer_full = lax.all_gather(outer_shard, AXES, axis=0, tiled=True)  53.1 us
    pallas_call x8, Pallas kernels, part_grads(): pl.pallas_call(partial(grads_kernel, plan, rows, (len(formers), len(latte...  48.3 us
    unnamed x241, local copies, waits for them, and re-layouts  34.6 us
    pallas_call x1, Pallas kernels, feed_forward(): pl.pallas_call(partial(ffn_kernel, rows, fold), grid=(steps,), in_specs=[...  27.2 us
    dynamic_slice x16, local copies, waits for them, and re-layouts, half(): lax.dynamic_index_in_dim(v, which, axis, keepdims=False).astype(jnp.float32)  27.2 us
  transfers between devices with their start and end apart: 60, of which 31 were waited for; matrix products, arithmetic and copies ran while one was open for 11% of the time, Pallas kernels for 12%

profile of v2, /device:TPU:0, one launch (start us, length us, event | category | flops | bytes accessed | tf_op | source)
XLA Modules:
  0.0 753.6 jit_solution(15315843961907581755)
XLA Ops:
  35.0 7.0 collective-permute-done.4
  42.1 25.1 %collective-permute-done.6 = bf16[1,32,2048]{2,1,0:T(8,128)(2,1)S(1)} collective-permute-done((bf16[1,32,2048]{2,1,0:T(8,128)(2,1)S(1)}, bf16[1,32,2048]{2,1,0:T(8,128)(2,1)S(1)}, u32[]{:S(2)}, u32[]{:S(2)}) %collective-permute-start.6) | collective-permute-done | bytes 131104 | tf_op jit(solution)/shard_map/ppermute | solution.py:553
  69.4 28.9 %collective-permute-done.8 = bf16[2,32,2048]{2,1,0:T(8,128)(2,1)S(1)} collective-permute-done((bf16[2,32,2048]{2,1,0:T(8,128)(2,1)S(1)}, bf16[2,32,2048]{2,1,0:T(8,128)(2,1)S(1)}, u32[]{:S(2)}, u32[]{:S(2)}) %collective-permute-start.8) | collective-permute-done | bytes 262176 | tf_op jit(solution)/shard_map/ppermute | solution.py:553
  101.5 11.8 %collective-permute-done.10 = bf16[4,32,2048]{2,1,0:T(8,128)(2,1)S(1)} collective-permute-done((bf16[4,32,2048]{2,1,0:T(8,128)(2,1)S(1)}, bf16[4,32,2048]{2,1,0:T(8,128)(2,1)S(1)}, u32[]{:S(2)}, u32[]{:S(2)}) %collective-permute-start.10) | collective-permute-done | bytes 524320 | tf_op jit(solution)/shard_map/ppermute | solution.py:553
  113.3 12.7 %collective-permute-done.9 = bf16[4,32,2432]{2,1,0:T(8,128)(2,1)S(1)} collective-permute-done((bf16[4,32,2432]{2,1,0:T(8,128)(2,1)S(1)}, bf16[4,32,2432]{2,1,0:T(8,128)(2,1)S(1)}, u32[]{:S(2)}, u32[]{:S(2)}) %collective-permute-start.9) | collective-permute-done | bytes 622624 | tf_op jit(solution)/shard_map/ppermute | solution.py:553
  135.2 19.9 %collective-permute-done.12.refs_1_ = bf16[8,32,2048]{2,1,0:T(8,128)(2,1)} collective-permute-done((bf16[8,32,2048]{2,1,0:T(8,128)(2,1)}, bf16[8,32,2048]{2,1,0:T(8,128)(2,1)}, u32[]{:S(2)}, u32[]{:S(2)}) %collective-permute-start.12) | collective-permute-done | bytes 1048608 | tf_op jit(solution)/shard_map/ppermute | solution.py:553
  193.0 14.5 %shard_map.392 = (bf16[2,208,2048]{2,1,0:T(8,128)(2,1)S(1)}, bf16[2,208,256]{2,1,0:T(8,128)(2,1)S(1)}, f32[2,208,2048]{2,1,0:T(8,128)}, bf16[2,208,2048]{2,1,0:T(8,128)(2,1)S(1)}) custom-call(f32[2,208,2432]{2,1,0:T(8,128)} %fusion.107.raw_ref, f32[2,208,2048]{2,1,0:T(8,128)} %fusion.108.zgate_ref, f32[2,208,1]{2,1,0:T(8,128)S(1)} %copy.87.ids_column_ref, ...), custom_call_target="tpu_custom_call" | custom-call | flops 1024 | bytes 1024 | tf_op jit(solution)/shard_map/pallas_call | solution.py:319
  209.4 53.1 %all-gather.2.cloned.1.call-done.gate_ref.upper_ref.folded_ref = bf16[1024,18432]{1,0:T(8,128)(2,1)} async-done(((bf16[32,18432]{1,0:T(8,128)(2,1)}), bf16[1024,18432]{1,0:T(8,128)(2,1)}) %all-gather.2.cloned.1.call-update) | async-done | bytes 37748752 | tf_op jit(solution)/shard_map/all_gather | solution.py:965
  268.6 6.5 fusion.4
  284.9 27.2 %shard_map.395 = (bf16[416,4096]{1,0:T(8,128)(2,1)}, bf16[416,4096]{1,0:T(8,128)(2,1)}, bf16[416,4096]{1,0:T(8,128)(2,1)}, f32[416,1024]{1,0:T(8,128)S(1)}, f32[416,1024]{1,0:T(8,128)S(1)}) custom-call(bf16[416,1024]{1,0:T(8,128)(2,1)S(1)} %multiply_convert_fusion.1.source_ref.refs_0_, bf16[416,1024]{1,0:T(8,128)(2,1)S(1)} %bitcast.233, ...), custom_call_target="tpu_custom_call" | custom-call | flops 1024 | bytes 1024 | tf_op jit(solution)/shard_map/pallas_call | solution.py:510
  316.5 11.8 %shard_map.396 = (bf16[512,6144]{1,0:T(8,128)(2,1)}, bf16[512,6144]{1,0:T(8,128)(2,1)}) custom-call(s32[1]{0:T(128)} %bitcast.20.core_ref, bf16[416,1024]{1,0:T(8,128)(2,1)S(1)} %multiply_convert_fusion.1.source_ref.refs_0_, bf16[416,4096]{1,0:T(8,128)(2,1)S(1)} %copy-done.3, bf16[416,4096]{1,0:T(8,128)(2,1)} %get-tuple-element.278.refs_2_, ...), custom_call_target="tpu_custom_call" | custom-call | flops 1024 | bytes 1024 | tf_op jit(solution)/shard_map/pallas_call | solution.py:749
  330.7 11.9 %shard_map.397 = (bf16[512,6144]{1,0:T(8,128)(2,1)}, bf16[512,6144]{1,0:T(8,128)(2,1)}) custom-call(s32[1]{0:T(128)} %bitcast.21.core_ref, bf16[416,1024]{1,0:T(8,128)(2,1)S(1)} %multiply_convert_fusion.1.source_ref.refs_0_, bf16[416,4096]{1,0:T(8,128)(2,1)S(1)} %copy-done.4, bf16[416,4096]{1,0:T(8,128)(2,1)} %get-tuple-element.278.refs_2_, ...), custom_call_target="tpu_custom_call" | custom-call | flops 1024 | bytes 1024 | tf_op jit(solution)/shard_map/pallas_call | solution.py:749
  360.2 6.2 constant_dynamic-slice_fusion.32
  382.9 17.7 %shard_map.398 = bf16[2,208,3072]{2,1,0:T(8,128)(2,1)S(1)} custom-call(bf16[2,208,3072]{2,1,0:T(8,128)(2,1)S(1)} %bitcast.237, bf16[2,208,1024]{2,1,0:T(8,128)(2,1)S(1)} %bitcast.259, f32[2,208,1]{2,1,0:T(8,128)S(1)} %copy-done.21, f32[2,1,208]{2,1,0:T(1,128)S(1)} %broadcast_in_dim.19.ids_row_ref), custom_call_target="tpu_custom_call" | custom-call | flops 1024 | bytes 1024 | tf_op jit(solution)/shard_map/pallas_call | solution.py:455
  400.6 48.1 %collective-permute-done.19 = bf16[2,2,2,32,6144]{4,3,0,1,2:T(8,128)(2,1)} collective-permute-done((bf16[2,2,2,32,6144]{4,3,0,1,2:T(8,128)(2,1)}, bf16[2,2,2,32,6144]{4,3,0,1,2:T(8,128)(2,1)}, u32[]{:S(2)}, u32[]{:S(2)}) %collective-permute-start.19) | collective-permute-done | bytes 3145760 | tf_op jit(solution)/shard_map/ppermute | solution.py:553
  469.0 5.9 shard_map.400
  482.4 20.1 %collective-permute-done.21 = bf16[2,2,32,6144]{3,2,0,1:T(8,128)(2,1)} collective-permute-done((bf16[2,2,32,6144]{3,2,0,1:T(8,128)(2,1)}, bf16[2,2,32,6144]{3,2,0,1:T(8,128)(2,1)}, u32[]{:S(2)}, u32[]{:S(2)}) %collective-permute-start.21) | collective-permute-done | bytes 1572896 | tf_op jit(solution)/shard_map/ppermute | solution.py:553
  523.8 6.8 shard_map.401
  545.5 17.5 %collective-permute-done.26 = bf16[2,2,2,32,2048]{4,3,0,1,2:T(8,128)(2,1)} collective-permute-done((bf16[2,2,2,32,2048]{4,3,0,1,2:T(8,128)(2,1)}, bf16[2,2,2,32,2048]{4,3,0,1,2:T(8,128)(2,1)}, u32[]{:S(2)}, u32[]{:S(2)}) %collective-permute-start.26) | collective-permute-done | bytes 1048608 | tf_op jit(solution)/shard_map/ppermute | solution.py:553
  563.1 10.0 %collective-permute-done.25 = bf16[2,32,12288]{2,1,0:T(8,128)(2,1)} collective-permute-done((bf16[2,32,12288]{2,1,0:T(8,128)(2,1)}, bf16[2,32,12288]{2,1,0:T(8,128)(2,1)}, u32[]{:S(2)}, u32[]{:S(2)}) %collective-permute-start.25) | collective-permute-done | bytes 1572896 | tf_op jit(solution)/shard_map/ppermute | solution.py:553
  603.4 24.8 %shard_map.404 = (bf16[2,208,2432]{2,1,0:T(8,128)(2,1)S(1)}, f32[4,2304]{1,0:T(4,128)S(1)}, f32[1,2304]{1,0:T(1,128)S(1)}, f32[1,128]{1,0:T(1,128)S(1)}, f32[1,128]{1,0:T(1,128)S(1)}) custom-call(bf16[2,208,2048]{2,1,0:T(8,128)(2,1)S(1)} %copy-done.28, f32[2,208,2432]{2,1,0:T(8,128)} %fusion.107.raw_ref, f32[2,208,1]{2,1,0:T(8,128)S(1)} %copy-done.22, ...), custom_call_target="tpu_custom_call" | custom-call | flops 1024 | bytes 1024 | tf_op jit(solution)/shard_map/pallas_call | solution.py:363
  631.7 5.9 fusion.110
  655.4 6.2 collective-permute-done.37
  685.0 6.1 collective-permute-done.46
  (558 shorter events, 331.3 us)
Async XLA Ops:
  7.3 255.2 %all-gather.2.cloned.1.call-start = ((), (), s32[]{:S(2)}) async-start(), calls=%async_computation | async-start | bytes 38928384 | tf_op jit(solution)/shard_map/all_gather | solution.py:965
  32.0 35.2 %collective-permute-start.5 = (bf16[1,32,2432]{2,1,0:T(8,128)(2,1)S(1)}, bf16[1,32,2432]{2,1,0:T(8,128)(2,1)S(1)}, u32[]{:S(2)}, u32[]{:S(2)}) collective-permute-start(bf16[1,32,2432]{2,1,0:T(8,128)(2,1)S(1)} %fusion.79), channel_id=1, source_target_pairs={{0,16},{4,20},{8,24},{12,28},{16,0},{20,4},{24,8},{28,12},{1,17},{... | collective-permute-start | bytes 466952 | tf_op jit(solution)/shard_map/ppermute | solution.py:553
  32.1 35.1 %collective-permute-start.6 = (bf16[1,32,2048]{2,1,0:T(8,128)(2,1)S(1)}, bf16[1,32,2048]{2,1,0:T(8,128)(2,1)S(1)}, u32[]{:S(2)}, u32[]{:S(2)}) collective-permute-start(bf16[1,32,2048]{2,1,0:T(8,128)(2,1)S(1)} %bitcast.285), channel_id=1, source_target_pairs={{0,16},{4,20},{8,24},{12,28},{16,0},{20,4},{24,8},{28,12},{1,17},{... | collective-permute-start | bytes 393224 | tf_op jit(solution)/shard_map/ppermute | solution.py:553
  67.3 31.1 %collective-permute-start.7 = (bf16[2,32,2432]{2,1,0:T(8,128)(2,1)S(1)}, bf16[2,32,2432]{2,1,0:T(8,128)(2,1)S(1)}, u32[]{:S(2)}, u32[]{:S(2)}) collective-permute-start(bf16[2,32,2432]{2,1,0:T(8,128)(2,1)S(1)} %constant_dynamic-update-slice_fusion), channel_id=1, source_target_pairs={{0,8},{4,12},{8,0},{12,4},{16,24},{20,28},{24,16},{28,20},{1,9},{5... | collective-permute-start | bytes 933896 | tf_op jit(solution)/shard_map/ppermute | solution.py:553
  67.4 31.0 %collective-permute-start.8 = (bf16[2,32,2048]{2,1,0:T(8,128)(2,1)S(1)}, bf16[2,32,2048]{2,1,0:T(8,128)(2,1)S(1)}, u32[]{:S(2)}, u32[]{:S(2)}) collective-permute-start(bf16[2,32,2048]{2,1,0:T(8,128)(2,1)S(1)} %constant_dynamic-update-slice_fusion.2), channel_id=1, source_target_pairs={{0,8},{4,12},{8,0},{12,4},{16,24},{20,28},{24,16},{28,20},{1,9},{5... | collective-permute-start | bytes 786440 | tf_op jit(solution)/shard_map/ppermute | solution.py:553
  98.4 27.6 %collective-permute-start.9 = (bf16[4,32,2432]{2,1,0:T(8,128)(2,1)S(1)}, bf16[4,32,2432]{2,1,0:T(8,128)(2,1)S(1)}, u32[]{:S(2)}, u32[]{:S(2)}) collective-permute-start(bf16[4,32,2432]{2,1,0:T(8,128)(2,1)S(1)} %constant_dynamic-update-slice_fusion.4), channel_id=1, source_target_pairs={{0,1},{1,0},{2,3},{3,2},{4,5},{5,4},{6,7},{7,6},{8,9},{9,8},{10,11... | collective-permute-start | bytes 1867784 | tf_op jit(solution)/shard_map/ppermute | solution.py:553
  126.2 32.0 %collective-permute-start.11 = (bf16[8,32,2432]{2,1,0:T(8,128)(2,1)S(1)}, bf16[8,32,2432]{2,1,0:T(8,128)(2,1)}, u32[]{:S(2)}, u32[]{:S(2)}) collective-permute-start(bf16[8,32,2432]{2,1,0:T(8,128)(2,1)S(1)} %constant_dynamic-update-slice_fusion.8.refs_0_), channel_id=1, source_target_pairs={{0,2},{1,3},{2,0},{3,1},{4,6},{5,7},{6,4},{7,5},{8,10},{9,11},{10,... | collective-permute-start | bytes 3735560 | tf_op jit(solution)/shard_map/ppermute | solution.py:553
  129.4 25.8 %collective-permute-start.12 = (bf16[8,32,2048]{2,1,0:T(8,128)(2,1)}, bf16[8,32,2048]{2,1,0:T(8,128)(2,1)}, u32[]{:S(2)}, u32[]{:S(2)}) collective-permute-start(bf16[8,32,2048]{2,1,0:T(8,128)(2,1)} %constant_dynamic-update-slice_fusion.10.refs_0_), channel_id=1, source_target_pairs={{0,1},{1,0},{2,3},{3,2},{4,5},{5,4},{6,7},{7,6},{8,9},{9,8},{10,11... | collective-permute-start | bytes 3145736 | tf_op jit(solution)/shard_map/ppermute | solution.py:553
  378.1 70.6 %collective-permute-start.19 = (bf16[2,2,2,32,6144]{4,3,0,1,2:T(8,128)(2,1)}, bf16[2,2,2,32,6144]{4,3,0,1,2:T(8,128)(2,1)}, u32[]{:S(2)}, u32[]{:S(2)}) collective-permute-start(bf16[2,2,2,32,6144]{4,3,0,1,2:T(8,128)(2,1)} %fusion.9), channel_id=1, source_target_pairs={{0,2},{1,3},{2,0},{3,1},{4,6},{5,7},{6,4},{7,5},{8,10},{9,11},{10,... | collective-permute-start | bytes 9437192 | tf_op jit(solution)/shard_map/ppermute | solution.py:553
  379.5 70.3 %collective-permute-start.20 = (bf16[2,2,2,32,6144]{4,3,0,1,2:T(8,128)(2,1)}, bf16[2,2,2,32,6144]{4,3,0,1,2:T(8,128)(2,1)}, u32[]{:S(2)}, u32[]{:S(2)}) collective-permute-start(bf16[2,2,2,32,6144]{4,3,0,1,2:T(8,128)(2,1)} %fusion.10), channel_id=1, source_target_pairs={{0,1},{1,0},{2,3},{3,2},{4,5},{5,4},{6,7},{7,6},{8,9},{9,8},{10,11... | collective-permute-start | bytes 9437192 | tf_op jit(solution)/shard_map/ppermute | solution.py:553
  465.3 37.4 %collective-permute-start.23 = (bf16[512,2048]{1,0:T(8,128)(2,1)}, bf16[512,2048]{1,0:T(8,128)(2,1)}, u32[]{:S(2)}, u32[]{:S(2)}) collective-permute-start(bf16[512,2048]{1,0:T(8,128)(2,1)} %get-tuple-element.304), channel_id=1, source_target_pairs={{0,4},{4,0},{8,12},{12,8},{16,20},{20,16},{24,28},{28,24},{1,5},{5... | collective-permute-start | bytes 6291464 | tf_op jit(solution)/shard_map/ppermute | solution.py:553
  465.3 37.4 %collective-permute-start.24 = (bf16[512,2048]{1,0:T(8,128)(2,1)}, bf16[512,2048]{1,0:T(8,128)(2,1)}, u32[]{:S(2)}, u32[]{:S(2)}) collective-permute-start(bf16[512,2048]{1,0:T(8,128)(2,1)} %get-tuple-element.305), channel_id=1, source_target_pairs={{0,4},{4,0},{8,12},{12,8},{16,20},{20,16},{24,28},{28,24},{1,5},{5... | collective-permute-start | bytes 6291464 | tf_op jit(solution)/shard_map/ppermute | solution.py:553
  465.9 36.6 %collective-permute-start.21 = (bf16[2,2,32,6144]{3,2,0,1:T(8,128)(2,1)}, bf16[2,2,32,6144]{3,2,0,1:T(8,128)(2,1)}, u32[]{:S(2)}, u32[]{:S(2)}) collective-permute-start(bf16[2,2,32,6144]{3,2,0,1:T(8,128)(2,1)} %get-tuple-element.302), channel_id=1, source_target_pairs={{0,1},{1,0},{2,3},{3,2},{4,5},{5,4},{6,7},{7,6},{8,9},{9,8},{10,11... | collective-permute-start | bytes 4718600 | tf_op jit(solution)/shard_map/ppermute | solution.py:553
  466.4 36.3 %collective-permute-start.22 = (bf16[2,2,32,6144]{3,2,0,1:T(8,128)(2,1)}, bf16[2,2,32,6144]{3,2,0,1:T(8,128)(2,1)}, u32[]{:S(2)}, u32[]{:S(2)}) collective-permute-start(bf16[2,2,32,6144]{3,2,0,1:T(8,128)(2,1)} %get-tuple-element.303), channel_id=1, source_target_pairs={{0,2},{1,3},{2,0},{3,1},{4,6},{5,7},{6,4},{7,5},{8,10},{9,11},{10,... | collective-permute-start | bytes 4718600 | tf_op jit(solution)/shard_map/ppermute | solution.py:553
  536.0 37.1 %collective-permute-start.28 = (bf16[512,2048]{1,0:T(8,128)(2,1)}, bf16[512,2048]{1,0:T(8,128)(2,1)}, u32[]{:S(2)}, u32[]{:S(2)}) collective-permute-start(bf16[512,2048]{1,0:T(8,128)(2,1)} %get-tuple-element.329), channel_id=1, source_target_pairs={{0,4},{4,0},{8,12},{12,8},{16,20},{20,16},{24,28},{28,24},{1,5},{5... | collective-permute-start | bytes 6291464 | tf_op jit(solution)/shard_map/ppermute | solution.py:553
  536.0 37.1 %collective-permute-start.29 = (bf16[512,2048]{1,0:T(8,128)(2,1)}, bf16[512,2048]{1,0:T(8,128)(2,1)}, u32[]{:S(2)}, u32[]{:S(2)}) collective-permute-start(bf16[512,2048]{1,0:T(8,128)(2,1)} %get-tuple-element.330), channel_id=1, source_target_pairs={{0,4},{4,0},{8,12},{12,8},{16,20},{20,16},{24,28},{28,24},{1,5},{5... | collective-permute-start | bytes 6291464 | tf_op jit(solution)/shard_map/ppermute | solution.py:553
  536.5 36.6 %collective-permute-start.25 = (bf16[2,32,12288]{2,1,0:T(8,128)(2,1)}, bf16[2,32,12288]{2,1,0:T(8,128)(2,1)}, u32[]{:S(2)}, u32[]{:S(2)}) collective-permute-start(bf16[2,32,12288]{2,1,0:T(8,128)(2,1)} %pad_maximum_fusion), channel_id=1, source_target_pairs={{0,8},{4,12},{8,0},{12,4},{16,24},{20,28},{24,16},{28,20},{1,9},{5... | collective-permute-start | bytes 4718600 | tf_op jit(solution)/shard_map/ppermute | solution.py:553
  537.9 25.1 %collective-permute-start.26 = (bf16[2,2,2,32,2048]{4,3,0,1,2:T(8,128)(2,1)}, bf16[2,2,2,32,2048]{4,3,0,1,2:T(8,128)(2,1)}, u32[]{:S(2)}, u32[]{:S(2)}) collective-permute-start(bf16[2,2,2,32,2048]{4,3,0,1,2:T(8,128)(2,1)} %fusion.33), channel_id=1, source_target_pairs={{0,2},{1,3},{2,0},{3,1},{4,6},{5,7},{6,4},{7,5},{8,10},{9,11},{10,... | collective-permute-start | bytes 3145736 | tf_op jit(solution)/shard_map/ppermute | solution.py:553
  538.2 24.8 %collective-permute-start.27 = (bf16[2,2,2,32,2048]{4,3,0,1,2:T(8,128)(2,1)}, bf16[2,2,2,32,2048]{4,3,0,1,2:T(8,128)(2,1)}, u32[]{:S(2)}, u32[]{:S(2)}) collective-permute-start(bf16[2,2,2,32,2048]{4,3,0,1,2:T(8,128)(2,1)} %fusion.34), channel_id=1, source_target_pairs={{0,1},{1,0},{2,3},{3,2},{4,5},{5,4},{6,7},{7,6},{8,9},{9,8},{10,11... | collective-permute-start | bytes 3145736 | tf_op jit(solution)/shard_map/ppermute | solution.py:553
  592.9 44.7 %collective-permute-start.33 = (bf16[2,2,2,32,2048]{4,3,0,1,2:T(8,128)(2,1)}, bf16[2,2,2,32,2048]{4,3,0,1,2:T(8,128)(2,1)}, u32[]{:S(2)}, u32[]{:S(2)}) collective-permute-start(bf16[2,2,2,32,2048]{4,3,0,1,2:T(8,128)(2,1)} %fusion.37), channel_id=1, source_target_pairs={{0,2},{1,3},{2,0},{3,1},{4,6},{5,7},{6,4},{7,5},{8,10},{9,11},{10,... | collective-permute-start | bytes 3145736 | tf_op jit(solution)/shard_map/ppermute | solution.py:553
  594.3 43.3 %collective-permute-start.34 = (bf16[2,2,2,32,2048]{4,3,0,1,2:T(8,128)(2,1)}, bf16[2,2,2,32,2048]{4,3,0,1,2:T(8,128)(2,1)}, u32[]{:S(2)}, u32[]{:S(2)}) collective-permute-start(bf16[2,2,2,32,2048]{4,3,0,1,2:T(8,128)(2,1)} %fusion.38), channel_id=1, source_target_pairs={{0,1},{1,0},{2,3},{3,2},{4,5},{5,4},{6,7},{7,6},{8,9},{9,8},{10,11... | collective-permute-start | bytes 3145736 | tf_op jit(solution)/shard_map/ppermute | solution.py:553
  596.9 40.7 %collective-permute-start.30 = (bf16[32,12288]{1,0:T(8,128)(2,1)}, bf16[32,12288]{1,0:T(8,128)(2,1)}, u32[]{:S(2)}, u32[]{:S(2)}) collective-permute-start(bf16[32,12288]{1,0:T(8,128)(2,1)} %get-tuple-element.352), channel_id=1, source_target_pairs={{0,16},{4,20},{8,24},{12,28},{16,0},{20,4},{24,8},{28,12},{1,17},{... | collective-permute-start | bytes 2359304 | tf_op jit(solution)/shard_map/ppermute | solution.py:553
  598.5 39.1 %collective-permute-start.31 = (bf16[2,2,32,2048]{3,2,0,1:T(8,128)(2,1)}, bf16[2,2,32,2048]{3,2,0,1:T(8,128)(2,1)}, u32[]{:S(2)}, u32[]{:S(2)}) collective-permute-start(bf16[2,2,32,2048]{3,2,0,1:T(8,128)(2,1)} %get-tuple-element.353), channel_id=1, source_target_pairs={{0,1},{1,0},{2,3},{3,2},{4,5},{5,4},{6,7},{7,6},{8,9},{9,8},{10,11... | collective-permute-start | bytes 1572872 | tf_op jit(solution)/shard_map/ppermute | solution.py:553
  599.9 37.7 %collective-permute-start.32 = (bf16[2,2,32,2048]{3,2,0,1:T(8,128)(2,1)}, bf16[2,2,32,2048]{3,2,0,1:T(8,128)(2,1)}, u32[]{:S(2)}, u32[]{:S(2)}) collective-permute-start(bf16[2,2,32,2048]{3,2,0,1:T(8,128)(2,1)} %get-tuple-element.354), channel_id=1, source_target_pairs={{0,2},{1,3},{2,0},{3,1},{4,6},{5,7},{6,4},{7,5},{8,10},{9,11},{10,... | collective-permute-start | bytes 1572872 | tf_op jit(solution)/shard_map/ppermute | solution.py:553
  (148 other events, 1606.3 us)
Sparse Core Ops, SparseCore 0:
  15.0 247.4 all-gather.1

commit v3 on v2

--- a/solution.py
+++ b/solution.py
@@ -178,9 +178,11 @@
 
 
 def gate_backward_kernel(
-    grad_ref, zgate_ref, gain_ref, values_ref, combined_ref,
-    zgrad_ref, heads_ref, gain_grad_ref, skip_grad_ref,
+    upper_ref, weight_ref, zgate_ref, gain_ref, values_ref, combined_ref,
+    zgrad_ref, heads_ref, gain_grad_ref, skip_grad_ref, grad_ref,
 ):
+    grad_ref[0] = matmul_right(upper_ref[0], weight_ref[...])
+
     @pl.when(pl.program_id(0) == 0)
     def _():
         for ref in (gain_grad_ref, skip_grad_ref):
@@ -284,6 +286,9 @@
     grad_raw = jnp.where(lane < HM, grad_step * sigmoid(shifted_step), 0.0)
     bias_grad_ref[...] += column_sum(grad_raw)
     xgrad_ref[0, :, channels : channels + 128] = grad_raw.astype(jnp.bfloat16)
+    extra = xgrad_ref.shape[2] - channels - 128
+    if extra:
+        xgrad_ref[0, :, channels + 128 :] = jnp.zeros((length, extra), jnp.bfloat16)
     gram_low = grad_gram.astype(jnp.bfloat16)
     grad_in = matmul_left(gram_low, state_out)
     grad_out = matmul(gram_low, state_in)
@@ -336,29 +341,33 @@
     )(raw, zgate, ids[:, :, None], ids[:, None, :], taps, offset, bias, decay, skip, gain)
 
 
-def gate_backward(grad, zgate, gain, values, combined):
-    count, length, _ = grad.shape
+def gate_backward(upper, weight, zgate, gain, values, combined):
+    count, length, width = upper.shape
     row = lambda c: pl.BlockSpec((1, length, c), lambda n: (n, 0, 0))
     one = lambda r, c: jax.ShapeDtypeStruct((r, c), jnp.float32)
     return pl.pallas_call(
         gate_backward_kernel,
         grid=(count,),
-        in_specs=[row(DI), row(DI), whole(1, DI), row(DI), row(DI)],
+        in_specs=[
+            row(width), whole(DI, width), row(DI), whole(1, DI), row(DI), row(DI)
+        ],
         out_specs=[row(DI), row(DI), whole(1, DI), whole(1, DI)],
         out_shape=[
             jax.ShapeDtypeStruct((count, length, DI), jnp.bfloat16),
             jax.ShapeDtypeStruct((count, length, DI), jnp.bfloat16),
             one(1, DI), one(1, DI),
         ],
+        scratch_shapes=[pltpu.VMEM((1, length, DI), jnp.float32)],
         compiler_params=pltpu.CompilerParams(vmem_limit_bytes=VMEM_LIMIT),
         cost_estimate=BRIEF,
-    )(grad, zgate, gain, values, combined)
+    )(upper, weight, zgate, gain, values, combined)
 
 
 def mixer_backward(heads, raw, ids, taps, offset, bias, decay, skip, values, states):
     count, length, columns = raw.shape
     row = lambda c: pl.BlockSpec((1, length, c), lambda n: (n, 0, 0))
     channels = taps.shape[1]
+    extra = -columns % 256
     one = lambda r, c: jax.ShapeDtypeStruct((r, c), jnp.float32)
     return pl.pallas_call(
         mixer_backward_kernel,
@@ -370,10 +379,11 @@
             whole(1, DI), row(DI), row(2 * NS),
         ],
         out_specs=[
-            row(columns), whole(*taps.shape), whole(1, channels), whole(1, 128), whole(1, 128),
+            row(columns + extra), whole(*taps.shape), whole(1, channels), whole(1, 128),
+            whole(1, 128),
         ],
         out_shape=[
-            jax.ShapeDtypeStruct((count, length, columns), jnp.bfloat16),
+            jax.ShapeDtypeStruct((count, length, columns + extra), jnp.bfloat16),
             one(*taps.shape), one(1, channels), one(1, 128), one(1, 128),
         ],
         scratch_shapes=[pltpu.VMEM((length, DI), jnp.float32)],
@@ -408,8 +418,10 @@
         )
 
 
-def attention_backward_kernel(joined_ref, grad_ref, ids_column_ref, ids_row_ref, *rest):
-    out_ref = rest[-1]
+def attention_backward_kernel(
+    joined_ref, upper_ref, weight_ref, ids_column_ref, ids_row_ref, out_ref, grad_ref
+):
+    grad_ref[0] = matmul_right(upper_ref[0], weight_ref[...]).astype(jnp.bfloat16)
     mask = allowed_mask(ids_column_ref[0], ids_row_ref[0])
     length, width = grad_ref.shape[1:]
     first = lax.broadcasted_iota(jnp.int32, (length, 2 * HD), 1) < HD
@@ -449,21 +461,70 @@
     )(joined, ids[:, :, None], ids[:, None, :])
 
 
-def attention_backward(joined, grad, ids, waits):
+def attention_backward(joined, upper, full, block, ids):
     count, length, columns = joined.shape
+    width = columns // 3
     row = lambda c: pl.BlockSpec((1, length, c), lambda n: (n, 0, 0))
     return pl.pallas_call(
         attention_backward_kernel,
         grid=(count,),
         in_specs=[
-            row(columns), row(columns // 3), row(1),
+            row(columns), row(width), pl.BlockSpec((width, width), lambda n: (0, block)), row(1),
             pl.BlockSpec((1, 1, length), lambda n: (n, 0, 0)),
-        ] + [pl.BlockSpec(memory_space=pl.ANY)] * len(waits),
+        ],
         out_specs=row(columns),
         out_shape=jax.ShapeDtypeStruct((count, length, columns), jnp.bfloat16),
+        scratch_shapes=[pltpu.VMEM((1, length, width), jnp.bfloat16)],
         compiler_params=pltpu.CompilerParams(vmem_limit_bytes=VMEM_LIMIT),
         cost_estimate=BRIEF,
-    )(joined, grad, ids[:, :, None], ids[:, None, :], *waits)
+    )(joined, upper, full, ids[:, :, None], ids[:, None, :])
+
+
+def norm_backward_kernel(count, *refs):
+    acts, weights = refs[:count], refs[count : 2 * count]
+    stream_ref, gain_ref, base_ref, total_ref, low_ref, gain_grad_ref, sum_ref = refs[2 * count :]
+    step = pl.program_id(0)
+    rows = weights[0].shape[0]
+    part = 0.0
+    for act, weight in zip(acts, weights):
+        part = part + matmul_right(act[:, : weight.shape[1]], weight[...])
+    sum_ref[:, pl.ds(pl.multiple_of(step * rows, rows), rows)] = part
+
+    @pl.when(step == pl.num_programs(0) - 1)
+    def _():
+        values, grad, gain = stream_ref[...], sum_ref[...], gain_ref[...]
+        scale = lax.rsqrt(jnp.mean(values * values, axis=1, keepdims=True) + EPS)
+        gain_grad_ref[...] = column_sum(grad * values * scale)
+        scaled = grad * gain
+        inner = jnp.mean(scaled * values, axis=1, keepdims=True)
+        total = base_ref[...] + scale * scaled - values * (scale * scale * scale * inner)
+        total_ref[...] = total
+        low_ref[...] = total.astype(jnp.bfloat16)
+
+
+def norm_backward(pairs, stream, gain, base):
+    tokens, width = stream.shape
+    rows = width // 4
+    fixed = lambda r, c, k=0: pl.BlockSpec((r, c), lambda i: (0, k))
+    return pl.pallas_call(
+        partial(norm_backward_kernel, len(pairs)),
+        grid=(4,),
+        in_specs=[fixed(tokens, a.shape[1] if w is None else w, k) for a, k, _, _, w in pairs]
+        + [
+            pl.BlockSpec((rows, m.shape[1] if w is None else w), lambda i, k=k: (i, k))
+            for _, _, m, k, w in pairs
+        ]
+        + [fixed(tokens, width), fixed(1, width), fixed(tokens, width)],
+        out_specs=[fixed(tokens, width), fixed(tokens, width), fixed(1, width)],
+        out_shape=[
+            jax.ShapeDtypeStruct((tokens, width), jnp.float32),
+            jax.ShapeDtypeStruct((tokens, width), jnp.bfloat16),
+            jax.ShapeDtypeStruct((1, width), jnp.float32),
+        ],
+        scratch_shapes=[pltpu.VMEM((tokens, width), jnp.float32)],
+        compiler_params=pltpu.CompilerParams(vmem_limit_bytes=VMEM_LIMIT),
+        cost_estimate=BRIEF,
+    )(*[p[0] for p in pairs], *[p[2] for p in pairs], stream, gain, base)
 
 
 def ffn_kernel(
@@ -540,12 +601,12 @@
     return bits
 
 
-def phases(flip):
+def phases(flip, turn=False):
     bits = axis_bits()
     outer = [k for k, b in enumerate(bits) if b[0] == "dp" and b[2] > 1]
     core = [k for k, b in enumerate(bits) if b[0] == "dp" and b[2] == 1]
     inner = [k for k, b in enumerate(bits) if b[0] == "fsdp"]
-    return bits, outer + (inner if flip else inner[::-1]) + core
+    return bits, (outer[::-1] if turn else outer) + (inner if flip else inner[::-1]) + core
 
 
 def swap(v, bit):
@@ -709,14 +770,18 @@
     for out_ref, items in zip(refs[counts[0] + counts[1] :], plan):
         start = 0
         for former, latter, fold, low, high in items:
-            if (former, latter) not in products:
-                products[former, latter] = matmul_left(
-                    formers[former][...], latters[latter][...]
-                ).astype(jnp.bfloat16)
-            product = products[former, latter]
             if fold == 1:
-                out_ref[:, start : start + high - low] = product[:, low:high]
+                for at in range(low, high, 512):
+                    to = min(at + 512, high)
+                    out_ref[:, start + at - low : start + to - low] = matmul_left(
+                        formers[former][...], latters[latter][:, at:to]
+                    ).astype(jnp.bfloat16)
             else:
+                if (former, latter) not in products:
+                    products[former, latter] = matmul_left(
+                        formers[former][...], latters[latter][...]
+                    ).astype(jnp.bfloat16)
+                product = products[former, latter]
                 width = product.shape[1]
                 for d in range(product.shape[0] // (fold * rows)):
                     for q in range(low // width, high // width):
@@ -761,97 +826,89 @@
     )(core.astype(jnp.int32).reshape(1), *formers, *latters)
 
 
+def add_halves_kernel(mine_ref, give, give_more, hold, hold_more, send_ref, keep_ref):
+    for former, latter, out in ((give, give_more, send_ref), (hold, hold_more, keep_ref)):
+        out[...] = (
+            former[...].astype(jnp.float32) + latter[...].astype(jnp.float32)
+        ).astype(jnp.bfloat16)
+
+
+def add_halves(keep, received, mine, part=0, parts=1):
+    before, _, rows, columns = keep.shape
+    columns //= parts
+    tiles = 1
+    while before * tiles < 4 and columns % (256 * tiles) == 0:
+        tiles *= 2
+    width = columns // tiles
+    several = max(1, before // 4)
+    other = pl.BlockSpec((several, None, rows, width), lambda i, j, m: (i, 1 - m[0], 0, part * tiles + j))
+    own = pl.BlockSpec((several, None, rows, width), lambda i, j, m: (i, m[0], 0, part * tiles + j))
+    out = pl.BlockSpec((several, rows, width), lambda i, j, m: (i, 0, j))
+    return pl.pallas_call(
+        add_halves_kernel,
+        grid_spec=pltpu.PrefetchScalarGridSpec(
+            num_scalar_prefetch=1,
+            grid=(before // several, tiles),
+            in_specs=[other, other, own, own],
+            out_specs=[out, out],
+        ),
+        out_shape=[jax.ShapeDtypeStruct((before, rows, columns), jnp.bfloat16)] * 2,
+        compiler_params=pltpu.CompilerParams(vmem_limit_bytes=VMEM_LIMIT),
+        cost_estimate=BRIEF,
+    )(mine.astype(jnp.int32).reshape(1), keep, received, keep, received)
+
+
 class Scatter:
-    def __init__(self, send, keep, flip):
-        self.bits, order = phases(flip)
-        self.core = [k for k, b in enumerate(self.bits) if b[0] == "dp" and b[2] == 1][0]
-        self.received = swap(send, self.bits[self.core])
-        self.keep = keep
-        self.names = [k for k in range(len(self.bits)) if k != self.core]
-        self.order = [k for k in order[::-1] if k != self.core]
-        self.partner = None
-
-    def step(self):
+    def __init__(self, keep, received, part):
+        self.bits, order = phases(part == 1, part == 1)
+        core = [k for k, b in enumerate(self.bits) if b[0] == "dp" and b[2] == 1][0]
+        self.names = [k for k in range(len(self.bits)) if k != core]
+        self.order = [k for k in order[::-1] if k != core]
+        self.keep, self.received = keep, received
+        self.step(part, 2)
+
+    def step(self, part=0, parts=1):
         self.send = None
         keep, received = self.keep, self.received
         if not self.names:
-            self.keep = keep.astype(jnp.float32) + received.astype(jnp.float32)
-            self.received = None
-            return
-        shape = [2] * len(self.names) + [-1, keep.shape[-1]]
-        keep, received = keep.reshape(shape), received.reshape(shape)
-        k = self.order.pop(0)
-        axis = self.names.index(k)
-        self.names.remove(k)
-        mine = own_bit(self.bits[k])
-
-        def half(which):
-            former, latter = (
-                lax.dynamic_index_in_dim(v, which, axis, keepdims=False).astype(jnp.float32)
-                for v in (keep, received)
-            )
-            return (former + latter).astype(jnp.bfloat16)
-
-        self.send = (half(1 - mine), self.bits[k])
-        self.keep = half(mine)
-
-    def merge(self):
-        other = self.partner
-        if other is None or self.send is None or self.send[1][0] != "dp":
-            return
-        side_by_side = lambda *v: jnp.concatenate(v, axis=-1)
-        self.send = (side_by_side(self.send[0], other.send[0]), self.send[1])
-        self.keep = side_by_side(self.keep, other.keep)
-        self.partner = other.received = other.send = None
-
-    def launch(self):
-        if self.send is not None:
-            self.received = swap(*self.send)
-
-    def done(self):
-        while self.received is not None:
-            self.step()
-            self.launch()
-        return self.keep
-
-
-def scatter_pair(formers, latters, plan, rows):
-    mine = own_bit(("dp", lax.axis_size("dp"), 1))
-    sends = part_grads(formers, latters, plan, rows, 1 - mine)
-    keeps = part_grads(formers, latters, plan, rows, mine)
-    pair = [Scatter(send, keep, flip) for send, keep, flip in zip(sends, keeps, (False, True))]
-    pair[0].partner = pair[1]
-    return pair
-
-
-class SmallScatter:
-    def __init__(self, part):
-        self.bits, order = phases(False)
-        self.names = list(range(len(self.bits)))
-        self.order = order[::-1]
-        self.keep = part.reshape([2] * len(self.bits) + [1, part.shape[1]])
-        self.received = None
-        self.step()
-        self.launch()
-
-    def step(self):
-        self.send = None
-        if self.received is not None:
-            self.keep = self.keep + self.received
-            self.received = None
-        if not self.names:
+            total = keep.astype(jnp.float32) + received.astype(jnp.float32)
+            self.keep, self.received = total.reshape(-1, total.shape[-1]), None
             return
         k = self.order.pop(0)
         axis = self.names.index(k)
         self.names.remove(k)
-        mine = own_bit(self.bits[k])
-        self.send = (
-            lax.dynamic_index_in_dim(self.keep, 1 - mine, axis, keepdims=False), self.bits[k]
+        columns = keep.shape[-1]
+        shape = (2**axis, 2, keep.size // columns // 2 ** (axis + 1), columns)
+        send, self.keep = add_halves(
+            keep.reshape(shape), received.reshape(shape), own_bit(self.bits[k]), part, parts
         )
-        self.keep = lax.dynamic_index_in_dim(self.keep, mine, axis, keepdims=False)
-
-    launch = Scatter.launch
-    done = Scatter.done
+        self.send = (send, self.bits[k])
+
+    def launch(self):
+        self.received, self.send = swap(*self.send), None
+
+
+class Pair:
+    def __init__(self, formers, latters, items, rows):
+        bit = ("dp", lax.axis_size("dp"), 1)
+        self.mine = own_bit(bit)
+        self.parts = (formers, latters, [items], rows)
+        (send,) = part_grads(*self.parts, 1 - self.mine)
+        self.send, self.received, self.keep = (send, bit), None, None
+
+    def own(self):
+        (self.keep,) = part_grads(*self.parts, self.mine)
+        return self
+
+    def launch(self):
+        self.received, self.send = swap(*self.send), None
+
+    def split(self):
+        self.pipes = [Scatter(self.keep, self.received, part) for part in range(2)]
+        return self.pipes
+
+    def done(self):
+        return jnp.concatenate([p.keep for p in self.pipes], axis=1)
 
 
 class SmallSum:
@@ -859,36 +916,59 @@
         bits, order = phases(False)
         self.bits = bits
         self.names = order[::-1]
-        self.keep = part
-        self.received = swap(part, bits[self.names.pop(0)])
+        self.keep, self.received = part, None
+        self.send = (part, bits[self.names.pop(0)])
 
     def step(self):
         self.keep = self.keep + self.received
         self.received = None
         self.send = (self.keep, self.bits[self.names.pop(0)]) if self.names else None
 
-    launch = Scatter.launch
-    done = Scatter.done
+    def launch(self):
+        self.received, self.send = swap(*self.send), None
+
+    def done(self):
+        return self.keep
 
 
 def advance(values, pipes):
-    pipes = [p for p in pipes if p.received is not None]
+    live = [p for p in pipes if p.received is not None]
+    fresh = [p for p in pipes if p.received is None and p.send is not None]
     size = len(values)
-    tied = tie(*values, *[p.received for p in pipes], *[p.keep for p in pipes])
-    for k, p in enumerate(pipes):
-        p.received, p.keep = tied[size + k], tied[size + len(pipes) + k]
-        p.step()
-    for p in pipes:
-        if isinstance(p, Scatter):
-            p.merge()
-    values = tied[:size]
-    pipes = [p for p in pipes if p.send is not None]
-    tied = tie(*values, *[p.send[0] for p in pipes], *[p.keep for p in pipes])
-    for k, p in enumerate(pipes):
-        p.send = (tied[size + k], p.send[1])
-        p.keep = tied[size + len(pipes) + k]
+    tied = list(
+        tie(
+            *values,
+            *[p.received for p in live],
+            *[p.keep for p in live],
+            *[p.send[0] for p in fresh],
+        )
+    )
+    values, tied = tied[:size], tied[size:]
+    for p in live:
+        p.received = tied.pop(0)
+    for p in live:
+        p.keep = tied.pop(0)
+    for p in fresh:
+        p.send = (tied.pop(0), p.send[1])
+    now = []
+    for p in live:
+        if isinstance(p, Pair):
+            now += p.split()
+        else:
+            p.step()
+            now.append(p)
+    now = [p for p in now + fresh if p.send is not None]
+    pipes[:] = now
+    held = [p for p in now if p.keep is not None]
+    tied = list(tie(*values, *[p.send[0] for p in now], *[p.keep for p in held]))
+    values, tied = tied[:size], tied[size:]
+    for p in now:
+        p.send = (tied.pop(0), p.send[1])
+    for p in held:
+        p.keep = tied.pop(0)
+    for p in now:
         p.launch()
-    return tied[:size]
+    return values
 
 
 def local(
@@ -976,7 +1056,7 @@
     onehot = (byte_ids.reshape(-1)[:, None] == symbols[None, :]).astype(jnp.bfloat16)
     embedded = matmul(onehot, table_full).reshape(tokens, model_width)
     stream_zero = embedded + context.reshape(tokens, model_width).astype(jnp.float32)
-    normed_one, norm_one_back = jax.vjp(rms_norm, stream_zero, gain_one.astype(jnp.float32))
+    normed_one = rms_norm(stream_zero, gain_one.astype(jnp.float32))
     normed_one_low = normed_one.astype(jnp.bfloat16)
     zgate = matmul(normed_one_low, zgate_full).reshape(row_count, length, -1)
     raw = matmul(normed_one_low, inputs_step_full).reshape(row_count, length, -1)
@@ -1003,7 +1083,7 @@
     mixed_full = unfold(outer_full, model_rows, mixed_start, fold_mixed, model_width)
     mixer_out = matmul(gate_low, mixed_full)
     stream_one = stream_zero + mixer_out
-    normed_two, norm_two_back = jax.vjp(rms_norm, stream_one, gain_two.astype(jnp.float32))
+    normed_two = rms_norm(stream_one, gain_two.astype(jnp.float32))
     normed_two_low = normed_two.astype(jnp.bfloat16)
     joined = matmul(normed_two_low, heads_full).astype(jnp.bfloat16)
     joined = joined.reshape(row_count, length, -1)
@@ -1029,77 +1109,88 @@
         ]
     )
     fold_width = fold_down * model_width
-    pipes = scatter_pair(
+    s_ffn = Pair(
         [normed_three_low, hidden_low],
         [gate_grad_low, upper_grad_low, ffn_grad_low],
         [
-            [(0, 0, 1, 0, hidden_width), (1, 2, fold_down, 0, fold_width // 2)],
-            [(0, 1, 1, 0, hidden_width), (1, 2, fold_down, fold_width // 2, fold_width)],
+            (0, 0, 1, 0, hidden_width),
+            (1, 2, fold_down, 0, fold_width // 2),
+            (0, 1, 1, 0, hidden_width),
+            (1, 2, fold_down, fold_width // 2, fold_width),
         ],
         model_rows,
     )
-    s_ffn = pipes[0]
+    pipes = [s_ffn]
+    (grad_normed_three,) = advance((grad_normed_three,), pipes)
+    s_ffn.own()
     stream_part, grad_norm_ffn = norm_three_back(grad_normed_three)
     grad_two = grad_three + stream_part
     attn_grad_low = grad_two.astype(jnp.bfloat16)
     attn_grad_low, grad_two = advance((attn_grad_low, grad_two), pipes)
-    grad_attended = (
-        matmul_right(attn_grad_low, attended_full)
-        .astype(jnp.bfloat16)
-        .reshape(row_count, length, model_width)
-    )
-    grad_joined = attention_backward(joined, grad_attended, ids, []).reshape(tokens, -1)
-    (grad_joined,) = advance((grad_joined,), pipes)
+    grad_joined = attention_backward(
+        joined,
+        attn_grad_low.reshape(row_count, length, model_width),
+        outer_full,
+        attended_start // model_width,
+        ids,
+    ).reshape(tokens, -1)
     heads_width = proj_heads.shape[1]
-    cut_heads = (heads_width + model_width) // 2
-    pair = scatter_pair(
-        [normed_two_low, attended_low],
-        [grad_joined, attn_grad_low],
+    grad_one, mixer_grad_low, grad_norm_attn = norm_backward(
         [
-            [(0, 0, 1, 0, cut_heads)],
-            [(0, 0, 1, cut_heads, heads_width), (1, 1, 1, 0, model_width)],
+            (grad_joined, q, outer_full, heads_start // model_width + q, model_width)
+            for q in range(3)
+        ],
+        stream_one,
+        gain_two.astype(jnp.float32).reshape(1, -1),
+        grad_two,
+    )
+    grad_norm_attn = grad_norm_attn.reshape(-1)
+    zgate_grad_low, heads_grad_low, grad_gated_gain, skip_lanes = gate_backward(
+        mixer_grad_low.reshape(row_count, length, model_width),
+        mixed_full,
+        zgate,
+        mixer_terms[-1],
+        values_low,
+        combined,
+    )
+    zgate_grad_low = zgate_grad_low.reshape(tokens, -1)
+    zgate_width = zgate_grad_low.shape[1]
+    s_middle = Pair(
+        [normed_two_low, attended_low, normed_one_low, gate_low],
+        [grad_joined, attn_grad_low, zgate_grad_low, mixer_grad_low],
+        [
+            (0, 0, 1, 0, heads_width),
+            (1, 1, 1, 0, model_width),
+            (2, 2, 1, 0, zgate_width),
+            (3, 3, fold_mixed, 0, fold_mixed * model_width),
         ],
         model_rows,
-    )
-    s_heads = pair[0]
-    pipes += pair
-    grad_normed_two = matmul_right(grad_joined, heads_full)
-    stream_part_two, grad_norm_attn = norm_two_back(grad_normed_two)
-    grad_one = grad_two + stream_part_two
-    mixer_grad_low = grad_one.astype(jnp.bfloat16)
-    mixer_grad_low, grad_one = advance((mixer_grad_low, grad_one), pipes)
-    grad_normed_gate = matmul_right(mixer_grad_low, mixed_full).reshape(row_count, length, -1)
-    zgate_grad_low, heads_grad_low, grad_gated_gain, skip_lanes = gate_backward(
-        grad_normed_gate, zgate, mixer_terms[-1], values_low, combined
-    )
-    zgate_grad_low = zgate_grad_low.reshape(tokens, -1)
-    pair = scatter_pair(
-        [normed_one_low, gate_low],
-        [zgate_grad_low, mixer_grad_low],
-        [
-            [(0, 0, 1, 0, zgate_grad_low.shape[1])],
-            [(1, 1, fold_mixed, 0, fold_mixed * model_width)],
-        ],
-        model_rows,
-    )
-    s_zgate = pair[0]
-    pipes += pair
-    zgate_grad_low, heads_grad_low = advance((zgate_grad_low, heads_grad_low), pipes)
+    ).own()
+    pipes += [s_middle]
+    heads_grad_low, grad_one = advance((heads_grad_low, grad_one), pipes)
     inputs_step_grad_low, grad_conv_kernel, grad_conv_bias, bias_lanes, decay_lanes = (
         mixer_backward(heads_grad_low, raw, *mixer_terms[:-1], values_low, states_low)
     )
     inputs_step_grad_low = inputs_step_grad_low.reshape(tokens, -1)
-    (inputs_step_grad_low,) = advance((inputs_step_grad_low,), pipes)
-    channels = inputs_step_grad_low.shape[1]
-    middle = (channels // 256) * 128
-    pair = scatter_pair(
+    inputs_step_grad_low, grad_one = advance((inputs_step_grad_low, grad_one), pipes)
+    s_inputs = Pair(
         [normed_one_low],
         [inputs_step_grad_low],
-        [[(0, 0, 1, 0, middle)], [(0, 0, 1, middle, channels)]],
+        [(0, 0, 1, 0, inputs_step_grad_low.shape[1])],
         model_rows,
-    )
-    s_inputs = pair[0]
-    pipes = pair + pipes
+    ).own()
+    grad_zero, embed_grad_low, grad_norm_mixer = norm_backward(
+        [
+            (zgate_grad_low, 0, zgate_full, 0, None),
+            (inputs_step_grad_low, 0, inputs_step_full, 0, None),
+        ],
+        stream_zero,
+        gain_one.astype(jnp.float32).reshape(1, -1),
+        grad_one,
+    )
+    grad_norm_mixer = grad_norm_mixer.reshape(-1)
+    embed_grad_low = embed_grad_low.reshape(-1, table_full.shape[1])
+    grad_byte_table = matmul_left(onehot, embed_grad_low)
     small_grads = [
         moments,
         bias_lanes[0, :HM],
@@ -1113,59 +1204,46 @@
     ]
     small_lengths = [v.shape[0] for v in small_grads]
     small_packed = jnp.concatenate(small_grads)
-    s_small = SmallSum(jnp.pad(small_packed, (0, -small_packed.shape[0] % 1024)).reshape(8, -1))
-    pipes += [s_small]
-    (inputs_step_grad_low,) = advance((inputs_step_grad_low,), pipes)
-    grad_normed_one = matmul_right(zgate_grad_low, zgate_full) + matmul_right(
-        inputs_step_grad_low, inputs_step_full
-    )
-    stream_part_one, grad_norm_mixer = norm_one_back(grad_normed_one)
-    grad_zero = grad_one + stream_part_one
-    embed_grad_low = grad_zero.reshape(-1, table_full.shape[1]).astype(jnp.bfloat16)
-    grad_byte_table = matmul_left(onehot, embed_grad_low)
-    late = jnp.concatenate(
-        [
-            grad_byte_table.reshape(-1, byte_table.size),
-            grad_norm_mixer.reshape(-1, model_rows),
-        ],
-        axis=1,
-    )
-    late = jnp.pad(late, ((0, 0), (0, -late.shape[1] % 128)))
-    s_late = SmallScatter(late)
-    pipes = pipes[:2] + [s_late] + pipes[2:]
-    while any(p.received is not None for p in pipes):
+    small_packed = jnp.pad(small_packed, (0, -small_packed.shape[0] % 1024)).reshape(-1, 128)
+    table_rows = grad_byte_table.shape[0]
+    s_small = SmallSum(
+        jnp.concatenate([grad_byte_table, grad_norm_mixer.reshape(-1, 128), small_packed], axis=0)
+    )
+    pipes = [s_inputs, s_small] + pipes
+    while pipes:
         advance((), pipes)
-    late = s_late.done().reshape(-1)
     grad_inputs_step = s_inputs.done()
-    zgate_mixed = s_zgate.done()
-    attention_sums = s_heads.done()
+    middle_sums = s_middle.done()
+    attention_sums = middle_sums[:, : heads_width + model_width]
+    zgate_mixed = middle_sums[:, heads_width + model_width :]
     ffn_sums = s_ffn.done()
     half_fold = fold_width // 2
     second = hidden_width + half_fold
     down_sums = [ffn_sums[:, hidden_width:second], ffn_sums[:, second + hidden_width :]]
-    zgate_width = zgate_grad_low.shape[1]
 
     def stacked(v):
         return jnp.concatenate(
             [v[:, q : q + model_width] for q in range(0, v.shape[1], model_width)], axis=0
         )
 
-    table_sum = late[: byte_table.size].reshape(byte_table.shape)
-    norm_mixer_sum = late[byte_table.size : byte_table.size + model_rows]
-    small_sums = s_small.done().reshape(-1)
+    def own_part(total, share):
+        length = share.shape[-1]
+        return lax.dynamic_slice_in_dim(total, own_index() * length, length, total.ndim - 1)
+
+    small_sums = s_small.done()
+    table_sum = lax.dynamic_slice_in_dim(
+        small_sums, own_index() * byte_table.shape[0], byte_table.shape[0], 0
+    )
+    small_sums = small_sums[table_rows:].reshape(-1)
+    norm_mixer_sum = own_part(small_sums[: grad_norm_mixer.shape[0]], norm_mixer)
     sums = []
-    start = 0
+    start = grad_norm_mixer.shape[0]
     for count in small_lengths:
         sums.append(small_sums[start : start + count])
         start += count
     totals, bias_total, decay_total, skip_total = sums[:4]
     kernel_sum = sums[4].reshape(taps, -1)
     offset_sum, gated_sum, norm_attn_sum, norm_ffn_sum = sums[5:]
-
-    def own_part(total, share):
-        length = share.shape[-1]
-        return lax.dynamic_slice_in_dim(total, own_index() * length, length, total.ndim - 1)
-
     rms_stats = jnp.sqrt(totals[:4] / (totals[4] * model_width))
     return (
         stream_three.reshape(row_count, length, model_width),

time: 763 us -> 690 us (0.904)
  Pallas kernels: 154 us -> 241 us
  other arithmetic: 77.1 us -> 19.4 us
  waiting for transfers between devices: 305 us -> 253 us
  local copies, waits for them, and re-layouts: 92.2 us -> 70.5 us
  matrix products: 48.5 us -> 27.3 us
    pallas_call x1 -> x27, Pallas kernels: 6.83 us -> 89.9 us  [the longest x24 62.1 us: add_halves(): pl.pallas_call(add_halves_kernel, grid_spec=pltpu.PrefetchScalarGridSpec(...]
    convert_element_type x38 -> x0, other arithmetic: 58 us -> none  [the longest x36 54.8 us: half(): return (former + latter).astype(jnp.bfloat16)]
    ppermute x59 -> x49, waiting for transfers between devices: 252 us -> 203 us  [swap(): return lax.ppermute(v, name, [(i, i ^ step) for i in range(size)])]
    dynamic_slice x16 -> x0, local copies, waits for them, and re-layouts: 27.2 us -> none  [half(): lax.dynamic_index_in_dim(v, which, axis, keepdims=False).astype(jnp.float32)]
    dot_general x5 -> x0, matrix products: 20.9 us -> none  [matmul_right(): lax.dot_general(former, latter, (((1,), (1,)), ((), ())), preferred_eleme...]
    ppermute x59 -> x49, starting transfers between devices: 60.2 us -> 53.2 us  [swap(): return lax.ppermute(v, name, [(i, i ^ step) for i in range(size)])]
    pallas_call x8 -> x6, Pallas kernels: 48.3 us -> 49.5 us  [part_grads(): pl.pallas_call(partial(grads_kernel, plan, rows, (len(formers), len(latte...]
    unnamed x241 -> x206, local copies, waits for them, and re-layouts: 34.6 us -> 35.3 us
  transfers between devices with their start and end apart: 60 -> 50, of which waited for: 31 -> 34; matrix products, arithmetic and copies ran while one was open for 11% -> 9% of each run, Pallas kernels for 12% -> 20%
where the time goes in v3:
time: 690 us; the launch traced here: 681 us
  waiting for transfers between devices  253 us (37%)
  Pallas kernels  241 us (35%)
  local copies, waits for them, and re-layouts  70.5 us (10%)
  starting transfers between devices  53.2 us (8%)
  matrix products  27.3 us (4%)
  other arithmetic  19.4 us (3%)
  between operations  16.2 us (2%)
    ppermute x49, waiting for transfers between devices, swap(): return lax.ppermute(v, name, [(i, i ^ step) for i in range(size)])  203 us
    pallas_call x24, Pallas kernels, add_halves(): pl.pallas_call(add_halves_kernel, grid_spec=pltpu.PrefetchScalarGridSpec(...  62.1 us
    ppermute x49, starting transfers between devices, swap(): return lax.ppermute(v, name, [(i, i ^ step) for i in range(size)])  53.2 us
    all_gather x1, waiting for transfers between devices, local(): outer_full = lax.all_gather(outer_shard, AXES, axis=0, tiled=True)  49.6 us
    pallas_call x6, Pallas kernels, part_grads(): pl.pallas_call(partial(grads_kernel, plan, rows, (len(formers), len(latte...  49.5 us
    unnamed x206, local copies, waits for them, and re-layouts  35.3 us
    pallas_call x1, Pallas kernels, feed_forward(): pl.pallas_call(partial(ffn_kernel, rows, fold), grid=(steps,), in_specs=[...  27 us
    pallas_call x1, Pallas kernels, mixer_backward(): pl.pallas_call(mixer_backward_kernel, grid=(count,), in_specs=[row(DI), r...  24.9 us
  transfers between devices with their start and end apart: 50, of which 34 were waited for; matrix products, arithmetic and copies ran while one was open for 9% of the time, Pallas kernels for 20%

profile of v3, /device:TPU:0, one launch (start us, length us, event | category | flops | bytes accessed | tf_op | source)
XLA Modules:
  0.0 680.8 jit_solution(16947873962138791559)
XLA Ops:
  43.3 23.9 %collective-permute-done.6 = bf16[1,32,2048]{2,1,0:T(8,128)(2,1)S(1)} collective-permute-done((bf16[1,32,2048]{2,1,0:T(8,128)(2,1)S(1)}, bf16[1,32,2048]{2,1,0:T(8,128)(2,1)S(1)}, u32[]{:S(2)}, u32[]{:S(2)}) %collective-permute-start.6) | collective-permute-done | bytes 131104 | tf_op jit(solution)/shard_map/ppermute | solution.py:614
  69.4 28.9 %collective-permute-done.8 = bf16[2,32,2048]{2,1,0:T(8,128)(2,1)S(1)} collective-permute-done((bf16[2,32,2048]{2,1,0:T(8,128)(2,1)S(1)}, bf16[2,32,2048]{2,1,0:T(8,128)(2,1)S(1)}, u32[]{:S(2)}, u32[]{:S(2)}) %collective-permute-start.8) | collective-permute-done | bytes 262176 | tf_op jit(solution)/shard_map/ppermute | solution.py:614
  101.5 11.8 %collective-permute-done.10 = bf16[4,32,2048]{2,1,0:T(8,128)(2,1)S(1)} collective-permute-done((bf16[4,32,2048]{2,1,0:T(8,128)(2,1)S(1)}, bf16[4,32,2048]{2,1,0:T(8,128)(2,1)S(1)}, u32[]{:S(2)}, u32[]{:S(2)}) %collective-permute-start.10) | collective-permute-done | bytes 524320 | tf_op jit(solution)/shard_map/ppermute | solution.py:614
  113.3 12.7 %collective-permute-done.9 = bf16[4,32,2432]{2,1,0:T(8,128)(2,1)S(1)} collective-permute-done((bf16[4,32,2432]{2,1,0:T(8,128)(2,1)S(1)}, bf16[4,32,2432]{2,1,0:T(8,128)(2,1)S(1)}, u32[]{:S(2)}, u32[]{:S(2)}) %collective-permute-start.9) | collective-permute-done | bytes 622624 | tf_op jit(solution)/shard_map/ppermute | solution.py:614
  137.7 14.7 %collective-permute-done.12.refs_1_ = bf16[8,32,2048]{2,1,0:T(8,128)(2,1)} collective-permute-done((bf16[8,32,2048]{2,1,0:T(8,128)(2,1)S(1)}, bf16[8,32,2048]{2,1,0:T(8,128)(2,1)}, u32[]{:S(2)}, u32[]{:S(2)}) %collective-permute-start.12) | collective-permute-done | bytes 1048608 | tf_op jit(solution)/shard_map/ppermute | solution.py:614
  196.2 14.8 %shard_map.392 = (bf16[2,208,2048]{2,1,0:T(8,128)(2,1)S(1)}, bf16[2,208,256]{2,1,0:T(8,128)(2,1)S(1)}, f32[2,208,2048]{2,1,0:T(8,128)}, bf16[2,208,2048]{2,1,0:T(8,128)(2,1)S(1)}) custom-call(f32[2,208,2432]{2,1,0:T(8,128)} %fusion.30.raw_ref, f32[2,208,2048]{2,1,0:T(8,128)} %fusion.31.zgate_ref, f32[2,208,1]{2,1,0:T(8,128)S(1)} %copy.55.ids_column_ref, ...), custom_call_target="tpu_custom_call" | custom-call | flops 1024 | bytes 1024 | tf_op jit(solution)/shard_map/pallas_call | solution.py:324
  213.4 49.6 %all-gather.2.cloned.1.call-done.gate_ref.upper_ref.folded_ref.weight_ref.refs_3_.refs_4_.refs_5_ = bf16[1024,18432]{1,0:T(8,128)(2,1)} async-done(((bf16[32,18432]{1,0:T(8,128)(2,1)}), bf16[1024,18432]{1,0:T(8,128)(2,1)}) %all-gather.2.cloned.1.call-update) | async-done | bytes 37748752 | tf_op jit(solution)/shard_map/all_gather | solution.py:1045
  283.9 27.0 %shard_map.395 = (bf16[416,4096]{1,0:T(8,128)(2,1)}, bf16[416,4096]{1,0:T(8,128)(2,1)}, bf16[416,4096]{1,0:T(8,128)(2,1)}, f32[416,1024]{1,0:T(8,128)S(1)}, f32[416,1024]{1,0:T(8,128)S(1)}) custom-call(bf16[416,1024]{1,0:T(8,128)(2,1)S(1)} %multiply_convert_fusion.1.source_ref.refs_0_, bf16[416,1024]{1,0:T(8,128)(2,1)S(1)} %bitcast.159, ...), custom_call_target="tpu_custom_call" | custom-call | flops 1024 | bytes 1024 | tf_op jit(solution)/shard_map/pallas_call | solution.py:571
  312.9 12.4 %shard_map.396 = bf16[512,12288]{1,0:T(8,128)(2,1)} custom-call(s32[1]{0:T(128)} %bitcast.20.core_ref, bf16[416,1024]{1,0:T(8,128)(2,1)S(1)} %multiply_convert_fusion.1.source_ref.refs_0_, bf16[416,4096]{1,0:T(8,128)(2,1)S(1)} %copy-done.8, bf16[416,4096]{1,0:T(8,128)(2,1)} %get-tuple-element.293.refs_2_, bf16[416,4096]{1,0:T(8,128)(2,1)} %get-tuple-element.294.refs_3_, ...), custom_call_target="tpu_custom_call" | custom-call | flops 1024 | bytes 1024 | tf_op jit(solution)/shard_map/pallas_call | solution.py:814
  325.5 12.3 %shard_map.397 = bf16[512,12288]{1,0:T(8,128)(2,1)} custom-call(s32[1]{0:T(128)} %bitcast.21.core_ref, bf16[416,1024]{1,0:T(8,128)(2,1)S(1)} %multiply_convert_fusion.1.source_ref.refs_0_, bf16[416,4096]{1,0:T(8,128)(2,1)S(1)} %copy-done.8, bf16[416,4096]{1,0:T(8,128)(2,1)} %get-tuple-element.293.refs_2_, bf16[416,4096]{1,0:T(8,128)(2,1)} %get-tuple-element.294.refs_3_, ...), custom_call_target="tpu_custom_call" | custom-call | flops 1024 | bytes 1024 | tf_op jit(solution)/shard_map/pallas_call | solution.py:814
  344.7 7.6 %shard_map.398 = (bf16[4,64,6144]{2,1,0:T(8,128)(2,1)}, bf16[4,64,6144]{2,1,0:T(8,128)(2,1)}) custom-call(s32[1]{0:T(128)} %bitcast.22.mine_ref, bf16[4,2,64,12288]{3,2,1,0:T(8,128)(2,1)} %bitcast.225, bf16[4,2,64,12288]{3,2,1,0:T(8,128)(2,1)} %bitcast.24.give_more.hold_more, bf16[4,2,64,12288]{3,2,1,0:T(8,128)(2,1)} %bitcast.226, ...), custom_call_target="tpu_custom_call" | custom-call | flops 1024 | bytes 1024 | tf_op jit(solution)/shard_map/pallas_call | solution.py:847
  352.3 7.6 %shard_map.399 = (bf16[8,32,6144]{2,1,0:T(8,128)(2,1)}, bf16[8,32,6144]{2,1,0:T(8,128)(2,1)}) custom-call(s32[1]{0:T(128)} %bitcast.25.mine_ref, bf16[8,2,32,12288]{3,2,1,0:T(8,128)(2,1)} %bitcast.227, bf16[8,2,32,12288]{3,2,1,0:T(8,128)(2,1)} %bitcast.27.give_more.hold_more, bf16[8,2,32,12288]{3,2,1,0:T(8,128)(2,1)} %bitcast.228, ...), custom_call_target="tpu_custom_call" | custom-call | flops 1024 | bytes 1024 | tf_op jit(solution)/shard_map/pallas_call | solution.py:847
  365.9 20.9 %shard_map.400 = bf16[2,208,3072]{2,1,0:T(8,128)(2,1)S(1)} custom-call(bf16[2,208,3072]{2,1,0:T(8,128)(2,1)S(1)} %bitcast.164, bf16[2,208,1024]{2,1,0:T(8,128)(2,1)S(1)} %bitcast.162, bf16[1024,18432]{1,0:T(8,128)(2,1)} %all-gather.2.cloned.1.call-done.gate_ref.upper_ref.folded_ref.weight_ref.refs_3_.refs_4_.refs_5_, f32[2,208,1]{2,1,0:T(8,128)S(1)} %copy-done.32, ...), custom_call_target="tpu_custom_call" | custom-call | flops 1024 | bytes 1024 | tf_op jit(solution)/shard_map/pallas_call | solution.py:468
  388.4 7.4 %shard_map.401 = (f32[416,1024]{1,0:T(8,128)S(1)}, bf16[416,1024]{1,0:T(8,128)(2,1)S(1)}, f32[1,1024]{1,0:T(1,128)S(1)}) custom-call(bf16[416,3072]{1,0:T(8,128)(2,1)} %bitcast.135, bf16[416,3072]{1,0:T(8,128)(2,1)} %bitcast.136, bf16[416,3072]{1,0:T(8,128)(2,1)} %bitcast.137, ...), custom_call_target="tpu_custom_call" | custom-call | flops 1024 | bytes 1024 | tf_op jit(solution)/shard_map/pallas_call | solution.py:509
  397.0 10.9 %shard_map.402 = (bf16[2,208,2048]{2,1,0:T(8,128)(2,1)S(1)}, bf16[2,208,2048]{2,1,0:T(8,128)(2,1)S(1)}, f32[1,2048]{1,0:T(1,128)S(1)}, f32[1,2048]{1,0:T(1,128)S(1)}) custom-call(bf16[2,208,1024]{2,1,0:T(8,128)(2,1)S(1)} %bitcast.169, bf16[2048,1024]{1,0:T(8,128)(2,1)} %bitcast.153, f32[2,208,2048]{2,1,0:T(8,128)} %fusion.31.zgate_ref, ...), custom_call_target="tpu_custom_call" | custom-call | flops 1024 | bytes 1024 | tf_op jit(solution)/shard_map/pallas_call | solution.py:348
  409.1 9.7 %shard_map.403 = bf16[512,8192]{1,0:T(8,128)(2,1)} custom-call(s32[1]{0:T(128)} %bitcast.20.core_ref, bf16[416,1024]{1,0:T(8,128)(2,1)S(1)} %copy-done.19, bf16[416,1024]{1,0:T(8,128)(2,1)S(1)} %bitcast.145, bf16[416,1024]{1,0:T(8,128)(2,1)S(1)} %get-tuple-element.511.refs_2_.refs_0_, bf16[416,2048]{1,0:T(8,128)(2,1)S(1)} %bitcast.171, ...), custom_call_target="tpu_custom_call" | custom-call | flops 1024 | bytes 1024 | tf_op jit(solution)/shard_map/pallas_call | solution.py:814
  418.8 9.3 %shard_map.406 = bf16[512,8192]{1,0:T(8,128)(2,1)} custom-call(s32[1]{0:T(128)} %bitcast.21.core_ref, bf16[416,1024]{1,0:T(8,128)(2,1)S(1)} %copy-done.19, bf16[416,1024]{1,0:T(8,128)(2,1)S(1)} %bitcast.146, bf16[416,1024]{1,0:T(8,128)(2,1)S(1)} %get-tuple-element.511.refs_2_.refs_0_, bf16[416,2048]{1,0:T(8,128)(2,1)S(1)} %bitcast.172, ...), custom_call_target="tpu_custom_call" | custom-call | flops 1024 | bytes 1024 | tf_op jit(solution)/shard_map/pallas_call | solution.py:814
  442.4 24.9 %shard_map.407 = (bf16[2,208,2560]{2,1,0:T(8,128)(2,1)S(1)}, f32[4,2304]{1,0:T(4,128)S(1)}, f32[1,2304]{1,0:T(1,128)S(1)}, f32[1,128]{1,0:T(1,128)S(1)}, f32[1,128]{1,0:T(1,128)S(1)}) custom-call(bf16[2,208,2048]{2,1,0:T(8,128)(2,1)S(1)} %copy-done.45, f32[2,208,2432]{2,1,0:T(8,128)} %fusion.30.raw_ref, f32[2,208,1]{2,1,0:T(8,128)S(1)} %copy-done.33, ...), custom_call_target="tpu_custom_call" | custom-call | flops 1024 | bytes 1024 | tf_op jit(solution)/shard_map/pallas_call | solution.py:372
  467.3 9.8 %collective-permute-done.20 = bf16[4,32,6144]{2,1,0:T(8,128)(2,1)S(1)} collective-permute-done((bf16[4,32,6144]{2,1,0:T(8,128)(2,1)S(1)}, bf16[4,32,6144]{2,1,0:T(8,128)(2,1)S(1)}, u32[]{:S(2)}, u32[]{:S(2)}) %collective-permute-start.20) | collective-permute-done | bytes 1572896 | tf_op jit(solution)/shard_map/ppermute | solution.py:614
  512.0 9.6 %shard_map.412 = (f32[416,1024]{1,0:T(8,128)}, bf16[416,1024]{1,0:T(8,128)(2,1)S(1)}, f32[1,1024]{1,0:T(1,128)S(1)}) custom-call(bf16[416,2048]{1,0:T(8,128)(2,1)S(1)} %bitcast.158, bf16[416,2560]{1,0:T(8,128)(2,1)} %bitcast.150, bf16[1024,2048]{1,0:T(8,128)(2,1)} %bitcast.155, bf16[1024,2432]{1,0:T(8,128)(2,1)} %bitcast.148, f32[416,1024]{1,0:T(8,128)S(1)} %copy-done.21, ...), custom_call_target="tpu_custom_call" | custom-call | flops 1024 | bytes 1024 | tf_op jit(solution)/shard_map/pallas_call | solution.py:509
  527.5 7.1 %collective-permute-done.23 = bf16[2,32,6144]{2,1,0:T(8,128)(2,1)} collective-permute-done((bf16[2,32,6144]{2,1,0:T(8,128)(2,1)}, bf16[2,32,6144]{2,1,0:T(8,128)(2,1)}, u32[]{:S(2)}, u32[]{:S(2)}) %collective-permute-start.23) | collective-permute-done | bytes 786464 | tf_op jit(solution)/shard_map/ppermute | solution.py:614
  565.4 17.0 %collective-permute-done.27 = bf16[1,32,6144]{2,1,0:T(8,128)(2,1)} collective-permute-done((bf16[1,32,6144]{2,1,0:T(8,128)(2,1)}, bf16[1,32,6144]{2,1,0:T(8,128)(2,1)}, u32[]{:S(2)}, u32[]{:S(2)}) %collective-permute-start.27) | collective-permute-done | bytes 393248 | tf_op jit(solution)/shard_map/ppermute | solution.py:614
  604.2 14.5 %collective-permute-done.37 = f32[392,128]{1,0:T(8,128)S(1)} collective-permute-done((f32[392,128]{1,0:T(8,128)S(1)}, f32[392,128]{1,0:T(8,128)S(1)}, u32[]{:S(2)}, u32[]{:S(2)}) %collective-permute-start.37) | collective-permute-done | bytes 200736 | tf_op jit(solution)/shard_map/ppermute | solution.py:614
  657.3 7.5 %collective-permute-done.46 = bf16[1,32,1280]{2,1,0:T(8,128)(2,1)S(1)} collective-permute-done((bf16[1,32,1280]{2,1,0:T(8,128)(2,1)S(1)}, bf16[1,32,1280]{2,1,0:T(8,128)(2,1)S(1)}, u32[]{:S(2)}, u32[]{:S(2)}) %collective-permute-start.46) | collective-permute-done | bytes 81952 | tf_op jit(solution)/shard_map/ppermute | solution.py:614
  (450 shorter events, 292.9 us)
Async XLA Ops:
  7.3 255.7 %all-gather.2.cloned.1.call-start = ((), (), s32[]{:S(2)}) async-start(), calls=%async_computation | async-start | bytes 38928384 | tf_op jit(solution)/shard_map/all_gather | solution.py:1045
  31.9 35.2 %collective-permute-start.5 = (bf16[1,32,2432]{2,1,0:T(8,128)(2,1)S(1)}, bf16[1,32,2432]{2,1,0:T(8,128)(2,1)S(1)}, u32[]{:S(2)}, u32[]{:S(2)}) collective-permute-start(bf16[1,32,2432]{2,1,0:T(8,128)(2,1)S(1)} %fusion.18), channel_id=1, source_target_pairs={{0,16},{4,20},{8,24},{12,28},{16,0},{20,4},{24,8},{28,12},{1,17},{... | collective-permute-start | bytes 466952 | tf_op jit(solution)/shard_map/ppermute | solution.py:614
  32.1 35.1 %collective-permute-start.6 = (bf16[1,32,2048]{2,1,0:T(8,128)(2,1)S(1)}, bf16[1,32,2048]{2,1,0:T(8,128)(2,1)S(1)}, u32[]{:S(2)}, u32[]{:S(2)}) collective-permute-start(bf16[1,32,2048]{2,1,0:T(8,128)(2,1)S(1)} %bitcast.245), channel_id=1, source_target_pairs={{0,16},{4,20},{8,24},{12,28},{16,0},{20,4},{24,8},{28,12},{1,17},{... | collective-permute-start | bytes 393224 | tf_op jit(solution)/shard_map/ppermute | solution.py:614
  67.2 31.1 %collective-permute-start.7 = (bf16[2,32,2432]{2,1,0:T(8,128)(2,1)S(1)}, bf16[2,32,2432]{2,1,0:T(8,128)(2,1)S(1)}, u32[]{:S(2)}, u32[]{:S(2)}) collective-permute-start(bf16[2,32,2432]{2,1,0:T(8,128)(2,1)S(1)} %constant_dynamic-update-slice_fusion), channel_id=1, source_target_pairs={{0,8},{4,12},{8,0},{12,4},{16,24},{20,28},{24,16},{28,20},{1,9},{5... | collective-permute-start | bytes 933896 | tf_op jit(solution)/shard_map/ppermute | solution.py:614
  67.3 31.0 %collective-permute-start.8 = (bf16[2,32,2048]{2,1,0:T(8,128)(2,1)S(1)}, bf16[2,32,2048]{2,1,0:T(8,128)(2,1)S(1)}, u32[]{:S(2)}, u32[]{:S(2)}) collective-permute-start(bf16[2,32,2048]{2,1,0:T(8,128)(2,1)S(1)} %constant_dynamic-update-slice_fusion.2), channel_id=1, source_target_pairs={{0,8},{4,12},{8,0},{12,4},{16,24},{20,28},{24,16},{28,20},{1,9},{5... | collective-permute-start | bytes 786440 | tf_op jit(solution)/shard_map/ppermute | solution.py:614
  98.4 27.6 %collective-permute-start.9 = (bf16[4,32,2432]{2,1,0:T(8,128)(2,1)S(1)}, bf16[4,32,2432]{2,1,0:T(8,128)(2,1)S(1)}, u32[]{:S(2)}, u32[]{:S(2)}) collective-permute-start(bf16[4,32,2432]{2,1,0:T(8,128)(2,1)S(1)} %constant_dynamic-update-slice_fusion.4), channel_id=1, source_target_pairs={{0,1},{1,0},{2,3},{3,2},{4,5},{5,4},{6,7},{7,6},{8,9},{9,8},{10,11... | collective-permute-start | bytes 1867784 | tf_op jit(solution)/shard_map/ppermute | solution.py:614
  126.1 31.5 %collective-permute-start.11 = (bf16[8,32,2432]{2,1,0:T(8,128)(2,1)S(1)}, bf16[8,32,2432]{2,1,0:T(8,128)(2,1)}, u32[]{:S(2)}, u32[]{:S(2)}) collective-permute-start(bf16[8,32,2432]{2,1,0:T(8,128)(2,1)S(1)} %constant_dynamic-update-slice_fusion.8.refs_0_), channel_id=1, source_target_pairs={{0,2},{1,3},{2,0},{3,1},{4,6},{5,7},{6,4},{7,5},{8,10},{9,11},{10,... | collective-permute-start | bytes 3735560 | tf_op jit(solution)/shard_map/ppermute | solution.py:614
  127.7 24.6 %collective-permute-start.12 = (bf16[8,32,2048]{2,1,0:T(8,128)(2,1)S(1)}, bf16[8,32,2048]{2,1,0:T(8,128)(2,1)}, u32[]{:S(2)}, u32[]{:S(2)}) collective-permute-start(bf16[8,32,2048]{2,1,0:T(8,128)(2,1)S(1)} %constant_dynamic-update-slice_fusion.10.refs_0_), channel_id=1, source_target_pairs={{0,1},{1,0},{2,3},{3,2},{4,5},{5,4},{6,7},{7,6},{8,9},{9,8},{10,11... | collective-permute-start | bytes 3145736 | tf_op jit(solution)/shard_map/ppermute | solution.py:614
  360.0 70.6 %collective-permute-start.18 = (bf16[4,64,6144]{2,1,0:T(8,128)(2,1)}, bf16[4,64,6144]{2,1,0:T(8,128)(2,1)}, u32[]{:S(2)}, u32[]{:S(2)}) collective-permute-start(bf16[4,64,6144]{2,1,0:T(8,128)(2,1)} %get-tuple-element.313), channel_id=1, source_target_pairs={{0,2},{1,3},{2,0},{3,1},{4,6},{5,7},{6,4},{7,5},{8,10},{9,11},{10,... | collective-permute-start | bytes 9437192 | tf_op jit(solution)/shard_map/ppermute | solution.py:614
  361.5 70.3 %collective-permute-start.19 = (bf16[8,32,6144]{2,1,0:T(8,128)(2,1)}, bf16[8,32,6144]{2,1,0:T(8,128)(2,1)}, u32[]{:S(2)}, u32[]{:S(2)}) collective-permute-start(bf16[8,32,6144]{2,1,0:T(8,128)(2,1)} %get-tuple-element.314), channel_id=1, source_target_pairs={{0,1},{1,0},{2,3},{3,2},{4,5},{5,4},{6,7},{7,6},{8,9},{9,8},{10,11... | collective-permute-start | bytes 9437192 | tf_op jit(solution)/shard_map/ppermute | solution.py:614
  440.3 37.3 %collective-permute-start.22 = (bf16[512,8192]{1,0:T(8,128)(2,1)}, bf16[512,8192]{1,0:T(8,128)(2,1)}, u32[]{:S(2)}, u32[]{:S(2)}) collective-permute-start(bf16[512,8192]{1,0:T(8,128)(2,1)} %shard_map.403), channel_id=1, source_target_pairs={{0,4},{4,0},{8,12},{12,8},{16,20},{20,16},{24,28},{28,24},{1,5},{5... | collective-permute-start | bytes 25165832 | tf_op jit(solution)/shard_map/ppermute | solution.py:614
  440.3 36.8 %collective-permute-start.20 = (bf16[4,32,6144]{2,1,0:T(8,128)(2,1)S(1)}, bf16[4,32,6144]{2,1,0:T(8,128)(2,1)S(1)}, u32[]{:S(2)}, u32[]{:S(2)}) collective-permute-start(bf16[4,32,6144]{2,1,0:T(8,128)(2,1)S(1)} %get-tuple-element.332), channel_id=1, source_target_pairs={{0,1},{1,0},{2,3},{3,2},{4,5},{5,4},{6,7},{7,6},{8,9},{9,8},{10,11... | collective-permute-start | bytes 4718600 | tf_op jit(solution)/shard_map/ppermute | solution.py:614
  440.9 36.7 %collective-permute-start.21 = (bf16[4,32,6144]{2,1,0:T(8,128)(2,1)}, bf16[4,32,6144]{2,1,0:T(8,128)(2,1)S(1)}, u32[]{:S(2)}, u32[]{:S(2)}) collective-permute-start(bf16[4,32,6144]{2,1,0:T(8,128)(2,1)} %get-tuple-element.333), channel_id=1, source_target_pairs={{0,2},{1,3},{2,0},{3,1},{4,6},{5,7},{6,4},{7,5},{8,10},{9,11},{10,... | collective-permute-start | bytes 4718600 | tf_op jit(solution)/shard_map/ppermute | solution.py:614
  494.8 47.6 %collective-permute-start.25 = (bf16[4,64,4096]{2,1,0:T(8,128)(2,1)}, bf16[4,64,4096]{2,1,0:T(8,128)(2,1)}, u32[]{:S(2)}, u32[]{:S(2)}) collective-permute-start(bf16[4,64,4096]{2,1,0:T(8,128)(2,1)} %get-tuple-element.359), channel_id=1, source_target_pairs={{0,2},{1,3},{2,0},{3,1},{4,6},{5,7},{6,4},{7,5},{8,10},{9,11},{10,... | collective-permute-start | bytes 6291464 | tf_op jit(solution)/shard_map/ppermute | solution.py:614
  496.3 47.0 %collective-permute-start.26 = (bf16[8,32,4096]{2,1,0:T(8,128)(2,1)}, bf16[8,32,4096]{2,1,0:T(8,128)(2,1)}, u32[]{:S(2)}, u32[]{:S(2)}) collective-permute-start(bf16[8,32,4096]{2,1,0:T(8,128)(2,1)} %get-tuple-element.360), channel_id=1, source_target_pairs={{0,1},{1,0},{2,3},{3,2},{4,5},{5,4},{6,7},{7,6},{8,9},{9,8},{10,11... | collective-permute-start | bytes 6291464 | tf_op jit(solution)/shard_map/ppermute | solution.py:614
  499.0 35.6 %collective-permute-start.23 = (bf16[2,32,6144]{2,1,0:T(8,128)(2,1)}, bf16[2,32,6144]{2,1,0:T(8,128)(2,1)}, u32[]{:S(2)}, u32[]{:S(2)}) collective-permute-start(bf16[2,32,6144]{2,1,0:T(8,128)(2,1)} %copy-done.59), channel_id=1, source_target_pairs={{0,8},{4,12},{8,0},{12,4},{16,24},{20,28},{24,16},{28,20},{1,9},{5... | collective-permute-start | bytes 2359304 | tf_op jit(solution)/shard_map/ppermute | solution.py:614
  499.9 36.1 %collective-permute-start.24 = (bf16[1,64,6144]{2,1,0:T(8,128)(2,1)}, bf16[1,64,6144]{2,1,0:T(8,128)(2,1)}, u32[]{:S(2)}, u32[]{:S(2)}) collective-permute-start(bf16[1,64,6144]{2,1,0:T(8,128)(2,1)} %copy-done.60), channel_id=1, source_target_pairs={{0,16},{4,20},{8,24},{12,28},{16,0},{20,4},{24,8},{28,12},{1,17},{... | collective-permute-start | bytes 2359304 | tf_op jit(solution)/shard_map/ppermute | solution.py:614
  559.2 26.6 %collective-permute-start.31 = (bf16[512,2560]{1,0:T(8,128)(2,1)}, bf16[512,2560]{1,0:T(8,128)(2,1)}, u32[]{:S(2)}, u32[]{:S(2)}) collective-permute-start(bf16[512,2560]{1,0:T(8,128)(2,1)} %shard_map.413), channel_id=1, source_target_pairs={{0,4},{4,0},{8,12},{12,8},{16,20},{20,16},{24,28},{28,24},{1,5},{5... | collective-permute-start | bytes 7864328 | tf_op jit(solution)/shard_map/ppermute | solution.py:614
  559.2 25.9 %collective-permute-start.29 = (bf16[4,32,4096]{2,1,0:T(8,128)(2,1)}, bf16[4,32,4096]{2,1,0:T(8,128)(2,1)}, u32[]{:S(2)}, u32[]{:S(2)}) collective-permute-start(bf16[4,32,4096]{2,1,0:T(8,128)(2,1)} %get-tuple-element.394), channel_id=1, source_target_pairs={{0,1},{1,0},{2,3},{3,2},{4,5},{5,4},{6,7},{7,6},{8,9},{9,8},{10,11... | collective-permute-start | bytes 3145736 | tf_op jit(solution)/shard_map/ppermute | solution.py:614
  560.1 25.6 %collective-permute-start.30 = (bf16[4,32,4096]{2,1,0:T(8,128)(2,1)}, bf16[4,32,4096]{2,1,0:T(8,128)(2,1)}, u32[]{:S(2)}, u32[]{:S(2)}) collective-permute-start(bf16[4,32,4096]{2,1,0:T(8,128)(2,1)} %get-tuple-element.395), channel_id=1, source_target_pairs={{0,2},{1,3},{2,0},{3,1},{4,6},{5,7},{6,4},{7,5},{8,10},{9,11},{10,... | collective-permute-start | bytes 3145736 | tf_op jit(solution)/shard_map/ppermute | solution.py:614
  597.0 24.3 %collective-permute-start.33 = (bf16[2,32,4096]{2,1,0:T(8,128)(2,1)S(1)}, bf16[2,32,4096]{2,1,0:T(8,128)(2,1)S(1)}, u32[]{:S(2)}, u32[]{:S(2)}) collective-permute-start(bf16[2,32,4096]{2,1,0:T(8,128)(2,1)S(1)} %get-tuple-element.420), channel_id=1, source_target_pairs={{0,8},{4,12},{8,0},{12,4},{16,24},{20,28},{24,16},{28,20},{1,9},{5... | collective-permute-start | bytes 1572872 | tf_op jit(solution)/shard_map/ppermute | solution.py:614
  597.6 25.1 %collective-permute-start.34 = (bf16[1,64,4096]{2,1,0:T(8,128)(2,1)S(1)}, bf16[1,64,4096]{2,1,0:T(8,128)(2,1)S(1)}, u32[]{:S(2)}, u32[]{:S(2)}) collective-permute-start(bf16[1,64,4096]{2,1,0:T(8,128)(2,1)S(1)} %get-tuple-element.421), channel_id=1, source_target_pairs={{0,16},{4,20},{8,24},{12,28},{16,0},{20,4},{24,8},{28,12},{1,17},{... | collective-permute-start | bytes 1572872 | tf_op jit(solution)/shard_map/ppermute | solution.py:614
  598.9 23.8 %collective-permute-start.35 = (bf16[4,64,1280]{2,1,0:T(8,128)(2,1)S(1)}, bf16[4,64,1280]{2,1,0:T(8,128)(2,1)S(1)}, u32[]{:S(2)}, u32[]{:S(2)}) collective-permute-start(bf16[4,64,1280]{2,1,0:T(8,128)(2,1)S(1)} %get-tuple-element.422), channel_id=1, source_target_pairs={{0,2},{1,3},{2,0},{3,1},{4,6},{5,7},{6,4},{7,5},{8,10},{9,11},{10,... | collective-permute-start | bytes 1966088 | tf_op jit(solution)/shard_map/ppermute | solution.py:614
  600.2 22.5 %collective-permute-start.36 = (bf16[8,32,1280]{2,1,0:T(8,128)(2,1)S(1)}, bf16[8,32,1280]{2,1,0:T(8,128)(2,1)S(1)}, u32[]{:S(2)}, u32[]{:S(2)}) collective-permute-start(bf16[8,32,1280]{2,1,0:T(8,128)(2,1)S(1)} %get-tuple-element.423), channel_id=1, source_target_pairs={{0,1},{1,0},{2,3},{3,2},{4,5},{5,4},{6,7},{7,6},{8,9},{9,8},{10,11... | collective-permute-start | bytes 1966088 | tf_op jit(solution)/shard_map/ppermute | solution.py:614
  (121 other events, 1177.2 us)
Sparse Core Ops, SparseCore 0:
  15.0 247.9 all-gather.1

commit v4 on v3

--- a/solution.py
+++ b/solution.py
@@ -826,36 +826,62 @@
     )(core.astype(jnp.int32).reshape(1), *formers, *latters)
 
 
-def add_halves_kernel(mine_ref, give, give_more, hold, hold_more, send_ref, keep_ref):
-    for former, latter, out in ((give, give_more, send_ref), (hold, hold_more, keep_ref)):
-        out[...] = (
-            former[...].astype(jnp.float32) + latter[...].astype(jnp.float32)
-        ).astype(jnp.bfloat16)
-
-
-def add_halves(keep, received, mine, part=0, parts=1):
-    before, _, rows, columns = keep.shape
-    columns //= parts
-    tiles = 1
-    while before * tiles < 4 and columns % (256 * tiles) == 0:
-        tiles *= 2
-    width = columns // tiles
-    several = max(1, before // 4)
-    other = pl.BlockSpec((several, None, rows, width), lambda i, j, m: (i, 1 - m[0], 0, part * tiles + j))
-    own = pl.BlockSpec((several, None, rows, width), lambda i, j, m: (i, m[0], 0, part * tiles + j))
-    out = pl.BlockSpec((several, rows, width), lambda i, j, m: (i, 0, j))
-    return pl.pallas_call(
-        add_halves_kernel,
-        grid_spec=pltpu.PrefetchScalarGridSpec(
-            num_scalar_prefetch=1,
-            grid=(before // several, tiles),
-            in_specs=[other, other, own, own],
-            out_specs=[out, out],
-        ),
-        out_shape=[jax.ShapeDtypeStruct((before, rows, columns), jnp.bfloat16)] * 2,
-        compiler_params=pltpu.CompilerParams(vmem_limit_bytes=VMEM_LIMIT),
-        cost_estimate=BRIEF,
-    )(mine.astype(jnp.int32).reshape(1), keep, received, keep, received)
+def add_halves_kernel(count, mine_ref, *refs):
+    for k in range(count):
+        give, give_more, hold, hold_more = refs[4 * k : 4 * k + 4]
+        send_ref, keep_ref = refs[4 * count + 2 * k : 4 * count + 2 * k + 2]
+        for former, latter, out in ((give, give_more, send_ref), (hold, hold_more, keep_ref)):
+            out[...] = (
+                former[...].astype(jnp.float32) + latter[...].astype(jnp.float32)
+            ).astype(jnp.bfloat16)
+
+
+def add_halves(jobs):
+    groups = {}
+    for number, (keep, _, _, _, parts) in enumerate(jobs):
+        before, columns = keep.shape[0], keep.shape[3] // parts
+        tiles = 1
+        while before * tiles < 4 and columns % (256 * tiles) == 0:
+            tiles *= 2
+        several = max(1, before // 4)
+        groups.setdefault(before // several * tiles, []).append((number, tiles, several))
+    results = [None] * len(jobs)
+    for steps, members in groups.items():
+        in_specs, out_specs, shapes, operands, bits = [], [], [], [], []
+        for at, (number, tiles, several) in enumerate(members):
+            keep, received, mine, part, parts = jobs[number]
+            before, _, rows, columns = keep.shape
+            width = columns // parts // tiles
+
+            def spec(own, at=at, tiles=tiles, first=part * tiles, several=several, rows=rows, width=width):
+                return pl.BlockSpec(
+                    (several, None, rows, width),
+                    lambda i, m: (
+                        i // tiles, m[at] if own else 1 - m[at], 0, first + i % tiles
+                    ),
+                )
+
+            in_specs += [spec(False), spec(False), spec(True), spec(True)]
+            out_specs += [
+                pl.BlockSpec(
+                    (several, rows, width), lambda i, m, tiles=tiles: (i // tiles, 0, i % tiles)
+                )
+            ] * 2
+            shapes += [jax.ShapeDtypeStruct((before, rows, columns // parts), jnp.bfloat16)] * 2
+            operands += [keep, received, keep, received]
+            bits.append(mine)
+        outs = pl.pallas_call(
+            partial(add_halves_kernel, len(members)),
+            grid_spec=pltpu.PrefetchScalarGridSpec(
+                num_scalar_prefetch=1, grid=(steps,), in_specs=in_specs, out_specs=out_specs
+            ),
+            out_shape=shapes,
+            compiler_params=pltpu.CompilerParams(vmem_limit_bytes=VMEM_LIMIT),
+            cost_estimate=BRIEF,
+        )(jnp.stack(bits).astype(jnp.int32), *operands)
+        for at, (number, _, _) in enumerate(members):
+            results[number] = outs[2 * at : 2 * at + 2]
+    return results
 
 
 class Scatter:
@@ -865,24 +891,29 @@
         self.names = [k for k in range(len(self.bits)) if k != core]
         self.order = [k for k in order[::-1] if k != core]
         self.keep, self.received = keep, received
-        self.step(part, 2)
-
-    def step(self, part=0, parts=1):
+        self.part, self.parts = part, 2
+
+    def job(self):
         self.send = None
         keep, received = self.keep, self.received
         if not self.names:
             total = keep.astype(jnp.float32) + received.astype(jnp.float32)
             self.keep, self.received = total.reshape(-1, total.shape[-1]), None
-            return
+            return None
         k = self.order.pop(0)
         axis = self.names.index(k)
         self.names.remove(k)
         columns = keep.shape[-1]
         shape = (2**axis, 2, keep.size // columns // 2 ** (axis + 1), columns)
-        send, self.keep = add_halves(
-            keep.reshape(shape), received.reshape(shape), own_bit(self.bits[k]), part, parts
+        self.bit = self.bits[k]
+        job = (
+            keep.reshape(shape), received.reshape(shape), own_bit(self.bit), self.part, self.parts
         )
-        self.send = (send, self.bits[k])
+        self.part, self.parts = 0, 1
+        return job
+
+    def take(self, send, keep):
+        self.send, self.keep = (send, self.bit), keep
 
     def launch(self):
         self.received, self.send = swap(*self.send), None
@@ -955,8 +986,18 @@
         if isinstance(p, Pair):
             now += p.split()
         else:
+            now.append(p)
+    waiting, jobs = [], []
+    for p in now:
+        if isinstance(p, SmallSum):
             p.step()
-            now.append(p)
+            continue
+        job = p.job()
+        if job is not None:
+            waiting.append(p)
+            jobs.append(job)
+    for p, halves in zip(waiting, add_halves(jobs)):
+        p.take(*halves)
     now = [p for p in now + fresh if p.send is not None]
     pipes[:] = now
     held = [p for p in now if p.keep is not None]

time: 690 us -> 673 us (0.975)
  Pallas kernels: 241 us -> 231 us
    pallas_call x24 -> x9, Pallas kernels: 62.1 us -> 51.7 us  [add_halves(): pl.pallas_call(partial(add_halves_kernel, len(members)), grid_spec=pltpu....]
    unnamed x206 -> x180, local copies, waits for them, and re-layouts: 35.3 us -> 34.6 us
  transfers between devices with their start and end apart: 50 -> 50, of which waited for: 34 -> 34; matrix products, arithmetic and copies ran while one was open for 9% -> 8% of each run, Pallas kernels for 20% -> 20%
where the time goes in v4:
time: 673 us; the launch traced here: 664 us
  waiting for transfers between devices  254 us (38%)
  Pallas kernels  231 us (34%)
  local copies, waits for them, and re-layouts  64.8 us (10%)
  starting transfers between devices  54.3 us (8%)
  matrix products  27.5 us (4%)
  other arithmetic  16.5 us (2%)
  between operations  16.1 us (2%)
    ppermute x49, waiting for transfers between devices, swap(): return lax.ppermute(v, name, [(i, i ^ step) for i in range(size)])  202 us
    ppermute x49, starting transfers between devices, swap(): return lax.ppermute(v, name, [(i, i ^ step) for i in range(size)])  54.2 us
    all_gather x1, waiting for transfers between devices, local(): outer_full = lax.all_gather(outer_shard, AXES, axis=0, tiled=True)  51.7 us
    pallas_call x9, Pallas kernels, add_halves(): pl.pallas_call(partial(add_halves_kernel, len(members)), grid_spec=pltpu....  51.7 us
    pallas_call x6, Pallas kernels, part_grads(): pl.pallas_call(partial(grads_kernel, plan, rows, (len(formers), len(latte...  49.1 us
    unnamed x180, local copies, waits for them, and re-layouts  34.6 us
    pallas_call x1, Pallas kernels, feed_forward(): pl.pallas_call(partial(ffn_kernel, rows, fold), grid=(steps,), in_specs=[...  27 us
    pallas_call x1, Pallas kernels, mixer_backward(): pl.pallas_call(mixer_backward_kernel, grid=(count,), in_specs=[row(DI), r...  24.9 us
  transfers between devices with their start and end apart: 50, of which 34 were waited for; matrix products, arithmetic and copies ran while one was open for 8% of the time, Pallas kernels for 20%

profile of v4, /device:TPU:0, one launch (start us, length us, event | category | flops | bytes accessed | tf_op | source)
XLA Modules:
  0.0 664.2 jit_solution(2722926442437427776)
XLA Ops:
  42.0 25.1 %collective-permute-done.6 = bf16[1,32,2048]{2,1,0:T(8,128)(2,1)S(1)} collective-permute-done((bf16[1,32,2048]{2,1,0:T(8,128)(2,1)S(1)}, bf16[1,32,2048]{2,1,0:T(8,128)(2,1)S(1)}, u32[]{:S(2)}, u32[]{:S(2)}) %collective-permute-start.6) | collective-permute-done | bytes 131104 | tf_op jit(solution)/shard_map/ppermute | solution.py:614
  69.4 28.9 %collective-permute-done.8 = bf16[2,32,2048]{2,1,0:T(8,128)(2,1)S(1)} collective-permute-done((bf16[2,32,2048]{2,1,0:T(8,128)(2,1)S(1)}, bf16[2,32,2048]{2,1,0:T(8,128)(2,1)S(1)}, u32[]{:S(2)}, u32[]{:S(2)}) %collective-permute-start.8) | collective-permute-done | bytes 262176 | tf_op jit(solution)/shard_map/ppermute | solution.py:614
  101.5 11.8 %collective-permute-done.10 = bf16[4,32,2048]{2,1,0:T(8,128)(2,1)S(1)} collective-permute-done((bf16[4,32,2048]{2,1,0:T(8,128)(2,1)S(1)}, bf16[4,32,2048]{2,1,0:T(8,128)(2,1)S(1)}, u32[]{:S(2)}, u32[]{:S(2)}) %collective-permute-start.10) | collective-permute-done | bytes 524320 | tf_op jit(solution)/shard_map/ppermute | solution.py:614
  113.3 12.7 %collective-permute-done.9 = bf16[4,32,2432]{2,1,0:T(8,128)(2,1)S(1)} collective-permute-done((bf16[4,32,2432]{2,1,0:T(8,128)(2,1)S(1)}, bf16[4,32,2432]{2,1,0:T(8,128)(2,1)S(1)}, u32[]{:S(2)}, u32[]{:S(2)}) %collective-permute-start.9) | collective-permute-done | bytes 622624 | tf_op jit(solution)/shard_map/ppermute | solution.py:614
  135.2 20.0 %collective-permute-done.12.refs_1_ = bf16[8,32,2048]{2,1,0:T(8,128)(2,1)} collective-permute-done((bf16[8,32,2048]{2,1,0:T(8,128)(2,1)}, bf16[8,32,2048]{2,1,0:T(8,128)(2,1)}, u32[]{:S(2)}, u32[]{:S(2)}) %collective-permute-start.12) | collective-permute-done | bytes 1048608 | tf_op jit(solution)/shard_map/ppermute | solution.py:614
  192.8 14.8 %shard_map.392 = (bf16[2,208,2048]{2,1,0:T(8,128)(2,1)S(1)}, bf16[2,208,256]{2,1,0:T(8,128)(2,1)S(1)}, f32[2,208,2048]{2,1,0:T(8,128)}, bf16[2,208,2048]{2,1,0:T(8,128)(2,1)S(1)}) custom-call(f32[2,208,2432]{2,1,0:T(8,128)} %fusion.30.raw_ref, f32[2,208,2048]{2,1,0:T(8,128)} %fusion.31.zgate_ref, f32[2,208,1]{2,1,0:T(8,128)S(1)} %copy.55.ids_column_ref, ...), custom_call_target="tpu_custom_call" | custom-call | flops 1024 | bytes 1024 | tf_op jit(solution)/shard_map/pallas_call | solution.py:324
  210.7 51.7 %all-gather.2.cloned.1.call-done.gate_ref.upper_ref.folded_ref.weight_ref.refs_3_.refs_4_.refs_5_ = bf16[1024,18432]{1,0:T(8,128)(2,1)} async-done(((bf16[32,18432]{1,0:T(8,128)(2,1)}), bf16[1024,18432]{1,0:T(8,128)(2,1)}) %all-gather.2.cloned.1.call-update) | async-done | bytes 37748752 | tf_op jit(solution)/shard_map/all_gather | solution.py:1086
  283.4 27.0 %shard_map.395 = (bf16[416,4096]{1,0:T(8,128)(2,1)}, bf16[416,4096]{1,0:T(8,128)(2,1)}, bf16[416,4096]{1,0:T(8,128)(2,1)}, f32[416,1024]{1,0:T(8,128)S(1)}, f32[416,1024]{1,0:T(8,128)S(1)}) custom-call(bf16[416,1024]{1,0:T(8,128)(2,1)S(1)} %multiply_convert_fusion.1.source_ref.refs_0_, bf16[416,1024]{1,0:T(8,128)(2,1)S(1)} %bitcast.159, ...), custom_call_target="tpu_custom_call" | custom-call | flops 1024 | bytes 1024 | tf_op jit(solution)/shard_map/pallas_call | solution.py:571
  312.4 12.3 %shard_map.396 = bf16[512,12288]{1,0:T(8,128)(2,1)} custom-call(s32[1]{0:T(128)} %bitcast.20.core_ref, bf16[416,1024]{1,0:T(8,128)(2,1)S(1)} %multiply_convert_fusion.1.source_ref.refs_0_, bf16[416,4096]{1,0:T(8,128)(2,1)S(1)} %copy-done.9, bf16[416,4096]{1,0:T(8,128)(2,1)} %get-tuple-element.293.refs_2_, bf16[416,4096]{1,0:T(8,128)(2,1)} %get-tuple-element.294.refs_3_, ...), custom_call_target="tpu_custom_call" | custom-call | flops 1024 | bytes 1024 | tf_op jit(solution)/shard_map/pallas_call | solution.py:814
  325.1 12.3 %shard_map.397 = bf16[512,12288]{1,0:T(8,128)(2,1)} custom-call(s32[1]{0:T(128)} %bitcast.21.core_ref, bf16[416,1024]{1,0:T(8,128)(2,1)S(1)} %multiply_convert_fusion.1.source_ref.refs_0_, bf16[416,4096]{1,0:T(8,128)(2,1)S(1)} %copy-done.9, bf16[416,4096]{1,0:T(8,128)(2,1)} %get-tuple-element.293.refs_2_, bf16[416,4096]{1,0:T(8,128)(2,1)} %get-tuple-element.294.refs_3_, ...), custom_call_target="tpu_custom_call" | custom-call | flops 1024 | bytes 1024 | tf_op jit(solution)/shard_map/pallas_call | solution.py:814
  344.2 13.7 %shard_map.398 = (bf16[4,64,6144]{2,1,0:T(8,128)(2,1)}, bf16[4,64,6144]{2,1,0:T(8,128)(2,1)}, bf16[8,32,6144]{2,1,0:T(8,128)(2,1)}, bf16[8,32,6144]{2,1,0:T(8,128)(2,1)}) custom-call(s32[2]{0:T(128)S(1)} %get-tuple-element.555.mine_ref, bf16[4,2,64,12288]{3,2,1,0:T(8,128)(2,1)} %bitcast.213, bf16[4,2,64,12288]{3,2,1,0:T(8,128)(2,1)} %bitcast.25.refs_1_.refs_3_, ...), custom_call_target="tpu_custom_call" | custom-call | flops 1024 | bytes 1024 | tf_op jit(solution)/shard_map/pallas_call | solution.py:873
  363.9 20.9 %shard_map.399 = bf16[2,208,3072]{2,1,0:T(8,128)(2,1)S(1)} custom-call(bf16[2,208,3072]{2,1,0:T(8,128)(2,1)S(1)} %bitcast.164, bf16[2,208,1024]{2,1,0:T(8,128)(2,1)S(1)} %bitcast.162, bf16[1024,18432]{1,0:T(8,128)(2,1)} %all-gather.2.cloned.1.call-done.gate_ref.upper_ref.folded_ref.weight_ref.refs_3_.refs_4_.refs_5_, f32[2,208,1]{2,1,0:T(8,128)S(1)} %copy-done.27, ...), custom_call_target="tpu_custom_call" | custom-call | flops 1024 | bytes 1024 | tf_op jit(solution)/shard_map/pallas_call | solution.py:468
  386.3 7.5 %shard_map.400 = (f32[416,1024]{1,0:T(8,128)S(1)}, bf16[416,1024]{1,0:T(8,128)(2,1)S(1)}, f32[1,1024]{1,0:T(1,128)S(1)}) custom-call(bf16[416,3072]{1,0:T(8,128)(2,1)} %bitcast.135, bf16[416,3072]{1,0:T(8,128)(2,1)} %bitcast.136, bf16[416,3072]{1,0:T(8,128)(2,1)} %bitcast.137, ...), custom_call_target="tpu_custom_call" | custom-call | flops 1024 | bytes 1024 | tf_op jit(solution)/shard_map/pallas_call | solution.py:509
  395.0 10.8 %shard_map.401 = (bf16[2,208,2048]{2,1,0:T(8,128)(2,1)S(1)}, bf16[2,208,2048]{2,1,0:T(8,128)(2,1)S(1)}, f32[1,2048]{1,0:T(1,128)S(1)}, f32[1,2048]{1,0:T(1,128)S(1)}) custom-call(bf16[2,208,1024]{2,1,0:T(8,128)(2,1)S(1)} %bitcast.165, bf16[2048,1024]{1,0:T(8,128)(2,1)} %bitcast.153, f32[2,208,2048]{2,1,0:T(8,128)} %fusion.31.zgate_ref, ...), custom_call_target="tpu_custom_call" | custom-call | flops 1024 | bytes 1024 | tf_op jit(solution)/shard_map/pallas_call | solution.py:348
  407.0 9.3 %shard_map.402 = bf16[512,8192]{1,0:T(8,128)(2,1)} custom-call(s32[1]{0:T(128)} %bitcast.20.core_ref, bf16[416,1024]{1,0:T(8,128)(2,1)S(1)} %copy-done.16, bf16[416,1024]{1,0:T(8,128)(2,1)S(1)} %bitcast.145, bf16[416,1024]{1,0:T(8,128)(2,1)S(1)} %get-tuple-element.511.refs_2_.refs_0_, bf16[416,2048]{1,0:T(8,128)(2,1)S(1)} %bitcast.167, ...), custom_call_target="tpu_custom_call" | custom-call | flops 1024 | bytes 1024 | tf_op jit(solution)/shard_map/pallas_call | solution.py:814
  416.3 9.3 %shard_map.404 = bf16[512,8192]{1,0:T(8,128)(2,1)} custom-call(s32[1]{0:T(128)} %bitcast.21.core_ref, bf16[416,1024]{1,0:T(8,128)(2,1)S(1)} %copy-done.16, bf16[416,1024]{1,0:T(8,128)(2,1)S(1)} %bitcast.146, bf16[416,1024]{1,0:T(8,128)(2,1)S(1)} %get-tuple-element.511.refs_2_.refs_0_, bf16[416,2048]{1,0:T(8,128)(2,1)S(1)} %bitcast.168, ...), custom_call_target="tpu_custom_call" | custom-call | flops 1024 | bytes 1024 | tf_op jit(solution)/shard_map/pallas_call | solution.py:814
  439.0 24.9 %shard_map.405 = (bf16[2,208,2560]{2,1,0:T(8,128)(2,1)S(1)}, f32[4,2304]{1,0:T(4,128)S(1)}, f32[1,2304]{1,0:T(1,128)S(1)}, f32[1,128]{1,0:T(1,128)S(1)}, f32[1,128]{1,0:T(1,128)S(1)}) custom-call(bf16[2,208,2048]{2,1,0:T(8,128)(2,1)S(1)} %get-tuple-element.328.heads_ref, f32[2,208,2432]{2,1,0:T(8,128)} %fusion.30.raw_ref, f32[2,208,1]{2,1,0:T(8,128)S(1)} %copy-done.28, ...), custom_call_target="tpu_custom_call" | custom-call | flops 1024 | bytes 1024 | tf_op jit(solution)/shard_map/pallas_call | solution.py:372
  465.2 8.4 %collective-permute-done.20 = bf16[4,32,6144]{2,1,0:T(8,128)(2,1)S(1)} collective-permute-done((bf16[4,32,6144]{2,1,0:T(8,128)(2,1)S(1)}, bf16[4,32,6144]{2,1,0:T(8,128)(2,1)S(1)}, u32[]{:S(2)}, u32[]{:S(2)}) %collective-permute-start.20) | collective-permute-done | bytes 1572896 | tf_op jit(solution)/shard_map/ppermute | solution.py:614
  475.2 12.1 %shard_map.406 = (bf16[2,32,6144]{2,1,0:T(8,128)(2,1)S(1)}, bf16[2,32,6144]{2,1,0:T(8,128)(2,1)S(1)}, bf16[1,64,6144]{2,1,0:T(8,128)(2,1)S(1)}, bf16[1,64,6144]{...) custom-call(s32[4]{0:T(128)S(1)} %get-tuple-element.557.mine_ref, ...), custom_call_target="tpu_custom_call" | custom-call | flops 1024 | bytes 1024 | tf_op jit(solution)/shard_map/pallas_call | solution.py:873
  507.6 9.6 %shard_map.407 = (f32[416,1024]{1,0:T(8,128)}, bf16[416,1024]{1,0:T(8,128)(2,1)S(1)}, f32[1,1024]{1,0:T(1,128)S(1)}) custom-call(bf16[416,2048]{1,0:T(8,128)(2,1)S(1)} %bitcast.158, bf16[416,2560]{1,0:T(8,128)(2,1)} %bitcast.149, bf16[1024,2048]{1,0:T(8,128)(2,1)} %bitcast.155, bf16[1024,2432]{1,0:T(8,128)(2,1)} %bitcast.148, f32[416,1024]{1,0:T(8,128)S(1)} %copy-done.18, ...), custom_call_target="tpu_custom_call" | custom-call | flops 1024 | bytes 1024 | tf_op jit(solution)/shard_map/pallas_call | solution.py:509
  521.2 7.0 %collective-permute-done.23 = bf16[2,32,6144]{2,1,0:T(8,128)(2,1)S(1)} collective-permute-done((bf16[2,32,6144]{2,1,0:T(8,128)(2,1)}, bf16[2,32,6144]{2,1,0:T(8,128)(2,1)S(1)}, u32[]{:S(2)}, u32[]{:S(2)}) %collective-permute-start.23) | collective-permute-done | bytes 786464 | tf_op jit(solution)/shard_map/ppermute | solution.py:614
  537.3 7.2 %shard_map.409 = (bf16[1,32,6144]{2,1,0:T(8,128)(2,1)}, bf16[1,32,6144]{2,1,0:T(8,128)(2,1)S(1)}, bf16[1,32,6144]{2,1,0:T(8,128)(2,1)}, bf16[1,32,6144]{2,1,0:T(...) custom-call(s32[4]{0:T(128)S(1)} %get-tuple-element.558.mine_ref, ...), custom_call_target="tpu_custom_call" | custom-call | flops 1024 | bytes 1024 | tf_op jit(solution)/shard_map/pallas_call | solution.py:873
  551.6 16.4 %collective-permute-done.27 = bf16[1,32,6144]{2,1,0:T(8,128)(2,1)} collective-permute-done((bf16[1,32,6144]{2,1,0:T(8,128)(2,1)}, bf16[1,32,6144]{2,1,0:T(8,128)(2,1)}, u32[]{:S(2)}, u32[]{:S(2)}) %collective-permute-start.27) | collective-permute-done | bytes 393248 | tf_op jit(solution)/shard_map/ppermute | solution.py:614
  587.0 14.5 %collective-permute-done.37 = f32[392,128]{1,0:T(8,128)S(1)} collective-permute-done((f32[392,128]{1,0:T(8,128)S(1)}, f32[392,128]{1,0:T(8,128)S(1)}, u32[]{:S(2)}, u32[]{:S(2)}) %collective-permute-start.37) | collective-permute-done | bytes 200736 | tf_op jit(solution)/shard_map/ppermute | solution.py:614
  (412 shorter events, 259.7 us)
Async XLA Ops:
  7.3 255.2 %all-gather.2.cloned.1.call-start = ((), (), s32[]{:S(2)}) async-start(), calls=%async_computation | async-start | bytes 38928384 | tf_op jit(solution)/shard_map/all_gather | solution.py:1086
  31.9 35.2 %collective-permute-start.5 = (bf16[1,32,2432]{2,1,0:T(8,128)(2,1)S(1)}, bf16[1,32,2432]{2,1,0:T(8,128)(2,1)S(1)}, u32[]{:S(2)}, u32[]{:S(2)}) collective-permute-start(bf16[1,32,2432]{2,1,0:T(8,128)(2,1)S(1)} %fusion.18), channel_id=1, source_target_pairs={{0,16},{4,20},{8,24},{12,28},{16,0},{20,4},{24,8},{28,12},{1,17},{... | collective-permute-start | bytes 466952 | tf_op jit(solution)/shard_map/ppermute | solution.py:614
  32.1 35.1 %collective-permute-start.6 = (bf16[1,32,2048]{2,1,0:T(8,128)(2,1)S(1)}, bf16[1,32,2048]{2,1,0:T(8,128)(2,1)S(1)}, u32[]{:S(2)}, u32[]{:S(2)}) collective-permute-start(bf16[1,32,2048]{2,1,0:T(8,128)(2,1)S(1)} %bitcast.251), channel_id=1, source_target_pairs={{0,16},{4,20},{8,24},{12,28},{16,0},{20,4},{24,8},{28,12},{1,17},{... | collective-permute-start | bytes 393224 | tf_op jit(solution)/shard_map/ppermute | solution.py:614
  67.2 31.1 %collective-permute-start.7 = (bf16[2,32,2432]{2,1,0:T(8,128)(2,1)S(1)}, bf16[2,32,2432]{2,1,0:T(8,128)(2,1)S(1)}, u32[]{:S(2)}, u32[]{:S(2)}) collective-permute-start(bf16[2,32,2432]{2,1,0:T(8,128)(2,1)S(1)} %constant_dynamic-update-slice_fusion), channel_id=1, source_target_pairs={{0,8},{4,12},{8,0},{12,4},{16,24},{20,28},{24,16},{28,20},{1,9},{5... | collective-permute-start | bytes 933896 | tf_op jit(solution)/shard_map/ppermute | solution.py:614
  67.3 31.0 %collective-permute-start.8 = (bf16[2,32,2048]{2,1,0:T(8,128)(2,1)S(1)}, bf16[2,32,2048]{2,1,0:T(8,128)(2,1)S(1)}, u32[]{:S(2)}, u32[]{:S(2)}) collective-permute-start(bf16[2,32,2048]{2,1,0:T(8,128)(2,1)S(1)} %constant_dynamic-update-slice_fusion.2), channel_id=1, source_target_pairs={{0,8},{4,12},{8,0},{12,4},{16,24},{20,28},{24,16},{28,20},{1,9},{5... | collective-permute-start | bytes 786440 | tf_op jit(solution)/shard_map/ppermute | solution.py:614
  98.4 27.6 %collective-permute-start.9 = (bf16[4,32,2432]{2,1,0:T(8,128)(2,1)S(1)}, bf16[4,32,2432]{2,1,0:T(8,128)(2,1)S(1)}, u32[]{:S(2)}, u32[]{:S(2)}) collective-permute-start(bf16[4,32,2432]{2,1,0:T(8,128)(2,1)S(1)} %constant_dynamic-update-slice_fusion.4), channel_id=1, source_target_pairs={{0,1},{1,0},{2,3},{3,2},{4,5},{5,4},{6,7},{7,6},{8,9},{9,8},{10,11... | collective-permute-start | bytes 1867784 | tf_op jit(solution)/shard_map/ppermute | solution.py:614
  126.1 32.0 %collective-permute-start.11 = (bf16[8,32,2432]{2,1,0:T(8,128)(2,1)S(1)}, bf16[8,32,2432]{2,1,0:T(8,128)(2,1)}, u32[]{:S(2)}, u32[]{:S(2)}) collective-permute-start(bf16[8,32,2432]{2,1,0:T(8,128)(2,1)S(1)} %constant_dynamic-update-slice_fusion.8.refs_0_), channel_id=1, source_target_pairs={{0,2},{1,3},{2,0},{3,1},{4,6},{5,7},{6,4},{7,5},{8,10},{9,11},{10,... | collective-permute-start | bytes 3735560 | tf_op jit(solution)/shard_map/ppermute | solution.py:614
  129.4 25.8 %collective-permute-start.12 = (bf16[8,32,2048]{2,1,0:T(8,128)(2,1)}, bf16[8,32,2048]{2,1,0:T(8,128)(2,1)}, u32[]{:S(2)}, u32[]{:S(2)}) collective-permute-start(bf16[8,32,2048]{2,1,0:T(8,128)(2,1)} %constant_dynamic-update-slice_fusion.10.refs_0_), channel_id=1, source_target_pairs={{0,1},{1,0},{2,3},{3,2},{4,5},{5,4},{6,7},{7,6},{8,9},{9,8},{10,11... | collective-permute-start | bytes 3145736 | tf_op jit(solution)/shard_map/ppermute | solution.py:614
  357.9 70.6 %collective-permute-start.18 = (bf16[4,64,6144]{2,1,0:T(8,128)(2,1)}, bf16[4,64,6144]{2,1,0:T(8,128)(2,1)}, u32[]{:S(2)}, u32[]{:S(2)}) collective-permute-start(bf16[4,64,6144]{2,1,0:T(8,128)(2,1)} %get-tuple-element.313), channel_id=1, source_target_pairs={{0,2},{1,3},{2,0},{3,1},{4,6},{5,7},{6,4},{7,5},{8,10},{9,11},{10,... | collective-permute-start | bytes 9437192 | tf_op jit(solution)/shard_map/ppermute | solution.py:614
  359.4 70.3 %collective-permute-start.19 = (bf16[8,32,6144]{2,1,0:T(8,128)(2,1)}, bf16[8,32,6144]{2,1,0:T(8,128)(2,1)}, u32[]{:S(2)}, u32[]{:S(2)}) collective-permute-start(bf16[8,32,6144]{2,1,0:T(8,128)(2,1)} %get-tuple-element.314), channel_id=1, source_target_pairs={{0,1},{1,0},{2,3},{3,2},{4,5},{5,4},{6,7},{7,6},{8,9},{9,8},{10,11... | collective-permute-start | bytes 9437192 | tf_op jit(solution)/shard_map/ppermute | solution.py:614
  436.8 37.1 %collective-permute-start.22 = (bf16[512,8192]{1,0:T(8,128)(2,1)}, bf16[512,8192]{1,0:T(8,128)(2,1)}, u32[]{:S(2)}, u32[]{:S(2)}) collective-permute-start(bf16[512,8192]{1,0:T(8,128)(2,1)} %shard_map.402), channel_id=1, source_target_pairs={{0,4},{4,0},{8,12},{12,8},{16,20},{20,16},{24,28},{28,24},{1,5},{5... | collective-permute-start | bytes 25165832 | tf_op jit(solution)/shard_map/ppermute | solution.py:614
  436.8 36.8 %collective-permute-start.20 = (bf16[4,32,6144]{2,1,0:T(8,128)(2,1)S(1)}, bf16[4,32,6144]{2,1,0:T(8,128)(2,1)S(1)}, u32[]{:S(2)}, u32[]{:S(2)}) collective-permute-start(bf16[4,32,6144]{2,1,0:T(8,128)(2,1)S(1)} %get-tuple-element.332), channel_id=1, source_target_pairs={{0,1},{1,0},{2,3},{3,2},{4,5},{5,4},{6,7},{7,6},{8,9},{9,8},{10,11... | collective-permute-start | bytes 4718600 | tf_op jit(solution)/shard_map/ppermute | solution.py:614
  437.4 36.5 %collective-permute-start.21 = (bf16[4,32,6144]{2,1,0:T(8,128)(2,1)S(1)}, bf16[4,32,6144]{2,1,0:T(8,128)(2,1)S(1)}, u32[]{:S(2)}, u32[]{:S(2)}) collective-permute-start(bf16[4,32,6144]{2,1,0:T(8,128)(2,1)S(1)} %get-tuple-element.333), channel_id=1, source_target_pairs={{0,2},{1,3},{2,0},{3,1},{4,6},{5,7},{6,4},{7,5},{8,10},{9,11},{10,... | collective-permute-start | bytes 4718600 | tf_op jit(solution)/shard_map/ppermute | solution.py:614
  489.2 47.5 %collective-permute-start.25 = (bf16[4,64,4096]{2,1,0:T(8,128)(2,1)}, bf16[4,64,4096]{2,1,0:T(8,128)(2,1)}, u32[]{:S(2)}, u32[]{:S(2)}) collective-permute-start(bf16[4,64,4096]{2,1,0:T(8,128)(2,1)} %get-tuple-element.359), channel_id=1, source_target_pairs={{0,2},{1,3},{2,0},{3,1},{4,6},{5,7},{6,4},{7,5},{8,10},{9,11},{10,... | collective-permute-start | bytes 6291464 | tf_op jit(solution)/shard_map/ppermute | solution.py:614
  490.4 46.9 %collective-permute-start.26 = (bf16[8,32,4096]{2,1,0:T(8,128)(2,1)}, bf16[8,32,4096]{2,1,0:T(8,128)(2,1)}, u32[]{:S(2)}, u32[]{:S(2)}) collective-permute-start(bf16[8,32,4096]{2,1,0:T(8,128)(2,1)} %get-tuple-element.360), channel_id=1, source_target_pairs={{0,1},{1,0},{2,3},{3,2},{4,5},{5,4},{6,7},{7,6},{8,9},{9,8},{10,11... | collective-permute-start | bytes 6291464 | tf_op jit(solution)/shard_map/ppermute | solution.py:614
  493.2 35.0 %collective-permute-start.23 = (bf16[2,32,6144]{2,1,0:T(8,128)(2,1)}, bf16[2,32,6144]{2,1,0:T(8,128)(2,1)S(1)}, u32[]{:S(2)}, u32[]{:S(2)}) collective-permute-start(bf16[2,32,6144]{2,1,0:T(8,128)(2,1)} %copy-done.48), channel_id=1, source_target_pairs={{0,8},{4,12},{8,0},{12,4},{16,24},{20,28},{24,16},{28,20},{1,9},{5... | collective-permute-start | bytes 2359304 | tf_op jit(solution)/shard_map/ppermute | solution.py:614
  494.6 36.1 %collective-permute-start.24 = (bf16[1,64,6144]{2,1,0:T(8,128)(2,1)}, bf16[1,64,6144]{2,1,0:T(8,128)(2,1)}, u32[]{:S(2)}, u32[]{:S(2)}) collective-permute-start(bf16[1,64,6144]{2,1,0:T(8,128)(2,1)} %copy-done.47), channel_id=1, source_target_pairs={{0,16},{4,20},{8,24},{12,28},{16,0},{20,4},{24,8},{28,12},{1,17},{... | collective-permute-start | bytes 2359304 | tf_op jit(solution)/shard_map/ppermute | solution.py:614
  544.5 26.8 %collective-permute-start.31 = (bf16[512,2560]{1,0:T(8,128)(2,1)}, bf16[512,2560]{1,0:T(8,128)(2,1)S(1)}, u32[]{:S(2)}, u32[]{:S(2)}) collective-permute-start(bf16[512,2560]{1,0:T(8,128)(2,1)} %shard_map.408), channel_id=1, source_target_pairs={{0,4},{4,0},{8,12},{12,8},{16,20},{20,16},{24,28},{28,24},{1,5},{5... | collective-permute-start | bytes 7864328 | tf_op jit(solution)/shard_map/ppermute | solution.py:614
  544.6 25.9 %collective-permute-start.29 = (bf16[4,32,4096]{2,1,0:T(8,128)(2,1)}, bf16[4,32,4096]{2,1,0:T(8,128)(2,1)}, u32[]{:S(2)}, u32[]{:S(2)}) collective-permute-start(bf16[4,32,4096]{2,1,0:T(8,128)(2,1)} %get-tuple-element.394), channel_id=1, source_target_pairs={{0,1},{1,0},{2,3},{3,2},{4,5},{5,4},{6,7},{7,6},{8,9},{9,8},{10,11... | collective-permute-start | bytes 3145736 | tf_op jit(solution)/shard_map/ppermute | solution.py:614
  545.7 25.5 %collective-permute-start.30 = (bf16[4,32,4096]{2,1,0:T(8,128)(2,1)}, bf16[4,32,4096]{2,1,0:T(8,128)(2,1)}, u32[]{:S(2)}, u32[]{:S(2)}) collective-permute-start(bf16[4,32,4096]{2,1,0:T(8,128)(2,1)} %get-tuple-element.395), channel_id=1, source_target_pairs={{0,2},{1,3},{2,0},{3,1},{4,6},{5,7},{6,4},{7,5},{8,10},{9,11},{10,... | collective-permute-start | bytes 3145736 | tf_op jit(solution)/shard_map/ppermute | solution.py:614
  579.8 23.8 %collective-permute-start.33 = (bf16[2,32,4096]{2,1,0:T(8,128)(2,1)S(1)}, bf16[2,32,4096]{2,1,0:T(8,128)(2,1)S(1)}, u32[]{:S(2)}, u32[]{:S(2)}) collective-permute-start(bf16[2,32,4096]{2,1,0:T(8,128)(2,1)S(1)} %get-tuple-element.420), channel_id=1, source_target_pairs={{0,8},{4,12},{8,0},{12,4},{16,24},{20,28},{24,16},{28,20},{1,9},{5... | collective-permute-start | bytes 1572872 | tf_op jit(solution)/shard_map/ppermute | solution.py:614
  580.8 25.1 %collective-permute-start.34 = (bf16[1,64,4096]{2,1,0:T(8,128)(2,1)S(1)}, bf16[1,64,4096]{2,1,0:T(8,128)(2,1)S(1)}, u32[]{:S(2)}, u32[]{:S(2)}) collective-permute-start(bf16[1,64,4096]{2,1,0:T(8,128)(2,1)S(1)} %get-tuple-element.421), channel_id=1, source_target_pairs={{0,16},{4,20},{8,24},{12,28},{16,0},{20,4},{24,8},{28,12},{1,17},{... | collective-permute-start | bytes 1572872 | tf_op jit(solution)/shard_map/ppermute | solution.py:614
  581.8 24.0 %collective-permute-start.35 = (bf16[4,64,1280]{2,1,0:T(8,128)(2,1)S(1)}, bf16[4,64,1280]{2,1,0:T(8,128)(2,1)S(1)}, u32[]{:S(2)}, u32[]{:S(2)}) collective-permute-start(bf16[4,64,1280]{2,1,0:T(8,128)(2,1)S(1)} %get-tuple-element.422), channel_id=1, source_target_pairs={{0,2},{1,3},{2,0},{3,1},{4,6},{5,7},{6,4},{7,5},{8,10},{9,11},{10,... | collective-permute-start | bytes 1966088 | tf_op jit(solution)/shard_map/ppermute | solution.py:614
  582.9 23.0 %collective-permute-start.36 = (bf16[8,32,1280]{2,1,0:T(8,128)(2,1)S(1)}, bf16[8,32,1280]{2,1,0:T(8,128)(2,1)S(1)}, u32[]{:S(2)}, u32[]{:S(2)}) collective-permute-start(bf16[8,32,1280]{2,1,0:T(8,128)(2,1)S(1)} %get-tuple-element.423), channel_id=1, source_target_pairs={{0,1},{1,0},{2,3},{3,2},{4,5},{5,4},{6,7},{7,6},{8,9},{9,8},{10,11... | collective-permute-start | bytes 1966088 | tf_op jit(solution)/shard_map/ppermute | solution.py:614
  (108 other events, 1128.0 us)
Sparse Core Ops, SparseCore 0:
  15.0 247.4 all-gather.1

commit v5 on v4

--- a/solution.py
+++ b/solution.py
@@ -650,7 +650,7 @@
 class Gather:
     def __init__(self, shard, flip):
         self.rows, self.columns = shard.shape
-        self.bits, self.order = phases(flip)
+        self.bits, self.order = phases(flip, True)
         self.pieces = [(shard[None], [0])]
         self.phase = 0
 

time: 673 us -> 674 us (level)
  starting transfers between devices: 54.3 us -> 69.6 us
  waiting for transfers between devices: 254 us -> 240 us
    all_gather x1, waiting for transfers between devices: 51.7 us -> 36 us  [local(): outer_full = lax.all_gather(outer_shard, AXES, axis=0, tiled=True)]
    ppermute x49, starting transfers between devices: 54.2 us -> 69.6 us  [swap(): return lax.ppermute(v, name, [(i, i ^ step) for i in range(size)])]
  transfers between devices with their start and end apart: 50 -> 50, of which waited for: 34 -> 31; matrix products, arithmetic and copies ran while one was open for 8% -> 8% of each run, Pallas kernels for 20% -> 20%
where the time goes in v5:
time: 674 us; the launch traced here: 665 us
  waiting for transfers between devices  240 us (36%)
  Pallas kernels  231 us (34%)
  starting transfers between devices  69.6 us (10%)
  local copies, waits for them, and re-layouts  64.5 us (10%)
  matrix products  27.5 us (4%)
  other arithmetic  16.5 us (2%)
  between operations  16.1 us (2%)
    ppermute x49, waiting for transfers between devices, swap(): return lax.ppermute(v, name, [(i, i ^ step) for i in range(size)])  204 us
    ppermute x49, starting transfers between devices, swap(): return lax.ppermute(v, name, [(i, i ^ step) for i in range(size)])  69.6 us
    pallas_call x9, Pallas kernels, add_halves(): pl.pallas_call(partial(add_halves_kernel, len(members)), grid_spec=pltpu....  51.7 us
    pallas_call x6, Pallas kernels, part_grads(): pl.pallas_call(partial(grads_kernel, plan, rows, (len(formers), len(latte...  49.1 us
    all_gather x1, waiting for transfers between devices, local(): outer_full = lax.all_gather(outer_shard, AXES, axis=0, tiled=True)  36 us
    unnamed x180, local copies, waits for them, and re-layouts  34.3 us
    pallas_call x1, Pallas kernels, feed_forward(): pl.pallas_call(partial(ffn_kernel, rows, fold), grid=(steps,), in_specs=[...  27 us
    pallas_call x1, Pallas kernels, mixer_backward(): pl.pallas_call(mixer_backward_kernel, grid=(count,), in_specs=[row(DI), r...  24.9 us
  transfers between devices with their start and end apart: 50, of which 31 were waited for; matrix products, arithmetic and copies ran while one was open for 8% of the time, Pallas kernels for 20%

profile of v5, /device:TPU:0, one launch (start us, length us, event | category | flops | bytes accessed | tf_op | source)
XLA Modules:
  0.0 665.5 jit_solution(8877174666919214426)
XLA Ops:
  38.0 21.3 %collective-permute-done.6 = bf16[1,32,2048]{2,1,0:T(8,128)(2,1)S(1)} collective-permute-done((bf16[1,32,2048]{2,1,0:T(8,128)(2,1)S(1)}, bf16[1,32,2048]{2,1,0:T(8,128)(2,1)S(1)}, u32[]{:S(2)}, u32[]{:S(2)}) %collective-permute-start.6) | collective-permute-done | bytes 131104 | tf_op jit(solution)/shard_map/ppermute | solution.py:614
  62.5 51.9 %collective-permute-done.8 = bf16[2,32,2048]{2,1,0:T(8,128)(2,1)S(1)} collective-permute-done((bf16[2,32,2048]{2,1,0:T(8,128)(2,1)S(1)}, bf16[2,32,2048]{2,1,0:T(8,128)(2,1)S(1)}, u32[]{:S(2)}, u32[]{:S(2)}) %collective-permute-start.8) | collective-permute-done | bytes 262176 | tf_op jit(solution)/shard_map/ppermute | solution.py:614
  117.5 10.2 %collective-permute-done.10 = bf16[4,32,2048]{2,1,0:T(8,128)(2,1)S(1)} collective-permute-done((bf16[4,32,2048]{2,1,0:T(8,128)(2,1)S(1)}, bf16[4,32,2048]{2,1,0:T(8,128)(2,1)S(1)}, u32[]{:S(2)}, u32[]{:S(2)}) %collective-permute-start.10) | collective-permute-done | bytes 524320 | tf_op jit(solution)/shard_map/ppermute | solution.py:614
  138.7 29.2 %collective-permute-done.12.refs_1_ = bf16[8,32,2048]{2,1,0:T(8,128)(2,1)} collective-permute-done((bf16[8,32,2048]{2,1,0:T(8,128)(2,1)}, bf16[8,32,2048]{2,1,0:T(8,128)(2,1)}, u32[]{:S(2)}, u32[]{:S(2)}) %collective-permute-start.12) | collective-permute-done | bytes 1048608 | tf_op jit(solution)/shard_map/ppermute | solution.py:614
  204.4 14.8 %shard_map.392 = (bf16[2,208,2048]{2,1,0:T(8,128)(2,1)S(1)}, bf16[2,208,256]{2,1,0:T(8,128)(2,1)S(1)}, f32[2,208,2048]{2,1,0:T(8,128)}, bf16[2,208,2048]{2,1,0:T(8,128)(2,1)S(1)}) custom-call(f32[2,208,2432]{2,1,0:T(8,128)} %fusion.30.raw_ref, f32[2,208,2048]{2,1,0:T(8,128)} %fusion.31.zgate_ref, f32[2,208,1]{2,1,0:T(8,128)S(1)} %copy.55.ids_column_ref, ...), custom_call_target="tpu_custom_call" | custom-call | flops 1024 | bytes 1024 | tf_op jit(solution)/shard_map/pallas_call | solution.py:324
  222.3 36.0 %all-gather.2.cloned.1.call-done.gate_ref.upper_ref.folded_ref.weight_ref.refs_3_.refs_4_.refs_5_ = bf16[1024,18432]{1,0:T(8,128)(2,1)} async-done(((bf16[32,18432]{1,0:T(8,128)(2,1)}), bf16[1024,18432]{1,0:T(8,128)(2,1)}) %all-gather.2.cloned.1.call-update) | async-done | bytes 37748752 | tf_op jit(solution)/shard_map/all_gather | solution.py:1086
  279.2 27.0 %shard_map.395 = (bf16[416,4096]{1,0:T(8,128)(2,1)}, bf16[416,4096]{1,0:T(8,128)(2,1)}, bf16[416,4096]{1,0:T(8,128)(2,1)}, f32[416,1024]{1,0:T(8,128)S(1)}, f32[416,1024]{1,0:T(8,128)S(1)}) custom-call(bf16[416,1024]{1,0:T(8,128)(2,1)S(1)} %multiply_convert_fusion.1.source_ref.refs_0_, bf16[416,1024]{1,0:T(8,128)(2,1)S(1)} %bitcast.159, ...), custom_call_target="tpu_custom_call" | custom-call | flops 1024 | bytes 1024 | tf_op jit(solution)/shard_map/pallas_call | solution.py:571
  308.2 12.3 %shard_map.396 = bf16[512,12288]{1,0:T(8,128)(2,1)} custom-call(s32[1]{0:T(128)} %bitcast.20.core_ref, bf16[416,1024]{1,0:T(8,128)(2,1)S(1)} %multiply_convert_fusion.1.source_ref.refs_0_, bf16[416,4096]{1,0:T(8,128)(2,1)S(1)} %copy-done.9, bf16[416,4096]{1,0:T(8,128)(2,1)} %get-tuple-element.293.refs_2_, bf16[416,4096]{1,0:T(8,128)(2,1)} %get-tuple-element.294.refs_3_, ...), custom_call_target="tpu_custom_call" | custom-call | flops 1024 | bytes 1024 | tf_op jit(solution)/shard_map/pallas_call | solution.py:814
  320.9 12.3 %shard_map.397 = bf16[512,12288]{1,0:T(8,128)(2,1)} custom-call(s32[1]{0:T(128)} %bitcast.21.core_ref, bf16[416,1024]{1,0:T(8,128)(2,1)S(1)} %multiply_convert_fusion.1.source_ref.refs_0_, bf16[416,4096]{1,0:T(8,128)(2,1)S(1)} %copy-done.9, bf16[416,4096]{1,0:T(8,128)(2,1)} %get-tuple-element.293.refs_2_, bf16[416,4096]{1,0:T(8,128)(2,1)} %get-tuple-element.294.refs_3_, ...), custom_call_target="tpu_custom_call" | custom-call | flops 1024 | bytes 1024 | tf_op jit(solution)/shard_map/pallas_call | solution.py:814
  340.0 13.7 %shard_map.398 = (bf16[4,64,6144]{2,1,0:T(8,128)(2,1)}, bf16[4,64,6144]{2,1,0:T(8,128)(2,1)}, bf16[8,32,6144]{2,1,0:T(8,128)(2,1)}, bf16[8,32,6144]{2,1,0:T(8,128)(2,1)}) custom-call(s32[2]{0:T(128)S(1)} %get-tuple-element.555.mine_ref, bf16[4,2,64,12288]{3,2,1,0:T(8,128)(2,1)} %bitcast.213, bf16[4,2,64,12288]{3,2,1,0:T(8,128)(2,1)} %bitcast.25.refs_1_.refs_3_, ...), custom_call_target="tpu_custom_call" | custom-call | flops 1024 | bytes 1024 | tf_op jit(solution)/shard_map/pallas_call | solution.py:873
  360.0 20.9 %shard_map.399 = bf16[2,208,3072]{2,1,0:T(8,128)(2,1)S(1)} custom-call(bf16[2,208,3072]{2,1,0:T(8,128)(2,1)S(1)} %bitcast.164, bf16[2,208,1024]{2,1,0:T(8,128)(2,1)S(1)} %bitcast.162, bf16[1024,18432]{1,0:T(8,128)(2,1)} %all-gather.2.cloned.1.call-done.gate_ref.upper_ref.folded_ref.weight_ref.refs_3_.refs_4_.refs_5_, f32[2,208,1]{2,1,0:T(8,128)S(1)} %copy-done.27, ...), custom_call_target="tpu_custom_call" | custom-call | flops 1024 | bytes 1024 | tf_op jit(solution)/shard_map/pallas_call | solution.py:468
  382.4 7.5 %shard_map.400 = (f32[416,1024]{1,0:T(8,128)S(1)}, bf16[416,1024]{1,0:T(8,128)(2,1)S(1)}, f32[1,1024]{1,0:T(1,128)S(1)}) custom-call(bf16[416,3072]{1,0:T(8,128)(2,1)} %bitcast.135, bf16[416,3072]{1,0:T(8,128)(2,1)} %bitcast.136, bf16[416,3072]{1,0:T(8,128)(2,1)} %bitcast.137, ...), custom_call_target="tpu_custom_call" | custom-call | flops 1024 | bytes 1024 | tf_op jit(solution)/shard_map/pallas_call | solution.py:509
  391.1 10.8 %shard_map.401 = (bf16[2,208,2048]{2,1,0:T(8,128)(2,1)S(1)}, bf16[2,208,2048]{2,1,0:T(8,128)(2,1)S(1)}, f32[1,2048]{1,0:T(1,128)S(1)}, f32[1,2048]{1,0:T(1,128)S(1)}) custom-call(bf16[2,208,1024]{2,1,0:T(8,128)(2,1)S(1)} %bitcast.165, bf16[2048,1024]{1,0:T(8,128)(2,1)} %bitcast.153, f32[2,208,2048]{2,1,0:T(8,128)} %fusion.31.zgate_ref, ...), custom_call_target="tpu_custom_call" | custom-call | flops 1024 | bytes 1024 | tf_op jit(solution)/shard_map/pallas_call | solution.py:348
  403.1 9.3 %shard_map.402 = bf16[512,8192]{1,0:T(8,128)(2,1)} custom-call(s32[1]{0:T(128)} %bitcast.20.core_ref, bf16[416,1024]{1,0:T(8,128)(2,1)S(1)} %copy-done.16, bf16[416,1024]{1,0:T(8,128)(2,1)S(1)} %bitcast.145, bf16[416,1024]{1,0:T(8,128)(2,1)S(1)} %get-tuple-element.511.refs_2_.refs_0_, bf16[416,2048]{1,0:T(8,128)(2,1)S(1)} %bitcast.167, ...), custom_call_target="tpu_custom_call" | custom-call | flops 1024 | bytes 1024 | tf_op jit(solution)/shard_map/pallas_call | solution.py:814
  412.4 9.3 %shard_map.404 = bf16[512,8192]{1,0:T(8,128)(2,1)} custom-call(s32[1]{0:T(128)} %bitcast.21.core_ref, bf16[416,1024]{1,0:T(8,128)(2,1)S(1)} %copy-done.16, bf16[416,1024]{1,0:T(8,128)(2,1)S(1)} %bitcast.146, bf16[416,1024]{1,0:T(8,128)(2,1)S(1)} %get-tuple-element.511.refs_2_.refs_0_, bf16[416,2048]{1,0:T(8,128)(2,1)S(1)} %bitcast.168, ...), custom_call_target="tpu_custom_call" | custom-call | flops 1024 | bytes 1024 | tf_op jit(solution)/shard_map/pallas_call | solution.py:814
  425.6 7.0 %shard_map.403 = (bf16[4,32,6144]{2,1,0:T(8,128)(2,1)S(1)}, bf16[4,32,6144]{2,1,0:T(8,128)(2,1)S(1)}, bf16[4,32,6144]{2,1,0:T(8,128)(2,1)S(1)}, bf16[4,32,6144]{2,1,0:T(8,128)(2,1)}) custom-call(s32[2]{0:T(128)S(1)} %get-tuple-element.556.mine_ref, bf16[4,2,32,6144]{3,2,1,0:T(8,128)(2,1)} %bitcast.225, bf16[4,2,32,6144]{3,2,1,0:T(8,128)(2,1)} %bitcast.33.refs_1_.refs_3_, ...), custom_call_target="tpu_custom_call" | custom-call | flops 1024 | bytes 1024 | tf_op jit(solution)/shard_map/pallas_call | solution.py:873
  434.1 24.9 %shard_map.405 = (bf16[2,208,2560]{2,1,0:T(8,128)(2,1)S(1)}, f32[4,2304]{1,0:T(4,128)S(1)}, f32[1,2304]{1,0:T(1,128)S(1)}, f32[1,128]{1,0:T(1,128)S(1)}, f32[1,128]{1,0:T(1,128)S(1)}) custom-call(bf16[2,208,2048]{2,1,0:T(8,128)(2,1)S(1)} %get-tuple-element.328.heads_ref, f32[2,208,2432]{2,1,0:T(8,128)} %fusion.30.raw_ref, f32[2,208,1]{2,1,0:T(8,128)S(1)} %copy-done.28, ...), custom_call_target="tpu_custom_call" | custom-call | flops 1024 | bytes 1024 | tf_op jit(solution)/shard_map/pallas_call | solution.py:372
  460.3 9.0 %collective-permute-done.20 = bf16[4,32,6144]{2,1,0:T(8,128)(2,1)S(1)} collective-permute-done((bf16[4,32,6144]{2,1,0:T(8,128)(2,1)S(1)}, bf16[4,32,6144]{2,1,0:T(8,128)(2,1)S(1)}, u32[]{:S(2)}, u32[]{:S(2)}) %collective-permute-start.20) | collective-permute-done | bytes 1572896 | tf_op jit(solution)/shard_map/ppermute | solution.py:614
  471.0 12.1 %shard_map.406 = (bf16[2,32,6144]{2,1,0:T(8,128)(2,1)S(1)}, bf16[2,32,6144]{2,1,0:T(8,128)(2,1)S(1)}, bf16[1,64,6144]{2,1,0:T(8,128)(2,1)S(1)}, bf16[1,64,6144]{...) custom-call(s32[4]{0:T(128)S(1)} %get-tuple-element.557.mine_ref, ...), custom_call_target="tpu_custom_call" | custom-call | flops 1024 | bytes 1024 | tf_op jit(solution)/shard_map/pallas_call | solution.py:873
  507.3 9.6 %shard_map.407 = (f32[416,1024]{1,0:T(8,128)}, bf16[416,1024]{1,0:T(8,128)(2,1)S(1)}, f32[1,1024]{1,0:T(1,128)S(1)}) custom-call(bf16[416,2048]{1,0:T(8,128)(2,1)S(1)} %bitcast.158, bf16[416,2560]{1,0:T(8,128)(2,1)} %bitcast.149, bf16[1024,2048]{1,0:T(8,128)(2,1)} %bitcast.155, bf16[1024,2432]{1,0:T(8,128)(2,1)} %bitcast.148, f32[416,1024]{1,0:T(8,128)S(1)} %copy-done.18, ...), custom_call_target="tpu_custom_call" | custom-call | flops 1024 | bytes 1024 | tf_op jit(solution)/shard_map/pallas_call | solution.py:509
  532.8 7.2 %shard_map.409 = (bf16[1,32,6144]{2,1,0:T(8,128)(2,1)}, bf16[1,32,6144]{2,1,0:T(8,128)(2,1)S(1)}, bf16[1,32,6144]{2,1,0:T(8,128)(2,1)}, bf16[1,32,6144]{2,1,0:T(...) custom-call(s32[4]{0:T(128)S(1)} %get-tuple-element.558.mine_ref, ...), custom_call_target="tpu_custom_call" | custom-call | flops 1024 | bytes 1024 | tf_op jit(solution)/shard_map/pallas_call | solution.py:873
  552.2 12.6 %collective-permute-done.27 = bf16[1,32,6144]{2,1,0:T(8,128)(2,1)} collective-permute-done((bf16[1,32,6144]{2,1,0:T(8,128)(2,1)}, bf16[1,32,6144]{2,1,0:T(8,128)(2,1)}, u32[]{:S(2)}, u32[]{:S(2)}) %collective-permute-start.27) | collective-permute-done | bytes 393248 | tf_op jit(solution)/shard_map/ppermute | solution.py:614
  575.1 6.4 collective-permute-start.33
  586.6 14.8 %collective-permute-done.37 = f32[392,128]{1,0:T(8,128)S(1)} collective-permute-done((f32[392,128]{1,0:T(8,128)S(1)}, f32[392,128]{1,0:T(8,128)S(1)}, u32[]{:S(2)}, u32[]{:S(2)}) %collective-permute-start.37) | collective-permute-done | bytes 200736 | tf_op jit(solution)/shard_map/ppermute | solution.py:614
  (412 shorter events, 259.2 us)
Async XLA Ops:
  7.3 251.0 %all-gather.2.cloned.1.call-start = ((), (), s32[]{:S(2)}) async-start(), calls=%async_computation | async-start | bytes 38928384 | tf_op jit(solution)/shard_map/all_gather | solution.py:1086
  31.9 27.4 %collective-permute-start.5 = (bf16[1,32,2432]{2,1,0:T(8,128)(2,1)S(1)}, bf16[1,32,2432]{2,1,0:T(8,128)(2,1)S(1)}, u32[]{:S(2)}, u32[]{:S(2)}) collective-permute-start(bf16[1,32,2432]{2,1,0:T(8,128)(2,1)S(1)} %fusion.18), channel_id=1, source_target_pairs={{0,8},{4,12},{8,0},{12,4},{16,24},{20,28},{24,16},{28,20},{1,9},{5... | collective-permute-start | bytes 466952 | tf_op jit(solution)/shard_map/ppermute | solution.py:614
  35.6 23.7 %collective-permute-start.6 = (bf16[1,32,2048]{2,1,0:T(8,128)(2,1)S(1)}, bf16[1,32,2048]{2,1,0:T(8,128)(2,1)S(1)}, u32[]{:S(2)}, u32[]{:S(2)}) collective-permute-start(bf16[1,32,2048]{2,1,0:T(8,128)(2,1)S(1)} %bitcast.251), channel_id=1, source_target_pairs={{0,8},{4,12},{8,0},{12,4},{16,24},{20,28},{24,16},{28,20},{1,9},{5... | collective-permute-start | bytes 393224 | tf_op jit(solution)/shard_map/ppermute | solution.py:614
  59.4 55.0 %collective-permute-start.7 = (bf16[2,32,2432]{2,1,0:T(8,128)(2,1)S(1)}, bf16[2,32,2432]{2,1,0:T(8,128)(2,1)S(1)}, u32[]{:S(2)}, u32[]{:S(2)}) collective-permute-start(bf16[2,32,2432]{2,1,0:T(8,128)(2,1)S(1)} %constant_dynamic-update-slice_fusion), channel_id=1, source_target_pairs={{0,16},{4,20},{8,24},{12,28},{16,0},{20,4},{24,8},{28,12},{1,17},{... | collective-permute-start | bytes 933896 | tf_op jit(solution)/shard_map/ppermute | solution.py:614
  59.5 54.9 %collective-permute-start.8 = (bf16[2,32,2048]{2,1,0:T(8,128)(2,1)S(1)}, bf16[2,32,2048]{2,1,0:T(8,128)(2,1)S(1)}, u32[]{:S(2)}, u32[]{:S(2)}) collective-permute-start(bf16[2,32,2048]{2,1,0:T(8,128)(2,1)S(1)} %constant_dynamic-update-slice_fusion.2), channel_id=1, source_target_pairs={{0,16},{4,20},{8,24},{12,28},{16,0},{20,4},{24,8},{28,12},{1,17},{... | collective-permute-start | bytes 786440 | tf_op jit(solution)/shard_map/ppermute | solution.py:614
  128.7 41.0 %collective-permute-start.11 = (bf16[8,32,2432]{2,1,0:T(8,128)(2,1)S(1)}, bf16[8,32,2432]{2,1,0:T(8,128)(2,1)}, u32[]{:S(2)}, u32[]{:S(2)}) collective-permute-start(bf16[8,32,2432]{2,1,0:T(8,128)(2,1)S(1)} %constant_dynamic-update-slice_fusion.8.refs_0_), channel_id=1, source_target_pairs={{0,2},{1,3},{2,0},{3,1},{4,6},{5,7},{6,4},{7,5},{8,10},{9,11},{10,... | collective-permute-start | bytes 3735560 | tf_op jit(solution)/shard_map/ppermute | solution.py:614
  131.9 35.9 %collective-permute-start.12 = (bf16[8,32,2048]{2,1,0:T(8,128)(2,1)}, bf16[8,32,2048]{2,1,0:T(8,128)(2,1)}, u32[]{:S(2)}, u32[]{:S(2)}) collective-permute-start(bf16[8,32,2048]{2,1,0:T(8,128)(2,1)} %constant_dynamic-update-slice_fusion.10.refs_0_), channel_id=1, source_target_pairs={{0,1},{1,0},{2,3},{3,2},{4,5},{5,4},{6,7},{7,6},{8,9},{9,8},{10,11... | collective-permute-start | bytes 3145736 | tf_op jit(solution)/shard_map/ppermute | solution.py:614
  353.7 70.6 %collective-permute-start.18 = (bf16[4,64,6144]{2,1,0:T(8,128)(2,1)}, bf16[4,64,6144]{2,1,0:T(8,128)(2,1)}, u32[]{:S(2)}, u32[]{:S(2)}) collective-permute-start(bf16[4,64,6144]{2,1,0:T(8,128)(2,1)} %get-tuple-element.313), channel_id=1, source_target_pairs={{0,2},{1,3},{2,0},{3,1},{4,6},{5,7},{6,4},{7,5},{8,10},{9,11},{10,... | collective-permute-start | bytes 9437192 | tf_op jit(solution)/shard_map/ppermute | solution.py:614
  355.2 70.3 %collective-permute-start.19 = (bf16[8,32,6144]{2,1,0:T(8,128)(2,1)}, bf16[8,32,6144]{2,1,0:T(8,128)(2,1)}, u32[]{:S(2)}, u32[]{:S(2)}) collective-permute-start(bf16[8,32,6144]{2,1,0:T(8,128)(2,1)} %get-tuple-element.314), channel_id=1, source_target_pairs={{0,1},{1,0},{2,3},{3,2},{4,5},{5,4},{6,7},{7,6},{8,9},{9,8},{10,11... | collective-permute-start | bytes 9437192 | tf_op jit(solution)/shard_map/ppermute | solution.py:614
  432.6 37.3 %collective-permute-start.22 = (bf16[512,8192]{1,0:T(8,128)(2,1)}, bf16[512,8192]{1,0:T(8,128)(2,1)}, u32[]{:S(2)}, u32[]{:S(2)}) collective-permute-start(bf16[512,8192]{1,0:T(8,128)(2,1)} %shard_map.402), channel_id=1, source_target_pairs={{0,4},{4,0},{8,12},{12,8},{16,20},{20,16},{24,28},{28,24},{1,5},{5... | collective-permute-start | bytes 25165832 | tf_op jit(solution)/shard_map/ppermute | solution.py:614
  432.6 36.8 %collective-permute-start.20 = (bf16[4,32,6144]{2,1,0:T(8,128)(2,1)S(1)}, bf16[4,32,6144]{2,1,0:T(8,128)(2,1)S(1)}, u32[]{:S(2)}, u32[]{:S(2)}) collective-permute-start(bf16[4,32,6144]{2,1,0:T(8,128)(2,1)S(1)} %get-tuple-element.332), channel_id=1, source_target_pairs={{0,1},{1,0},{2,3},{3,2},{4,5},{5,4},{6,7},{7,6},{8,9},{9,8},{10,11... | collective-permute-start | bytes 4718600 | tf_op jit(solution)/shard_map/ppermute | solution.py:614
  433.4 36.5 %collective-permute-start.21 = (bf16[4,32,6144]{2,1,0:T(8,128)(2,1)S(1)}, bf16[4,32,6144]{2,1,0:T(8,128)(2,1)S(1)}, u32[]{:S(2)}, u32[]{:S(2)}) collective-permute-start(bf16[4,32,6144]{2,1,0:T(8,128)(2,1)S(1)} %get-tuple-element.333), channel_id=1, source_target_pairs={{0,2},{1,3},{2,0},{3,1},{4,6},{5,7},{6,4},{7,5},{8,10},{9,11},{10,... | collective-permute-start | bytes 4718600 | tf_op jit(solution)/shard_map/ppermute | solution.py:614
  484.9 47.5 %collective-permute-start.25 = (bf16[4,64,4096]{2,1,0:T(8,128)(2,1)}, bf16[4,64,4096]{2,1,0:T(8,128)(2,1)}, u32[]{:S(2)}, u32[]{:S(2)}) collective-permute-start(bf16[4,64,4096]{2,1,0:T(8,128)(2,1)} %get-tuple-element.359), channel_id=1, source_target_pairs={{0,2},{1,3},{2,0},{3,1},{4,6},{5,7},{6,4},{7,5},{8,10},{9,11},{10,... | collective-permute-start | bytes 6291464 | tf_op jit(solution)/shard_map/ppermute | solution.py:614
  485.6 47.2 %collective-permute-start.26 = (bf16[8,32,4096]{2,1,0:T(8,128)(2,1)}, bf16[8,32,4096]{2,1,0:T(8,128)(2,1)}, u32[]{:S(2)}, u32[]{:S(2)}) collective-permute-start(bf16[8,32,4096]{2,1,0:T(8,128)(2,1)} %get-tuple-element.360), channel_id=1, source_target_pairs={{0,1},{1,0},{2,3},{3,2},{4,5},{5,4},{6,7},{7,6},{8,9},{9,8},{10,11... | collective-permute-start | bytes 6291464 | tf_op jit(solution)/shard_map/ppermute | solution.py:614
  488.9 36.1 %collective-permute-start.23 = (bf16[2,32,6144]{2,1,0:T(8,128)(2,1)}, bf16[2,32,6144]{2,1,0:T(8,128)(2,1)S(1)}, u32[]{:S(2)}, u32[]{:S(2)}) collective-permute-start(bf16[2,32,6144]{2,1,0:T(8,128)(2,1)} %copy-done.48), channel_id=1, source_target_pairs={{0,8},{4,12},{8,0},{12,4},{16,24},{20,28},{24,16},{28,20},{1,9},{5... | collective-permute-start | bytes 2359304 | tf_op jit(solution)/shard_map/ppermute | solution.py:614
  494.9 36.4 %collective-permute-start.24 = (bf16[1,64,6144]{2,1,0:T(8,128)(2,1)}, bf16[1,64,6144]{2,1,0:T(8,128)(2,1)}, u32[]{:S(2)}, u32[]{:S(2)}) collective-permute-start(bf16[1,64,6144]{2,1,0:T(8,128)(2,1)} %copy-done.47), channel_id=1, source_target_pairs={{0,16},{4,20},{8,24},{12,28},{16,0},{20,4},{24,8},{28,12},{1,17},{... | collective-permute-start | bytes 2359304 | tf_op jit(solution)/shard_map/ppermute | solution.py:614
  540.0 26.6 %collective-permute-start.31 = (bf16[512,2560]{1,0:T(8,128)(2,1)}, bf16[512,2560]{1,0:T(8,128)(2,1)S(1)}, u32[]{:S(2)}, u32[]{:S(2)}) collective-permute-start(bf16[512,2560]{1,0:T(8,128)(2,1)} %shard_map.408), channel_id=1, source_target_pairs={{0,4},{4,0},{8,12},{12,8},{16,20},{20,16},{24,28},{28,24},{1,5},{5... | collective-permute-start | bytes 7864328 | tf_op jit(solution)/shard_map/ppermute | solution.py:614
  540.1 25.9 %collective-permute-start.29 = (bf16[4,32,4096]{2,1,0:T(8,128)(2,1)}, bf16[4,32,4096]{2,1,0:T(8,128)(2,1)}, u32[]{:S(2)}, u32[]{:S(2)}) collective-permute-start(bf16[4,32,4096]{2,1,0:T(8,128)(2,1)} %get-tuple-element.394), channel_id=1, source_target_pairs={{0,1},{1,0},{2,3},{3,2},{4,5},{5,4},{6,7},{7,6},{8,9},{9,8},{10,11... | collective-permute-start | bytes 3145736 | tf_op jit(solution)/shard_map/ppermute | solution.py:614
  541.1 25.5 %collective-permute-start.30 = (bf16[4,32,4096]{2,1,0:T(8,128)(2,1)}, bf16[4,32,4096]{2,1,0:T(8,128)(2,1)}, u32[]{:S(2)}, u32[]{:S(2)}) collective-permute-start(bf16[4,32,4096]{2,1,0:T(8,128)(2,1)} %get-tuple-element.395), channel_id=1, source_target_pairs={{0,2},{1,3},{2,0},{3,1},{4,6},{5,7},{6,4},{7,5},{8,10},{9,11},{10,... | collective-permute-start | bytes 3145736 | tf_op jit(solution)/shard_map/ppermute | solution.py:614
  542.5 22.3 %collective-permute-start.27 = (bf16[1,32,6144]{2,1,0:T(8,128)(2,1)}, bf16[1,32,6144]{2,1,0:T(8,128)(2,1)}, u32[]{:S(2)}, u32[]{:S(2)}) collective-permute-start(bf16[1,32,6144]{2,1,0:T(8,128)(2,1)} %get-tuple-element.392), channel_id=1, source_target_pairs={{0,16},{4,20},{8,24},{12,28},{16,0},{20,4},{24,8},{28,12},{1,17},{... | collective-permute-start | bytes 1179656 | tf_op jit(solution)/shard_map/ppermute | solution.py:614
  575.1 26.4 %collective-permute-start.33 = (bf16[2,32,4096]{2,1,0:T(8,128)(2,1)S(1)}, bf16[2,32,4096]{2,1,0:T(8,128)(2,1)S(1)}, u32[]{:S(2)}, u32[]{:S(2)}) collective-permute-start(bf16[2,32,4096]{2,1,0:T(8,128)(2,1)S(1)} %get-tuple-element.420), channel_id=1, source_target_pairs={{0,8},{4,12},{8,0},{12,4},{16,24},{20,28},{24,16},{28,20},{1,9},{5... | collective-permute-start | bytes 1572872 | tf_op jit(solution)/shard_map/ppermute | solution.py:614
  581.5 25.1 %collective-permute-start.34 = (bf16[1,64,4096]{2,1,0:T(8,128)(2,1)S(1)}, bf16[1,64,4096]{2,1,0:T(8,128)(2,1)S(1)}, u32[]{:S(2)}, u32[]{:S(2)}) collective-permute-start(bf16[1,64,4096]{2,1,0:T(8,128)(2,1)S(1)} %get-tuple-element.421), channel_id=1, source_target_pairs={{0,16},{4,20},{8,24},{12,28},{16,0},{20,4},{24,8},{28,12},{1,17},{... | collective-permute-start | bytes 1572872 | tf_op jit(solution)/shard_map/ppermute | solution.py:614
  581.5 25.1 %collective-permute-start.35 = (bf16[4,64,1280]{2,1,0:T(8,128)(2,1)S(1)}, bf16[4,64,1280]{2,1,0:T(8,128)(2,1)S(1)}, u32[]{:S(2)}, u32[]{:S(2)}) collective-permute-start(bf16[4,64,1280]{2,1,0:T(8,128)(2,1)S(1)} %get-tuple-element.422), channel_id=1, source_target_pairs={{0,2},{1,3},{2,0},{3,1},{4,6},{5,7},{6,4},{7,5},{8,10},{9,11},{10,... | collective-permute-start | bytes 1966088 | tf_op jit(solution)/shard_map/ppermute | solution.py:614
  582.9 23.6 %collective-permute-start.36 = (bf16[8,32,1280]{2,1,0:T(8,128)(2,1)S(1)}, bf16[8,32,1280]{2,1,0:T(8,128)(2,1)S(1)}, u32[]{:S(2)}, u32[]{:S(2)}) collective-permute-start(bf16[8,32,1280]{2,1,0:T(8,128)(2,1)S(1)} %get-tuple-element.423), channel_id=1, source_target_pairs={{0,1},{1,0},{2,3},{3,2},{4,5},{5,4},{6,7},{7,6},{8,9},{9,8},{10,11... | collective-permute-start | bytes 1966088 | tf_op jit(solution)/shard_map/ppermute | solution.py:614
  (108 other events, 1171.5 us)
Sparse Core Ops, SparseCore 0:
  15.0 243.2 all-gather.1
